TPU v7x, 256 devices: a whole 4x4x8 slice. The times are simulated.
256 devices in a mesh: row: 16 (over z, core), col: 16 (over y, x).
Axes of the slice: x: 4, y: 4, z: 8, core: 2. Of those that a mesh axis runs over, the one named last changes fastest.
Arguments:
- patches: bfloat16 [16, 16, 2, 16, 128, 128], P('row', 'col'), as said below
- windows: bfloat16 [16, 16, 2, 16, 36864], P('row', 'col'), as said below
- candidates: int32 [16, 16, 2, 2, 128], P('row', 'col'), may hold values from -32 to 32, as said below
- live: int32 [16, 16, 2], replicated, may hold values from 1 to 16, as said below
- edges: int32 [16, 2, 11280], P('row', None, 'col'), may hold values from 0 to 255, as said below
- stiffness: float32 [16, 11280], P('row', 'col'), may hold values from 0.3 to 3
Outputs:
- matches: float32 [16, 16, 2, 3, 16], P('row', 'col')
- mesh_shift: float32 [16, 16, 2, 256], P('row', 'col')
Inputs may be any that keep to these rules, and one draw needn't show every extreme that they name: `candidates`: the candidate shifts of a patch need not be distinct. live[r, c, k] counts the live slots of seam k of tile (r, c): slots 0 to live - 1; the same for all devices. Each tile's springs are the edges of its 16 x 16 vertex grid, horizontal and vertical, and one diagonal of every cell, in any order. `windows`: window k of tile (r, c) serves the seam that tile (r, c-1) (k = 0) or tile (r-1, c) (k = 1) holds as its seam k. `patches`: patch p of seam k is scored against window p of the neighbour.
All inputs are finite; a program needn't handle non-finite values.
Results may differ from a plain program's by a relative error of at most 0.0003.
Values may be sent and summed in bfloat16 or wider, within the bound.
No kernel may reach another device: no remote copies, remote signals or barrier semaphores. Data moves between devices by JAX's collectives and lax.ppermute only.
A program may use at most 64 MiB of HBM per device.

v0:
```python
import jax
import jax.numpy as jnp
from jax import lax
from jax.sharding import PartitionSpec as P

REACH = 32
WIN = 192
NS = 8
P_SIZE = 16
BLK = 4
GV = 16
ITERS = 3


LAMBDA_REG = 0.05
EPSILON = 1e-05
PRECISE = lax.Precision.HIGHEST


def shifted(x, axis, by):
    length = lax.axis_size(axis)
    pairs = [(i, i + by) for i in range(length) if 0 <= i + by < length]
    return lax.ppermute(x, axis, pairs)


def with_halo(block, sides, width):
    for axis, dim in sides:
        count = lax.axis_size(axis)
        forward = [(i, i + 1) for i in range(count - 1)]
        backward = [(target, source) for source, target in forward]
        low = lax.ppermute(
            lax.slice_in_dim(block, block.shape[dim] - width, None, axis=dim), axis, forward
        )
        high = lax.ppermute(lax.slice_in_dim(block, 0, width, axis=dim), axis, backward)
        block = jnp.concatenate([low, block, high], axis=dim)
    return block


def match_block(patch_raw, frames, list_y, list_x):
    patch_size = patch_raw.shape[-1]
    cand_count = list_y.shape[-1]
    pixel_count = float(patch_size * patch_size)
    frame_pixels_all = frames.reshape(frames.shape[0], WIN, WIN)

    def crop_all(frame_pixels, shifts_y, shifts_x):

        def crop_one(move_y, move_x):
            return lax.dynamic_slice(
                frame_pixels, (REACH + move_y, REACH + move_x), (patch_size, patch_size)
            )

        return jax.vmap(crop_one)(shifts_y, shifts_x)

    cropped = jax.vmap(crop_all)(frame_pixels_all, list_y, list_x)
    unit_plane = jnp.ones((patch_size, patch_size), patch_raw.dtype)
    patch_sum = jnp.einsum("byx,yx->b", patch_raw, unit_plane, preferred_element_type=jnp.float32)
    patch_square = jnp.einsum(
        "byx,byx->b", patch_raw, patch_raw, preferred_element_type=jnp.float32
    )
    crop_sum = jnp.einsum("bsyx,yx->bs", cropped, unit_plane, preferred_element_type=jnp.float32)
    crop_square = jnp.einsum("bsyx,bsyx->bs", cropped, cropped, preferred_element_type=jnp.float32)
    cross_sum = jnp.einsum("byx,bsyx->bs", patch_raw, cropped, preferred_element_type=jnp.float32)
    patch_mean = patch_sum / pixel_count
    crop_mean = crop_sum / pixel_count
    patch_var = patch_square / pixel_count - patch_mean * patch_mean
    crop_var = crop_square / pixel_count - crop_mean * crop_mean
    cross_mean = cross_sum / pixel_count - patch_mean[:, None] * crop_mean
    correl = cross_mean / jnp.sqrt((patch_var[:, None] + EPSILON) * (crop_var + EPSILON))
    weight = (1.5 + correl) * (1.5 + correl)
    weight_sum = jnp.sum(weight, axis=1)
    along_y = jnp.sum(weight * list_y.astype(jnp.float32), axis=1) / (REACH * weight_sum)
    along_x = jnp.sum(weight * list_x.astype(jnp.float32), axis=1) / (REACH * weight_sum)
    return jnp.stack([along_y, along_x, weight_sum / cand_count])


def match_strip(patch_raw, frames, shift_list, live_count):
    shifts = shift_list.reshape(2, P_SIZE, NS)
    blocks = (live_count + BLK - 1) // BLK

    def one_block(block_index, result):
        block_start = (block_index * BLK).astype(jnp.int32)
        scored = match_block(
            lax.dynamic_slice_in_dim(patch_raw, block_start, BLK, 0),
            lax.dynamic_slice_in_dim(frames, block_start, BLK, 0),
            lax.dynamic_slice_in_dim(shifts[0], block_start, BLK, 0),
            lax.dynamic_slice_in_dim(shifts[1], block_start, BLK, 0),
        )
        return lax.dynamic_update_slice(result, scored, (jnp.zeros((), jnp.int32), block_start))

    result = lax.fori_loop(0, blocks, one_block, jnp.zeros((3, P_SIZE), jnp.float32))
    keeper = (jnp.arange(P_SIZE) < live_count).astype(jnp.float32)
    return result * keeper


def body(patches, windows, candidates, live, edges, stiffness):
    tile_row = lax.axis_index("row")
    tile_col = lax.axis_index("col")
    last_row = lax.axis_size("row") - 1
    last_col = lax.axis_size("col") - 1
    far_east = shifted(windows[0, 0, 0], "col", -1)
    far_south = shifted(windows[0, 0, 1], "row", -1)
    count_east = jnp.where(tile_col < last_col, live[tile_row, tile_col, 0], 0)
    count_south = jnp.where(tile_row < last_row, live[tile_row, tile_col, 1], 0)
    own_east = match_strip(patches[0, 0, 0], far_east, candidates[0, 0, 0], count_east)
    own_south = match_strip(patches[0, 0, 1], far_south, candidates[0, 0, 1], count_south)
    from_west = shifted(own_east, "col", 1)
    from_north = shifted(own_south, "row", 1)
    matches = jnp.stack([own_east, own_south])[None, None]
    slots = jnp.arange(P_SIZE)
    picker = (jnp.arange(GV)[None, :] == (slots * GV // P_SIZE)[:, None]).astype(jnp.float32)
    vertex = jnp.arange(GV * GV)
    incidence = (edges[0, 0][:, None] == vertex[None, :]).astype(jnp.float32) - (
        edges[0, 1][:, None] == vertex[None, :]
    ).astype(jnp.float32)
    spring = stiffness[0]

    def spread(values):
        return jnp.dot(values, picker, precision=PRECISE)

    def sample(values):
        return jnp.dot(values, picker.T, precision=PRECISE)

    conf_east = own_east[2]
    conf_south = own_south[2]
    conf_west = from_west[2]
    conf_north = from_north[2]
    forcing = jnp.zeros((2, GV, GV), jnp.float32)
    forcing = forcing.at[:, :, GV - 1].add(spread(conf_east * own_east[:2]))
    forcing = forcing.at[:, :, 0].add(-spread(conf_west * from_west[:2]))
    forcing = forcing.at[:, GV - 1, :].add(spread(conf_south * own_south[:2]))
    forcing = forcing.at[:, 0, :].add(-spread(conf_north * from_north[:2]))
    solution = jnp.zeros_like(forcing)
    residual = forcing

    def global_norm(values):
        return lax.psum(jnp.sum(values * values), ("row", "col"))

    direction = forcing
    norm_now = global_norm(residual)
    for iteration in range(ITERS):
        border = with_halo(direction, (("row", 1), ("col", 2)), 1)
        flat_field = direction.reshape(2, GV * GV)
        stretch = jnp.dot(flat_field, incidence.T, precision=PRECISE) * spring
        output = (LAMBDA_REG * flat_field + jnp.dot(stretch, incidence, precision=PRECISE)).reshape(
            2, GV, GV
        )
        output = output.at[:, :, GV - 1].add(
            spread(conf_east * sample(direction[:, :, GV - 1] - border[:, 1:-1, -1]))
        )
        output = output.at[:, :, 0].add(
            spread(conf_west * sample(direction[:, :, 0] - border[:, 1:-1, 0]))
        )
        output = output.at[:, GV - 1, :].add(
            spread(conf_south * sample(direction[:, GV - 1, :] - border[:, -1, 1:-1]))
        )
        output = output.at[:, 0, :].add(
            spread(conf_north * sample(direction[:, 0, :] - border[:, 0, 1:-1]))
        )
        step_length = norm_now / lax.psum(jnp.sum(direction * output), ("row", "col"))
        solution = solution + step_length * direction
        residual = residual - step_length * output
        norm_next = global_norm(residual)
        direction = residual + norm_next / norm_now * direction
        norm_now = norm_next
    mesh_shift = solution.reshape(2, GV * GV)[None, None]
    return (matches, mesh_shift)


def solution(mesh):
    return jax.shard_map(
        body,
        mesh=mesh,
        in_specs=(
            P("row", "col", None, None, None, None),
            P("row", "col", None, None, None),
            P("row", "col", None, None, None),
            P(),
            P("row", None, "col"),
            P("row", "col"),
        ),
        out_specs=(P("row", "col", None, None, None), P("row", "col", None, None)),
        check_vma=False,
    )
```

profile of v0, /device:TPU:1, one launch (start us, length us, event | category | flops | bytes accessed | tf_op | source)
XLA Modules:
  0.0 1201.1 jit_solution(6056158107751684459)
XLA Ops:
  0.7 2.9 slice_bitcast_fusion.1
  3.6 5.1 collective-permute-start.1
  15.8 7.0 collective-permute-done.1
  22.8 91.7 %while.49 = (s32[]{:T(128)}, f32[3,16]{1,0:T(4,128)S(1)}, s32[]{:T(128)}, bf16[16,128,128]{2,1,0:T(8,128)(2,1)S(1)}, bf16[16,36864]{1,0:T(8,128)(2,1)}, /*index=...) while((s32[]{:T(128)}, f32[3,16]{1,0:T(4,128)S(1)}, ...), condition=%wide.region_9.10_spmd, body=%wide.region_5.9_spmd.sunk | while | flops 5178357 | bytes 5322758 | solution.py:90
  25.1 87.7 %while.51 = (s32[]{:T(128)}, bf16[4,192,192]{2,1,0:T(8,128)(2,1)S(1)}, s32[32,3]{0,1:T(4,128)S(1)}, bf16[32,128,128]{2,1,0:T(8,128)(2,1)S(1)}, s32[]{:T(128)}) while((s32[]{:T(128)}, bf16[4,192,192]{2,1,0:T(8,128)(2,1)S(1)}, s32[32,3]{0,1:T(4,128)S(1)}, bf16[32,128,128]{2,1,0:T(8,128)(2,1)S(1)}, s32[]{:T(128)}) %tuple.208), condition=%wide.while_cond.17, body=%wide.while_body.17.sunk | while | flops 2 | bytes 65665 | solution.py:48
  25.7 2.0 dynamic-slice_dynamic-update-slice_fusion.4
  31.2 2.0 dynamic-slice_dynamic-update-slice_fusion.4
  34.0 2.0 dynamic-slice_dynamic-update-slice_fusion.4
  39.4 2.0 dynamic-slice_dynamic-update-slice_fusion.4
  42.2 2.0 dynamic-slice_dynamic-update-slice_fusion.4
  44.9 2.0 dynamic-slice_dynamic-update-slice_fusion.4
  47.7 2.0 dynamic-slice_dynamic-update-slice_fusion.4
  50.4 2.0 dynamic-slice_dynamic-update-slice_fusion.4
  53.1 2.0 dynamic-slice_dynamic-update-slice_fusion.4
  55.9 2.0 dynamic-slice_dynamic-update-slice_fusion.4
  58.6 2.0 dynamic-slice_dynamic-update-slice_fusion.4
  61.4 2.0 dynamic-slice_dynamic-update-slice_fusion.4
  116.5 88.6 %while.47 = (s32[]{:T(128)}, f32[3,16]{1,0:T(4,128)S(1)}, s32[]{:T(128)}, bf16[16,128,128]{2,1,0:T(8,128)(2,1)S(1)}, bf16[16,36864]{1,0:T(8,128)(2,1)}, /*index=...) while((s32[]{:T(128)}, f32[3,16]{1,0:T(4,128)S(1)}, ...), condition=%wide.region_4.5_spmd, body=%wide.region_0.4_spmd.sunk | while | flops 5178357 | bytes 5314510 | solution.py:90
  118.3 85.1 %while.50 = (s32[]{:T(128)}, bf16[4,192,192]{2,1,0:T(8,128)(2,1)S(1)}, s32[32,3]{0,1:T(4,128)S(1)}, bf16[32,128,128]{2,1,0:T(8,128)(2,1)S(1)}, s32[]{:T(128)}) while((s32[]{:T(128)}, bf16[4,192,192]{2,1,0:T(8,128)(2,1)S(1)}, s32[32,3]{0,1:T(4,128)S(1)}, bf16[32,128,128]{2,1,0:T(8,128)(2,1)S(1)}, s32[]{:T(128)}) %tuple.211), condition=%wide.while_cond.16, body=%wide.while_body.16.sunk | while | flops 2 | bytes 65665 | solution.py:48
  205.2 3.1 collective-permute-start.2
  210.7 3.1 collective-permute-start.5
  216.8 2.5 collective-permute-start.4
  222.2 94.5 %collective-permute-start.7 = (f32[2,18,1]{1,0,2:T(2,128)S(1)}, f32[2,18,1]{1,0,2:T(2,128)S(1)}, u32[]{:S(2)}, u32[]{:S(2)}) collective-permute-start(f32[2,18,1]{1,0,2:T(2,128)S(1)} %get-tuple-element.502), channel_id=1, source_target_pairs={{0,1},{1,2},{2,3},{3,4},{4,5},{5,6},{6,7},{7,8},{8,9},{9,10},{10,1... | collective-permute-start | bytes 440 | tf_op jit(solution)/shard_map/ppermute | solution.py:31
  319.9 532.2 %all-reduce.1 = (f32[]{:T(128)}, f32[]{:T(128)}) all-reduce(f32[]{:T(128)} %get-tuple-element.423, f32[]{:T(128)} %get-tuple-element.422), channel_id=1, replica_groups=mesh['row'=16,'col'=16] {'row','col'}, use_global_device_ids=true, to_apply=%region_11.12 | all-reduce | flops 2 | bytes 16 | tf_op jit(solution)/shard_map/psum | solution.py:136
  854.0 73.1 %psum.44 = f32[]{:T(128)} all-reduce(f32[]{:T(128)} %get-tuple-element.468), channel_id=1, replica_groups=mesh['row'=16,'col'=16] {'row','col'}, use_global_device_ids=true, to_apply=%region_15.16 | all-reduce | flops 1 | bytes 8 | tf_op jit(solution)/shard_map/psum | solution.py:136
  928.7 3.8 collective-permute-start.8
  940.2 4.2 collective-permute-start.11
  947.4 77.6 %psum.45 = f32[]{:T(128)} all-reduce(f32[]{:T(128)} %multiply_reduce_fusion.10), channel_id=1, replica_groups=mesh['row'=16,'col'=16] {'row','col'}, use_global_device_ids=true, to_apply=%region_17.18 | all-reduce | flops 1 | bytes 8 | tf_op jit(solution)/shard_map/psum | solution.py:159
  1026.9 73.2 %psum.46 = f32[]{:T(128)} all-reduce(f32[]{:T(128)} %multiply_reduce_fusion.9), channel_id=1, replica_groups=mesh['row'=16,'col'=16] {'row','col'}, use_global_device_ids=true, to_apply=%region_19.20 | all-reduce | flops 1 | bytes 8 | tf_op jit(solution)/shard_map/psum | solution.py:136
  1101.7 4.2 collective-permute-start.12
  1113.6 4.0 collective-permute-start.15
  1121.4 77.5 %psum.47 = f32[]{:T(128)} all-reduce(f32[]{:T(128)} %multiply_reduce_fusion.8), channel_id=1, replica_groups=mesh['row'=16,'col'=16] {'row','col'}, use_global_device_ids=true, to_apply=%region_21.22 | all-reduce | flops 1 | bytes 8 | tf_op jit(solution)/shard_map/psum | solution.py:159
  (382 shorter events, 197.8 us)
Async XLA Ops:
  0.6 12.1 %copy-start.10 = (s32[1,1,2,2,128]{4,3,2,1,0:T(2,128)S(1)}, s32[1,1,2,2,128]{4,3,2,1,0:T(2,128)}, u32[]{:S(2)}) copy-start(s32[1,1,2,2,128]{4,3,2,1,0:T(2,128)} %param.44) | copy-start | bytes 6148
  0.6 12.3 %copy-start.7 = (f32[1,705]{1,0:T(1,128)S(1)}, f32[1,705]{1,0:T(1,128)}, u32[]{:S(2)}) copy-start(f32[1,705]{1,0:T(1,128)} %param.47) | copy-start | bytes 8464
  0.7 14.4 %copy-start.3 = (s32[1,2,705]{2,1,0:T(2,128)S(1)}, s32[1,2,705]{2,1,0:T(2,128)}, u32[]{:S(2)}) copy-start(s32[1,2,705]{2,1,0:T(2,128)} %param.46) | copy-start | bytes 16924
  0.7 15.1 %copy-start = (bf16[1,1,2,16,128,128]{5,4,3,2,1,0:T(8,128)(2,1)S(1)}, bf16[1,1,2,16,128,128]{5,4,3,2,1,0:T(8,128)(2,1)}, u32[]{:S(2)}) copy-start(bf16[1,1,2,16,128,128]{5,4,3,2,1,0:T(8,128)(2,1)} %param.42) | copy-start | bytes 3145732
  3.6 19.2 %collective-permute-start.1 = (bf16[16,36864]{1,0:T(8,128)(2,1)S(1)}, bf16[16,36864]{1,0:T(8,128)(2,1)}, u32[]{:S(2)}, u32[]{:S(2)}) collective-permute-start(bf16[16,36864]{1,0:T(8,128)(2,1)S(1)} %get-tuple-element.495), channel_id=1, source_target_pairs={{16,0},{32,16},{48,32},{64,48},{80,64},{96,80},{112,96},{128,112},... | collective-permute-start | bytes 3538952 | tf_op jit(solution)/shard_map/ppermute | solution.py:23
  8.7 107.7 %collective-permute-start = (bf16[16,36864]{1,0:T(8,128)(2,1)}, bf16[16,36864]{1,0:T(8,128)(2,1)}, u32[]{:S(2)}, u32[]{:S(2)}) collective-permute-start(bf16[16,36864]{1,0:T(8,128)(2,1)} %get-tuple-element.494), channel_id=1, source_target_pairs={{1,0},{2,1},{3,2},{4,3},{5,4},{6,5},{7,6},{8,7},{9,8},{10,9},{11,1... | collective-permute-start | bytes 3538952 | tf_op jit(solution)/shard_map/ppermute | solution.py:23
  22.8 91.7 %copy-start.8 = (f32[16]{0:T(128)S(1)}, f32[16]{0:T(128)}, u32[]{:S(2)}) copy-start(f32[16]{0:T(128)} %compare_convert_fusion) | copy-start | bytes 196
  22.8 0.6 copy-start.1
  112.7 1.7 copy-start.2
  114.5 94.3 %collective-permute-start.3 = (f32[3,16]{1,0:T(4,128)S(1)}, f32[3,16]{1,0:T(4,128)S(1)}, u32[]{:S(2)}, u32[]{:S(2)}) collective-permute-start(f32[3,16]{1,0:T(4,128)S(1)} %broadcast_multiply_fusion.2), channel_id=1, source_target_pairs={{0,16},{16,32},{32,48},{48,64},{64,80},{80,96},{96,112},{112,128},... | collective-permute-start | bytes 584 | tf_op jit(solution)/shard_map/ppermute | solution.py:23
  116.4 88.7 %copy-start.9 = (f32[16]{0:T(128)S(1)}, f32[16]{0:T(128)}, u32[]{:S(2)}) copy-start(f32[16]{0:T(128)} %compare_convert_fusion.1) | copy-start | bytes 196
  116.5 91.9 %copy-start.11 = (s32[16]{0:T(128)S(1)}, s32[16]{0:T(128)}, u32[]{:S(2)}) copy-start(s32[16]{0:T(128)} %and_select_fusion) | copy-start | bytes 196
  116.5 97.7 %copy-start.4 = (s32[705]{0:T(1024)S(1)}, s32[705]{0:T(1024)}, u32[]{:S(2)}) copy-start(s32[705]{0:T(1024)} %get-tuple-element.424) | copy-start | bytes 8464
  116.5 97.7 %copy-start.5 = (s32[705]{0:T(1024)S(1)}, s32[705]{0:T(1024)}, u32[]{:S(2)}) copy-start(s32[705]{0:T(1024)} %get-tuple-element.425) | copy-start | bytes 8464
  116.5 97.7 %copy-start.6 = (f32[705]{0:T(1024)S(1)}, f32[705]{0:T(1024)}, u32[]{:S(2)}) copy-start(f32[705]{0:T(1024)} %reduce.44) | copy-start | bytes 8464
  205.2 4.0 collective-permute-start.2
  210.7 6.1 collective-permute-start.5
  216.8 3.4 collective-permute-start.4
  220.9 95.8 %collective-permute-start.6 = (f32[2,18,1]{1,0,2:T(2,128)S(1)}, f32[2,18,1]{1,0,2:T(2,128)S(1)}, u32[]{:S(2)}, u32[]{:S(2)}) collective-permute-start(f32[2,18,1]{1,0,2:T(2,128)S(1)} %get-tuple-element.503), channel_id=1, source_target_pairs={{1,0},{2,1},{3,2},{4,3},{5,4},{6,5},{7,6},{8,7},{9,8},{10,9},{11,1... | collective-permute-start | bytes 440 | tf_op jit(solution)/shard_map/ppermute | solution.py:34
  222.2 95.2 %collective-permute-start.7 = (f32[2,18,1]{1,0,2:T(2,128)S(1)}, f32[2,18,1]{1,0,2:T(2,128)S(1)}, u32[]{:S(2)}, u32[]{:S(2)}) collective-permute-start(f32[2,18,1]{1,0,2:T(2,128)S(1)} %get-tuple-element.502), channel_id=1, source_target_pairs={{0,1},{1,2},{2,3},{3,4},{4,5},{5,6},{6,7},{7,8},{8,9},{9,10},{10,1... | collective-permute-start | bytes 440 | tf_op jit(solution)/shard_map/ppermute | solution.py:31
  928.7 7.5 collective-permute-start.8
  932.5 5.1 collective-permute-start.9
  938.9 5.5 collective-permute-start.10
  940.2 4.7 collective-permute-start.11
  1101.7 7.9 collective-permute-start.12
  1105.9 5.1 collective-permute-start.13
  1112.4 5.3 collective-permute-start.14
  1113.6 4.7 collective-permute-start.15
where the time goes:
time: 1210 us; the launch traced here: 1200 us
  blocking collectives  834 us (69%)
  local copies, waits for them, and re-layouts  190 us (16%)
  starting transfers between devices  135 us (11%)
    psum x3, blocking collectives, global_norm(): return lax.psum(jnp.sum(values * values), ('row', 'col'))  679 us
    gather x192, local copies, waits for them, and re-layouts  172 us
    psum x2, blocking collectives, body(): lax.psum(jnp.sum(direction * output), ('row', 'col'))  155 us
    ppermute x6, starting transfers between devices, with_halo(): lax.ppermute(lax.slice_in_dim(block, block.shape[dim] - width, None, axis...  113 us
  transfers between devices with their start and end apart: 16, of which 8 were waited for; matrix products, arithmetic and copies ran while one was open for 16% of the time, Pallas kernels for 0%

commit v1 on v0

v1 whole, which is shorter than its diff:
```python
import functools

import jax
import jax.numpy as jnp
from jax import lax
from jax.experimental import pallas as pl
from jax.experimental.pallas import tpu as pltpu
from jax.sharding import PartitionSpec as P

PATCH = 128
REACH = 32
WIN = 192
NS = 8
P_SIZE = 16
GV = 16
E = 705
E_PAD = 768
LINES = WIN * WIN // 128
PIXELS = float(PATCH * PATCH)
LAMBDA_REG = 0.05
EPSILON = 1e-05
THETA = 8.0
PRECISE = lax.Precision.HIGHEST
F32 = jnp.float32
VMEM = pl.BlockSpec(memory_space=pltpu.VMEM)
SMEM = pl.BlockSpec(memory_space=pltpu.SMEM)


def shifted(x, axis, by):
    length = lax.axis_size(axis)
    pairs = [(i, i + by) for i in range(length) if 0 <= i + by < length]
    return lax.ppermute(x, axis, pairs)


def iota(shape, dim):
    return lax.broadcasted_iota(jnp.int32, shape, dim)


def nt_dot(a, b):
    return lax.dot_general(
        a, b, (((1,), (1,)), ((), ())), precision=PRECISE, preferred_element_type=F32
    )


def frames_kernel(win_ref, out_ref):
    for seam in range(2):

        def one_line(j, carry, seam=seam):
            at = pl.multiple_of(j * 128, 128)
            pixels = win_ref[seam, :, pl.ds(at, 128)].astype(F32)
            base = seam * P_SIZE * LINES + j
            out_ref[pl.ds(base, 8, stride=LINES), :] = pixels[:8]
            out_ref[pl.ds(base + 8 * LINES, 8, stride=LINES), :] = pixels[8:]
            return carry

        lax.fori_loop(0, LINES, one_line, 0, unroll=8)


def springs_kernel(edges_ref, stiff_ref, out_ref, ends_scr, stiff_scr):
    ends_scr[...] = jnp.zeros_like(ends_scr)
    stiff_scr[...] = jnp.zeros_like(stiff_scr)
    ends_scr[0:2, 0:E] = edges_ref[...]
    stiff_scr[0:1, 0:E] = stiff_ref[...]
    first, second = ends_scr[0:1], ends_scr[1:2]
    strength = stiff_scr[0:1]
    low, high = jnp.minimum(first, second), jnp.maximum(first, second)
    gap = high - low
    kind = jnp.where(gap == 1, 0, jnp.where(gap == GV, 1, jnp.where(gap == GV + 1, 2, 3)))
    row_of = kind * GV + (low >> 4)
    col_of = low & (GV - 1)
    left = jnp.where(iota((64, E_PAD), 0) == row_of, strength, 0.0)
    lanes = iota((128, E_PAD), 0)
    right = ((lanes == col_of + 16) | (lanes == col_of + 80)).astype(F32)
    out_ref[...] = nt_dot(left, right)


def match_kernel(seam, count_ref, cand_s, cand_v, patch_ref, frame_ref, *rest):
    if seam == 0:
        other_ref, out_ref, a_scr, t_scr, s_scr = rest
    else:
        out_ref, a_scr, t_scr, s_scr = rest
    count = count_ref[seam]
    lane = iota((8, 128), 1)
    row = iota((8, 128), 0)

    def one_patch(p, carry):
        pixels = patch_ref[p].astype(F32)
        a_scr[...] = pixels
        a_sum = pixels[0:8]
        a_sq = pixels[0:8] * pixels[0:8]
        for t in range(1, 16):
            part = pixels[8 * t : 8 * t + 8]
            a_sum = a_sum + part
            a_sq = a_sq + part * part
        base = (seam * P_SIZE + p) * LINES
        for s in range(NS):
            move_y = cand_s[0, p * NS + s] + REACH
            move_x = cand_s[1, p * NS + s] + REACH
            odd = move_y & 1
            even_at = base + 3 * ((move_y + odd) >> 1)
            odd_at = base + 3 * ((move_y - odd) >> 1)
            even_late = lane < move_x
            odd_late = lane < move_x + 64
            odd_roll = (move_x + 64) & 127
            cross = jnp.zeros((8, 128), F32)
            total = jnp.zeros((8, 128), F32)
            square = jnp.zeros((8, 128), F32)
            for t in range(8):
                even_b = jnp.where(
                    even_late,
                    frame_ref[pl.ds(even_at + 24 * t + 1, 8, stride=3), :],
                    frame_ref[pl.ds(even_at + 24 * t, 8, stride=3), :],
                )
                odd_b = jnp.where(
                    odd_late,
                    frame_ref[pl.ds(odd_at + 24 * t + 2, 8, stride=3), :],
                    frame_ref[pl.ds(odd_at + 24 * t + 1, 8, stride=3), :],
                )
                even_a = pltpu.roll(a_scr[pl.ds(odd + 16 * t, 8, stride=2), :], move_x, 1)
                odd_a = pltpu.roll(a_scr[pl.ds(1 - odd + 16 * t, 8, stride=2), :], odd_roll, 1)
                cross = cross + even_a * even_b + odd_a * odd_b
                total = total + (even_b + odd_b)
                square = square + even_b * even_b + odd_b * odd_b
            t_scr[8 * s : 8 * s + 8, :] = cross
            t_scr[64 + 8 * s : 72 + 8 * s, :] = total
            t_scr[128 + 8 * s : 136 + 8 * s, :] = square
        spot = pl.multiple_of(p * 8, 8)
        for q in range(3):
            part = t_scr[pl.ds(64 * q, 8, stride=8), :]
            for k in range(1, 8):
                part = part + t_scr[pl.ds(64 * q + k, 8, stride=8), :]
            s_scr[pl.ds(q * 128 + spot, 8), :] = part
        for q, part in ((3, a_sum), (4, a_sq)):
            s_scr[pl.ds(q * 128 + spot, 8), :] = jnp.broadcast_to(
                jnp.sum(part, axis=0, keepdims=True), (8, 128)
            )
        return carry

    lax.fori_loop(0, count, one_patch, 0)
    ones = jnp.ones((8, 128), F32)
    cross, total, square, a_sum, a_sq = (
        nt_dot(ones, s_scr[128 * q : 128 * q + 128, :]) / PIXELS for q in range(5)
    )
    cov = cross - a_sum * total
    var_a = a_sq - a_sum * a_sum
    var_b = square - total * total
    ncc = cov / jnp.sqrt((var_a + EPSILON) * (var_b + EPSILON))
    weight = jnp.where((lane >> 3) < count, (1.5 + ncc) * (1.5 + ncc), 0.0)
    list_y = cand_v[0:1, :].astype(F32)
    list_x = cand_v[1:2, :].astype(F32)
    parts = jnp.where(
        row == 0,
        weight,
        jnp.where(row == 1, weight * list_y, jnp.where(row == 2, weight * list_x, 0.0)),
    )

    col = iota((128, 128), 1)
    slot_of = jnp.where(
        col < 16,
        col,
        jnp.where(col < 32, col - 16, jnp.where((col >= 80) & (col < 96), col - 80, -1)),
    )
    group = ((iota((128, 128), 0) >> 3) == slot_of).astype(F32)
    sums = jnp.dot(parts, group, precision=PRECISE, preferred_element_type=F32)
    w_sum, w_y, w_x = sums[0:1], sums[1:2], sums[2:3]
    slot = slot_of[0:1]
    alive = (slot >= 0) & (slot < count)
    conf = jnp.where(alive, w_sum / NS, 0.0)
    along_y = jnp.where(alive, w_y / (REACH * w_sum), 0.0)
    along_x = jnp.where(alive, w_x / (REACH * w_sum), 0.0)
    lane1 = lane[0:1]
    if seam == 1:
        q_row = jnp.where(lane1 < 16, 0.0, conf)
        f_row = q_row * jnp.where(lane1 < 64, along_y, along_x)
        out_ref[0:1, :] = q_row
        out_ref[1:2, :] = f_row
        out_ref[2:3, :] = along_y
        out_ref[3:4, :] = along_x
        out_ref[4:5, :] = conf
        out_ref[5:8, :] = jnp.zeros((3, 128), F32)
    else:
        gather = ((iota((16, 128), 1) >> 3) == iota((16, 128), 0)).astype(F32)
        cols = nt_dot(gather, parts)
        c_sum, c_y, c_x = cols[:, 0:1], cols[:, 1:2], cols[:, 2:3]
        alive_c = iota((16, 1), 0) < count
        conf_c = jnp.where(alive_c, c_sum / NS, 0.0)
        y_c = conf_c * jnp.where(alive_c, c_y / (REACH * c_sum), 0.0)
        x_c = conf_c * jnp.where(alive_c, c_x / (REACH * c_sum), 0.0)
        lane16 = iota((16, 128), 1)
        low, high = lane16 == 15, lane16 == 79
        out_ref[0:16, :] = jnp.where(low | high, conf_c, 0.0)
        out_ref[16:32, :] = jnp.where(low, y_c, jnp.where(high, x_c, 0.0))
        out_ref[32:40, :] = other_ref[...]
        out_ref[40:41, :] = along_y
        out_ref[41:42, :] = along_x
        out_ref[42:43, :] = conf
        out_ref[43:48, :] = jnp.zeros((5, 128), F32)


def krylov_kernel(pw_ref, pc_ref, pe_ref, ww_ref, wc_ref, we_ref, u_ref, mom_ref, match_ref):
    lane = iota((48, 128), 1)
    row = iota((48, 128), 0)

    def placed(west, centre, east):
        return pltpu.roll(west, 112, 1) + centre + pltpu.roll(east, 16, 1)

    def plane(t):
        rows = slice(16 * t, 16 * t + 16)
        stack = [
            jnp.concatenate([ref[a, rows, :] for a in range(3)], axis=0)
            for ref in (pw_ref, pc_ref, pe_ref)
        ]
        return placed(*stack)

    def west_seam(lo):
        centre = jnp.concatenate([wc_ref[a, lo : lo + 16, :] for a in range(3)], axis=0)
        east = jnp.concatenate([we_ref[a, lo : lo + 16, :] for a in range(3)], axis=0)
        return centre + pltpu.roll(east, 16, 1)

    def north_seam(r):
        out = jnp.zeros((48, 128), F32)
        for a in (1, 2):
            line = placed(*(ref[a, r : r + 1, :] for ref in (ww_ref, wc_ref, we_ref)))
            out = jnp.where(row == 16 * a - 1, line, out)
        return out

    q_h = plane(0) + west_seam(0)
    q_v = plane(1) + north_seam(32)
    q_d = plane(2)
    q_a = plane(3)
    f_h = west_seam(16)
    f_v = north_seam(33)

    def right(x):
        return pltpu.roll(x, 1, 1)

    def left(x):
        return pltpu.roll(x, 127, 1)

    def down(x):
        return pltpu.roll(x, 1, 0)

    def up(x):
        return pltpu.roll(x, 47, 0)

    def operate(v):
        below = up(v)
        h = q_h * (v - left(v))
        s = q_v * (v - below)
        d = q_d * (v - left(below))
        a = q_a * (v - right(below))
        out = (LAMBDA_REG - THETA) * v + (h + s) + (d + a)
        return out - right(h + down(d)) - down(s + left(a))

    u0 = f_h + f_v - right(f_h) - down(f_v)
    u1 = operate(u0)
    u2 = operate(u1)
    u3 = operate(u2)
    own = slice(16, 32)
    lane16 = lane[own]
    inside = ((lane16 >= 16) & (lane16 < 32)) | ((lane16 >= 80) & (lane16 < 96))
    parts = [jnp.where(inside, x[own], 0.0) for x in (u0, u1, u2, u3)]
    lane1 = iota((1, 128), 1)
    moments = jnp.zeros((1, 128), F32)
    for k in range(6):
        product = parts[k // 2] * parts[k // 2 + k % 2]
        value = jnp.sum(jnp.sum(product, axis=0, keepdims=True), axis=1, keepdims=True)
        moments = jnp.where(lane1 == k, value, moments)
    for k in range(3):
        u_ref[k] = parts[k]
    mom_ref[...] = jnp.broadcast_to(moments[None], mom_ref.shape)
    match_ref[0] = we_ref[1, 40:43, 0:16]
    match_ref[1] = wc_ref[2, 34:37, 0:16]


def combine_kernel(mom_ref, u_ref, out_ref):
    total = jnp.sum(mom_ref[...], axis=0)
    m = [total[:, k : k + 1] for k in range(6)]

    def gram(p, lift):
        out = None
        for i in range(3):
            for j in range(i, 3):
                if p[i] is None or p[j] is None:
                    continue
                term = m[i + j]
                if lift:
                    term = m[i + j + 1] + THETA * term
                term = (term * p[i]) * p[j]
                if j > i:
                    term = term + term
                out = term if out is None else out + term
        return out

    one = jnp.ones((1, 1), F32)
    r = [one, None, None]
    d = r
    rr = m[0]
    x = [None, None, None]

    def plus(a, b):
        return b if a is None else a if b is None else a + b

    def times(s, a):
        return None if a is None else s * a

    for step in range(3):
        alpha = rr / gram(d, True)
        x = [plus(x[i], times(alpha, d[i])) for i in range(3)]
        if step == 2:
            break
        image = [times(THETA, d[0]), plus(d[0], times(THETA, d[1])), plus(d[1], times(THETA, d[2]))]
        r = [plus(r[i], times(-alpha, image[i])) for i in range(3)]
        new = gram(r, False)
        d = [plus(r[i], times(new / rr, d[i])) for i in range(3)]
        rr = new
    field = x[0] * u_ref[0] + x[1] * u_ref[1] + x[2] * u_ref[2]
    vertex = iota((128, 256), 1)
    source = iota((128, 256), 0)
    keep = iota((16, 256), 0) == (iota((16, 256), 1) >> 4)
    for comp in range(2):
        spread = (source == (vertex & 15) + (16 + 64 * comp)).astype(F32)
        wide = jnp.dot(field, spread, precision=PRECISE, preferred_element_type=F32)
        out_ref[comp : comp + 1, :] = jnp.sum(jnp.where(keep, wide, 0.0), axis=0, keepdims=True)


def shape(dims, dtype=F32):
    return jax.ShapeDtypeStruct(dims, dtype)


def with_sides(x, axis):
    return shifted(x, axis, 1), shifted(x, axis, -1)


def body(patches, windows, candidates, live, edges, stiffness):
    tile_row = lax.axis_index("row")
    tile_col = lax.axis_index("col")
    west_patches = shifted(patches[0, 0, 0], "col", 1)
    north_patches = shifted(patches[0, 0, 1], "row", 1)
    west_cand = shifted(candidates[0, 0, 0], "col", 1)
    north_cand = shifted(candidates[0, 0, 1], "row", 1)
    count_west = jnp.where(tile_col > 0, live[tile_row, jnp.maximum(tile_col - 1, 0), 0], 0)
    count_north = jnp.where(tile_row > 0, live[jnp.maximum(tile_row - 1, 0), tile_col, 1], 0)
    counts = jnp.stack([count_west, count_north])

    frames = pl.pallas_call(
        frames_kernel,
        out_shape=shape((2 * P_SIZE * LINES, 128)),
        in_specs=[VMEM],
        out_specs=VMEM,
        compiler_params=pltpu.CompilerParams(vmem_limit_bytes=40 * 1024 * 1024),
    )(windows[0, 0])
    springs = pl.pallas_call(
        springs_kernel,
        out_shape=shape((64, 128)),
        in_specs=[VMEM, VMEM],
        out_specs=VMEM,
        scratch_shapes=[pltpu.VMEM((8, E_PAD), jnp.int32), pltpu.VMEM((8, E_PAD), F32)],
    )(edges[0], stiffness)
    north, south = with_sides(springs, "row")
    springs_c = jnp.stack([north, springs, south])
    springs_w, springs_e = with_sides(springs_c, "col")

    def match(seam, cand, raw, *other):
        return pl.pallas_call(
            functools.partial(match_kernel, seam),
            out_shape=shape((48 if seam == 0 else 8, 128)),
            in_specs=[SMEM, SMEM, VMEM, VMEM, VMEM] + [VMEM] * len(other),
            out_specs=VMEM,
            scratch_shapes=[
                pltpu.VMEM((128, 128), F32),
                pltpu.VMEM((192, 128), F32),
                pltpu.VMEM((640, 128), F32),
            ],
            compiler_params=pltpu.CompilerParams(vmem_limit_bytes=40 * 1024 * 1024),
        )(counts, cand, cand, raw, frames, *other)

    seam_north = match(1, north_cand, north_patches)
    seams = match(0, west_cand, west_patches, seam_north)
    north, south = with_sides(seams, "row")
    seams_c = jnp.stack([north, seams, south])
    seams_w, seams_e = with_sides(seams_c, "col")
    devices = lax.axis_size("row") * lax.axis_size("col")
    basis, moments, matches = pl.pallas_call(
        krylov_kernel,
        out_shape=(shape((3, 16, 128)), shape((devices, 1, 128)), shape((2, 3, P_SIZE))),
        in_specs=[VMEM] * 6,
        out_specs=(VMEM, VMEM, VMEM),
    )(springs_w, springs_c, springs_e, seams_w, seams_c, seams_e)
    moments = lax.all_to_all(moments, ("row", "col"), 0, 0)
    mesh_shift = pl.pallas_call(
        combine_kernel,
        out_shape=shape((2, GV * GV)),
        in_specs=[VMEM, VMEM],
        out_specs=VMEM,
    )(moments, basis)
    return matches[None, None], mesh_shift[None, None]


def solution(mesh):
    return jax.shard_map(
        body,
        mesh=mesh,
        in_specs=(
            P("row", "col", None, None, None, None),
            P("row", "col", None, None, None),
            P("row", "col", None, None, None),
            P(),
            P("row", None, "col"),
            P("row", "col"),
        ),
        out_specs=(P("row", "col", None, None, None), P("row", "col", None, None)),
        check_vma=False,
    )
```

time: 1210 us -> 99.9 us (0.08)
  blocking collectives: 834 us -> 0 us
  local copies, waits for them, and re-layouts: 190 us -> 7.51 us
  starting transfers between devices: 135 us -> 60.4 us
  Pallas kernels: 0 us -> 15.2 us
    psum x5 -> x0, blocking collectives: 834 us -> none  [the longest x3 679 us: global_norm(): return lax.psum(jnp.sum(values * values), ('row', 'col'))]
    gather x194 -> x0, local copies, waits for them, and re-layouts: 172 us -> none
    ppermute x12 -> x0, starting transfers between devices: 124 us -> none  [the longest x6 113 us: with_halo(): lax.ppermute(lax.slice_in_dim(block, block.shape[dim] - width, None, axis...]
    all_to_all x0 -> x1, starting transfers between devices: none -> 24.9 us  [body(): moments = lax.all_to_all(moments, ('row', 'col'), 0, 0)]
    ppermute x4 -> x12, starting transfers between devices: 11.5 us -> 35.5 us  [shifted(): return lax.ppermute(x, axis, pairs)]
    pallas_call x0 -> x6, Pallas kernels: none -> 15.2 us  [the longest x1 4.26 us: body(): pl.pallas_call(frames_kernel, out_shape=shape((2 * P_SIZE * LINES, 128)),...]
  transfers between devices with their start and end apart: 16 -> 13, of which waited for: 8 -> 3; matrix products, arithmetic and copies ran while one was open for 16% -> 3% of each run, Pallas kernels for 0% -> 10%
where the time goes in v1:
time: 99.9 us; the launch traced here: 99.2 us
  starting transfers between devices  60.4 us (60%)
  Pallas kernels  15.2 us (15%)
  waiting for transfers between devices  13.7 us (14%)
  local copies, waits for them, and re-layouts  7.51 us (8%)
  between operations  2.24 us (2%)
    ppermute x12, starting transfers between devices, shifted(): return lax.ppermute(x, axis, pairs)  35.5 us
    all_to_all x1, starting transfers between devices, body(): moments = lax.all_to_all(moments, ('row', 'col'), 0, 0)  24.9 us
    all_to_all x1, waiting for transfers between devices, body(): moments = lax.all_to_all(moments, ('row', 'col'), 0, 0)  11.8 us
    pallas_call x1, Pallas kernels, body(): pl.pallas_call(frames_kernel, out_shape=shape((2 * P_SIZE * LINES, 128)),...  4.26 us
    pallas_call x2, Pallas kernels, match(): pl.pallas_call(functools.partial(match_kernel, seam), out_shape=shape((48...  3.68 us
    unnamed x18, local copies, waits for them, and re-layouts  2.96 us
    pallas_call x1, Pallas kernels, body(): pl.pallas_call(combine_kernel, out_shape=shape((2, GV * GV)), in_specs=[V...  2.86 us
    pallas_call x1, Pallas kernels, body(): pl.pallas_call(krylov_kernel, out_shape=(shape((3, 16, 128)), shape((devi...  2.5 us
  transfers between devices with their start and end apart: 13, of which 3 were waited for; matrix products, arithmetic and copies ran while one was open for 3% of the time, Pallas kernels for 10%

profile of v1, /device:TPU:1, one launch (start us, length us, event | category | flops | bytes accessed | tf_op | source)
XLA Modules:
  0.0 99.2 jit_solution(9073021962183575096)
XLA Ops:
  0.6 1.3 %slice_bitcast_fusion = (bf16[16,128,128]{2,1,0:T(8,128)(2,1)S(1)}, bf16[16,128,128]{2,1,0:T(8,128)(2,1)S(1)}) fusion(bf16[1,1,2,16,128,128]{5,4,3,2,1,0:T(8,128)(2,1)} %param.6), kind=kLoop, calls=%fused_computation | loop fusion | bytes 2097152 | tf_op jit(solution)/shard_map/squeeze | solution.py:339
  1.9 4.9 %collective-permute-start.7 = (bf16[16,128,128]{2,1,0:T(8,128)(2,1)S(1)}, bf16[16,128,128]{2,1,0:T(8,128)(2,1)S(1)}, u32[]{:S(2)}, u32[]{:S(2)}) collective-permute-start(bf16[16,128,128]{2,1,0:T(8,128)(2,1)S(1)} %get-tuple-element.8), channel_id=1, source_target_pairs={{0,16},{16,32},{32,48},{48,64},{64,80},{80,96},{96,112},{112,128},... | collective-permute-start | bytes 1572872 | tf_op jit(solution)/shard_map/ppermute | solution.py:32
  6.9 3.1 %collective-permute-start.5 = (bf16[16,128,128]{2,1,0:T(8,128)(2,1)S(1)}, bf16[16,128,128]{2,1,0:T(8,128)(2,1)S(1)}, u32[]{:S(2)}, u32[]{:S(2)}) collective-permute-start(bf16[16,128,128]{2,1,0:T(8,128)(2,1)S(1)} %get-tuple-element.9), channel_id=1, source_target_pairs={{0,1},{1,2},{2,3},{3,4},{4,5},{5,6},{6,7},{7,8},{8,9},{9,10},{10,1... | collective-permute-start | bytes 1572872 | tf_op jit(solution)/shard_map/ppermute | solution.py:32
  10.0 1.9 %shard_map.77 = f32[64,128]{1,0:T(8,128)} custom-call(s32[2,705]{1,0:T(2,128)} %bitcast.31, f32[1,705]{1,0:T(1,128)} %stiff_ref.1), custom_call_target="tpu_custom_call" | custom-call | tf_op jit(solution)/shard_map/pallas_call | solution.py:353
  12.0 1.9 %collective-permute-start.1 = (f32[64,128]{1,0:T(8,128)}, f32[64,128]{1,0:T(8,128)S(1)}, u32[]{:S(2)}, u32[]{:S(2)}) collective-permute-start(f32[64,128]{1,0:T(8,128)} %shard_map.77), channel_id=1, source_target_pairs={{16,0},{32,16},{48,32},{64,48},{80,64},{96,80},{112,96},{128,112},... | collective-permute-start | bytes 98312 | tf_op jit(solution)/shard_map/ppermute | solution.py:32
  13.9 3.6 %collective-permute-start = (f32[64,128]{1,0:T(8,128)}, f32[64,128]{1,0:T(8,128)S(1)}, u32[]{:S(2)}, u32[]{:S(2)}) collective-permute-start(f32[64,128]{1,0:T(8,128)} %shard_map.77), channel_id=1, source_target_pairs={{0,16},{16,32},{32,48},{48,64},{64,80},{80,96},{96,112},{112,128},... | collective-permute-start | bytes 98312 | tf_op jit(solution)/shard_map/ppermute | solution.py:32
  17.5 0.7 slice_bitcast_fusion.2
  18.2 2.2 %collective-permute-start.6 = (s32[2,128]{1,0:T(2,128)S(1)}, s32[2,128]{1,0:T(2,128)S(1)}, u32[]{:S(2)}, u32[]{:S(2)}) collective-permute-start(s32[2,128]{1,0:T(2,128)S(1)} %get-tuple-element.12), channel_id=1, source_target_pairs={{0,16},{16,32},{32,48},{48,64},{64,80},{80,96},{96,112},{112,128},... | collective-permute-start | bytes 3080 | tf_op jit(solution)/shard_map/ppermute | solution.py:32
  20.4 1.3 %constant_dynamic-slice_fusion.1 = (s32[1,1,1]{1,2,0:T(1,128)}, s32[1,1,1]{1,2,0:T(1,128)}) fusion(s32[16,16,2]{1,2,0:T(2,128)} %param.9, s32[]{:T(128)S(6)} %select_n.15, s32[]{:T(128)S(6)} %max.6, s32[]{:T(128)S(6)} %max.7, s32[]{:T(128)S(6)} %select_n.17), kind=kLoop, calls=%fused_computation.9 | loop fusion | bytes 32 | tf_op jit(solution)/shard_map/dynamic_slice | solution.py:342
  23.0 0.0 collective-permute-done.6.cand_s.cand_v
  23.0 3.1 %collective-permute-start.4 = (s32[2,128]{1,0:T(2,128)S(1)}, s32[2,128]{1,0:T(2,128)S(1)}, u32[]{:S(2)}, u32[]{:S(2)}) collective-permute-start(s32[2,128]{1,0:T(2,128)S(1)} %get-tuple-element.13), channel_id=1, source_target_pairs={{0,1},{1,2},{2,3},{3,4},{4,5},{5,6},{6,7},{7,8},{8,9},{9,10},{10,1... | collective-permute-start | bytes 3080 | tf_op jit(solution)/shard_map/ppermute | solution.py:32
  26.1 0.1 pad_add_fusion.count_ref
  26.2 1.7 %copy-done = bf16[1,1,2,16,36864]{4,3,2,1,0:T(8,128)(2,1)S(1)} copy-done((bf16[1,1,2,16,36864]{4,3,2,1,0:T(8,128)(2,1)S(1)}, bf16[1,1,2,16,36864]{4,3,2,1,0:T(8,128)(2,1)}, u32[]{:S(2)}) %copy-start) | copy-done | bytes 2359320
  27.9 4.3 %shard_map.78.frame_ref = f32[9216,128]{1,0:T(8,128)S(1)} custom-call(bf16[2,16,36864]{2,1,0:T(8,128)(2,1)S(1)} %bitcast.24), custom_call_target="tpu_custom_call" | custom-call | tf_op jit(solution)/shard_map/pallas_call | solution.py:346
  32.2 2.0 %shard_map.79.rest_0_ = f32[8,128]{1,0:T(8,128)S(1)} custom-call(s32[2]{0:T(128)S(1)} %pad_add_fusion.count_ref, s32[2,128]{1,0:T(2,128)S(1)} %collective-permute-done.6.cand_s.cand_v, s32[2,128]{1,0:T(2,128)S(1)} %collective-permute-done.6.cand_s.cand_v, bf16[16,128,128]{2,1,0:T(8,128)(2,1)S(1)} %collective-permute-done.7.patch_ref, ...), custom_call_target="tpu_custom_call" | custom-call | tf_op jit(solution)/shard_map/pallas_call | solution.py:365
  34.2 0.0 collective-permute-done.4.cand_s.cand_v
  34.2 1.7 %shard_map.80 = f32[48,128]{1,0:T(8,128)S(1)} custom-call(s32[2]{0:T(128)S(1)} %pad_add_fusion.count_ref, s32[2,128]{1,0:T(2,128)S(1)} %collective-permute-done.4.cand_s.cand_v, s32[2,128]{1,0:T(2,128)S(1)} %collective-permute-done.4.cand_s.cand_v, bf16[16,128,128]{2,1,0:T(8,128)(2,1)S(1)} %collective-permute-done.5.patch_ref, ...), custom_call_target="tpu_custom_call" | custom-call | tf_op jit(solution)/shard_map/pallas_call | solution.py:365
  35.9 2.0 %collective-permute-start.9 = (f32[48,128]{1,0:T(8,128)S(1)}, f32[48,128]{1,0:T(8,128)S(1)}, u32[]{:S(2)}, u32[]{:S(2)}) collective-permute-start(f32[48,128]{1,0:T(8,128)S(1)} %shard_map.80), channel_id=1, source_target_pairs={{16,0},{32,16},{48,32},{64,48},{80,64},{96,80},{112,96},{128,112},... | collective-permute-start | bytes 73736 | tf_op jit(solution)/shard_map/ppermute | solution.py:32
  37.9 3.9 %collective-permute-start.8 = (f32[48,128]{1,0:T(8,128)S(1)}, f32[48,128]{1,0:T(8,128)S(1)}, u32[]{:S(2)}, u32[]{:S(2)}) collective-permute-start(f32[48,128]{1,0:T(8,128)S(1)} %shard_map.80), channel_id=1, source_target_pairs={{0,16},{16,32},{32,48},{48,64},{64,80},{80,96},{96,112},{112,128},... | collective-permute-start | bytes 73736 | tf_op jit(solution)/shard_map/ppermute | solution.py:32
  41.8 1.3 %collective-permute-start.3 = (f32[3,64,128]{2,1,0:T(8,128)S(1)}, f32[3,64,128]{2,1,0:T(8,128)S(1)}, u32[]{:S(2)}, u32[]{:S(2)}) collective-permute-start(f32[3,64,128]{2,1,0:T(8,128)S(1)} %pad_maximum_fusion.pc_ref), channel_id=1, source_target_pairs={{1,0},{2,1},{3,2},{4,3},{5,4},{6,5},{7,6},{8,7},{9,8},{10,9},{11,1... | collective-permute-start | bytes 294920 | tf_op jit(solution)/shard_map/ppermute | solution.py:32
  43.1 4.2 %collective-permute-start.2 = (f32[3,64,128]{2,1,0:T(8,128)S(1)}, f32[3,64,128]{2,1,0:T(8,128)S(1)}, u32[]{:S(2)}, u32[]{:S(2)}) collective-permute-start(f32[3,64,128]{2,1,0:T(8,128)S(1)} %pad_maximum_fusion.pc_ref), channel_id=1, source_target_pairs={{0,1},{1,2},{2,3},{3,4},{4,5},{5,6},{6,7},{7,8},{8,9},{9,10},{10,1... | collective-permute-start | bytes 294920 | tf_op jit(solution)/shard_map/ppermute | solution.py:32
  47.4 1.3 %collective-permute-start.11 = (f32[3,48,128]{2,1,0:T(8,128)S(1)}, f32[3,48,128]{2,1,0:T(8,128)S(1)}, u32[]{:S(2)}, u32[]{:S(2)}) collective-permute-start(f32[3,48,128]{2,1,0:T(8,128)S(1)} %pad_maximum_fusion.1.wc_ref), channel_id=1, source_target_pairs={{1,0},{2,1},{3,2},{4,3},{5,4},{6,5},{7,6},{8,7},{9,8},{10,9},{11,1... | collective-permute-start | bytes 221192 | tf_op jit(solution)/shard_map/ppermute | solution.py:32
  48.7 4.0 %collective-permute-start.10 = (f32[3,48,128]{2,1,0:T(8,128)S(1)}, f32[3,48,128]{2,1,0:T(8,128)S(1)}, u32[]{:S(2)}, u32[]{:S(2)}) collective-permute-start(f32[3,48,128]{2,1,0:T(8,128)S(1)} %pad_maximum_fusion.1.wc_ref), channel_id=1, source_target_pairs={{0,1},{1,2},{2,3},{3,4},{4,5},{5,6},{6,7},{7,8},{8,9},{9,10},{10,1... | collective-permute-start | bytes 221192 | tf_op jit(solution)/shard_map/ppermute | solution.py:32
  52.7 0.1 collective-permute-done.11.we_ref
  52.8 1.8 %collective-permute-done.10.ww_ref = f32[3,48,128]{2,1,0:T(8,128)S(1)} collective-permute-done((f32[3,48,128]{2,1,0:T(8,128)S(1)}, f32[3,48,128]{2,1,0:T(8,128)S(1)}, u32[]{:S(2)}, u32[]{:S(2)}) %collective-permute-start.10) | collective-permute-done | bytes 73760 | tf_op jit(solution)/shard_map/ppermute | solution.py:32
  54.6 0.6 copy-done.8
  55.2 2.5 %shard_map.81 = (f32[3,16,128]{2,1,0:T(8,128)}, f32[256,1,128]{2,1,0:T(1,128)}, f32[2,3,16]{2,1,0:T(4,128)}) custom-call(f32[3,64,128]{2,1,0:T(8,128)} %copy-done.6, f32[3,64,128]{2,1,0:T(8,128)} %copy-done.2, f32[3,64,128]{2,1,0:T(8,128)} %copy-done.5, f32[3,48,128]{2,1,0:T(8,128)} %copy-done.8, f32[3,48,128]{2,1,0:T(8,128)} %copy-done.3, ...), custom_call_target="tpu_custom_call" | custom-call | tf_op jit(solution)/shard_map/pallas_call | solution.py:384
  57.7 24.9 %all-to-all-start = ((f32[256,1,128]{2,1,0:T(1,128)}), f32[256,1,128]{2,1,0:T(1,128)S(1)}, u32[]{:S(2)}, u32[]{:S(2)}) async-start(f32[256,1,128]{2,1,0:T(1,128)} %get-tuple-element.6), calls=%async_computation | async-start | bytes 262144 | tf_op jit(solution)/shard_map/all_to_all | solution.py:390
  82.6 1.3 %copy.10 = f32[2,3,16]{2,0,1:T(2,128)} copy(f32[2,3,16]{2,1,0:T(4,128)} %get-tuple-element.5) | data formatting | bytes 768 | tf_op jit(solution)/shard_map/pallas_call | solution.py:384
  83.8 11.8 %all-to-all-done.mom_ref = f32[256,1,128]{2,1,0:T(1,128)S(1)} async-done(((f32[256,1,128]{2,1,0:T(1,128)}), f32[256,1,128]{2,1,0:T(1,128)S(1)}, u32[]{:S(2)}, u32[]{:S(2)}) %all-to-all-start) | async-done | bytes 131104 | tf_op jit(solution)/shard_map/all_to_all | solution.py:390
  95.7 0.7 copy-done.1
  96.3 2.9 %shard_map.82 = f32[2,256]{1,0:T(2,128)} custom-call(f32[256,1,128]{2,1,0:T(1,128)} %copy-done.1, f32[3,16,128]{2,1,0:T(8,128)} %get-tuple-element.7.u_ref), custom_call_target="tpu_custom_call" | custom-call | tf_op jit(solution)/shard_map/pallas_call | solution.py:391
  (25 shorter events, 0.1 us)
Async XLA Ops:
  1.9 30.2 %collective-permute-start.7 = (bf16[16,128,128]{2,1,0:T(8,128)(2,1)S(1)}, bf16[16,128,128]{2,1,0:T(8,128)(2,1)S(1)}, u32[]{:S(2)}, u32[]{:S(2)}) collective-permute-start(bf16[16,128,128]{2,1,0:T(8,128)(2,1)S(1)} %get-tuple-element.8), channel_id=1, source_target_pairs={{0,16},{16,32},{32,48},{48,64},{64,80},{80,96},{96,112},{112,128},... | collective-permute-start | bytes 1572872 | tf_op jit(solution)/shard_map/ppermute | solution.py:32
  6.9 27.3 %collective-permute-start.5 = (bf16[16,128,128]{2,1,0:T(8,128)(2,1)S(1)}, bf16[16,128,128]{2,1,0:T(8,128)(2,1)S(1)}, u32[]{:S(2)}, u32[]{:S(2)}) collective-permute-start(bf16[16,128,128]{2,1,0:T(8,128)(2,1)S(1)} %get-tuple-element.9), channel_id=1, source_target_pairs={{0,1},{1,2},{2,3},{3,4},{4,5},{5,6},{6,7},{7,8},{8,9},{9,10},{10,1... | collective-permute-start | bytes 1572872 | tf_op jit(solution)/shard_map/ppermute | solution.py:32
  12.0 29.8 %collective-permute-start.1 = (f32[64,128]{1,0:T(8,128)}, f32[64,128]{1,0:T(8,128)S(1)}, u32[]{:S(2)}, u32[]{:S(2)}) collective-permute-start(f32[64,128]{1,0:T(8,128)} %shard_map.77), channel_id=1, source_target_pairs={{16,0},{32,16},{48,32},{64,48},{80,64},{96,80},{112,96},{128,112},... | collective-permute-start | bytes 98312 | tf_op jit(solution)/shard_map/ppermute | solution.py:32
  13.9 27.9 %collective-permute-start = (f32[64,128]{1,0:T(8,128)}, f32[64,128]{1,0:T(8,128)S(1)}, u32[]{:S(2)}, u32[]{:S(2)}) collective-permute-start(f32[64,128]{1,0:T(8,128)} %shard_map.77), channel_id=1, source_target_pairs={{0,16},{16,32},{32,48},{48,64},{64,80},{80,96},{96,112},{112,128},... | collective-permute-start | bytes 98312 | tf_op jit(solution)/shard_map/ppermute | solution.py:32
  18.2 4.8 %collective-permute-start.6 = (s32[2,128]{1,0:T(2,128)S(1)}, s32[2,128]{1,0:T(2,128)S(1)}, u32[]{:S(2)}, u32[]{:S(2)}) collective-permute-start(s32[2,128]{1,0:T(2,128)S(1)} %get-tuple-element.12), channel_id=1, source_target_pairs={{0,16},{16,32},{32,48},{48,64},{64,80},{80,96},{96,112},{112,128},... | collective-permute-start | bytes 3080 | tf_op jit(solution)/shard_map/ppermute | solution.py:32
  23.0 11.1 %collective-permute-start.4 = (s32[2,128]{1,0:T(2,128)S(1)}, s32[2,128]{1,0:T(2,128)S(1)}, u32[]{:S(2)}, u32[]{:S(2)}) collective-permute-start(s32[2,128]{1,0:T(2,128)S(1)} %get-tuple-element.13), channel_id=1, source_target_pairs={{0,1},{1,2},{2,3},{3,4},{4,5},{5,6},{6,7},{7,8},{8,9},{9,10},{10,1... | collective-permute-start | bytes 3080 | tf_op jit(solution)/shard_map/ppermute | solution.py:32
  26.2 1.7 %copy-start = (bf16[1,1,2,16,36864]{4,3,2,1,0:T(8,128)(2,1)S(1)}, bf16[1,1,2,16,36864]{4,3,2,1,0:T(8,128)(2,1)}, u32[]{:S(2)}) copy-start(bf16[1,1,2,16,36864]{4,3,2,1,0:T(8,128)(2,1)} %param.7) | copy-start | bytes 7077892
  32.1 9.6 %copy-start.4 = (f32[64,128]{1,0:T(8,128)S(1)}, f32[64,128]{1,0:T(8,128)}, u32[]{:S(2)}) copy-start(f32[64,128]{1,0:T(8,128)} %shard_map.77) | copy-start | bytes 98308
  35.9 11.4 %collective-permute-start.9 = (f32[48,128]{1,0:T(8,128)S(1)}, f32[48,128]{1,0:T(8,128)S(1)}, u32[]{:S(2)}, u32[]{:S(2)}) collective-permute-start(f32[48,128]{1,0:T(8,128)S(1)} %shard_map.80), channel_id=1, source_target_pairs={{16,0},{32,16},{48,32},{64,48},{80,64},{96,80},{112,96},{128,112},... | collective-permute-start | bytes 73736 | tf_op jit(solution)/shard_map/ppermute | solution.py:32
  37.9 9.5 %collective-permute-start.8 = (f32[48,128]{1,0:T(8,128)S(1)}, f32[48,128]{1,0:T(8,128)S(1)}, u32[]{:S(2)}, u32[]{:S(2)}) collective-permute-start(f32[48,128]{1,0:T(8,128)S(1)} %shard_map.80), channel_id=1, source_target_pairs={{0,16},{16,32},{32,48},{48,64},{64,80},{80,96},{96,112},{112,128},... | collective-permute-start | bytes 73736 | tf_op jit(solution)/shard_map/ppermute | solution.py:32
  41.8 12.7 %copy-start.2 = (f32[3,64,128]{2,1,0:T(8,128)}, f32[3,64,128]{2,1,0:T(8,128)S(1)}, u32[]{:S(2)}) copy-start(f32[3,64,128]{2,1,0:T(8,128)S(1)} %pad_maximum_fusion.pc_ref) | copy-start | bytes 294916
  41.8 10.8 %collective-permute-start.3 = (f32[3,64,128]{2,1,0:T(8,128)S(1)}, f32[3,64,128]{2,1,0:T(8,128)S(1)}, u32[]{:S(2)}, u32[]{:S(2)}) collective-permute-start(f32[3,64,128]{2,1,0:T(8,128)S(1)} %pad_maximum_fusion.pc_ref), channel_id=1, source_target_pairs={{1,0},{2,1},{3,2},{4,3},{5,4},{6,5},{7,6},{8,7},{9,8},{10,9},{11,1... | collective-permute-start | bytes 294920 | tf_op jit(solution)/shard_map/ppermute | solution.py:32
  43.1 9.6 %collective-permute-start.2 = (f32[3,64,128]{2,1,0:T(8,128)S(1)}, f32[3,64,128]{2,1,0:T(8,128)S(1)}, u32[]{:S(2)}, u32[]{:S(2)}) collective-permute-start(f32[3,64,128]{2,1,0:T(8,128)S(1)} %pad_maximum_fusion.pc_ref), channel_id=1, source_target_pairs={{0,1},{1,2},{2,3},{3,4},{4,5},{5,6},{6,7},{7,8},{8,9},{9,10},{10,1... | collective-permute-start | bytes 294920 | tf_op jit(solution)/shard_map/ppermute | solution.py:32
  47.4 7.2 %copy-start.3 = (f32[3,48,128]{2,1,0:T(8,128)}, f32[3,48,128]{2,1,0:T(8,128)S(1)}, u32[]{:S(2)}) copy-start(f32[3,48,128]{2,1,0:T(8,128)S(1)} %pad_maximum_fusion.1.wc_ref) | copy-start | bytes 221188
  47.4 5.4 %collective-permute-start.11 = (f32[3,48,128]{2,1,0:T(8,128)S(1)}, f32[3,48,128]{2,1,0:T(8,128)S(1)}, u32[]{:S(2)}, u32[]{:S(2)}) collective-permute-start(f32[3,48,128]{2,1,0:T(8,128)S(1)} %pad_maximum_fusion.1.wc_ref), channel_id=1, source_target_pairs={{1,0},{2,1},{3,2},{4,3},{5,4},{6,5},{7,6},{8,7},{9,8},{10,9},{11,1... | collective-permute-start | bytes 221192 | tf_op jit(solution)/shard_map/ppermute | solution.py:32
  48.7 5.9 %collective-permute-start.10 = (f32[3,48,128]{2,1,0:T(8,128)S(1)}, f32[3,48,128]{2,1,0:T(8,128)S(1)}, u32[]{:S(2)}, u32[]{:S(2)}) collective-permute-start(f32[3,48,128]{2,1,0:T(8,128)S(1)} %pad_maximum_fusion.1.wc_ref), channel_id=1, source_target_pairs={{0,1},{1,2},{2,3},{3,4},{4,5},{5,6},{6,7},{7,8},{8,9},{9,10},{10,1... | collective-permute-start | bytes 221192 | tf_op jit(solution)/shard_map/ppermute | solution.py:32
  52.7 1.9 %copy-start.5 = (f32[3,64,128]{2,1,0:T(8,128)}, f32[3,64,128]{2,1,0:T(8,128)S(1)}, u32[]{:S(2)}) copy-start(f32[3,64,128]{2,1,0:T(8,128)S(1)} %collective-permute-done.3.pe_ref) | copy-start | bytes 294916
  52.7 1.8 %copy-start.6 = (f32[3,64,128]{2,1,0:T(8,128)}, f32[3,64,128]{2,1,0:T(8,128)S(1)}, u32[]{:S(2)}) copy-start(f32[3,64,128]{2,1,0:T(8,128)S(1)} %collective-permute-done.2.pw_ref) | copy-start | bytes 294916
  52.8 1.8 %copy-start.7 = (f32[3,48,128]{2,1,0:T(8,128)}, f32[3,48,128]{2,1,0:T(8,128)S(1)}, u32[]{:S(2)}) copy-start(f32[3,48,128]{2,1,0:T(8,128)S(1)} %collective-permute-done.11.we_ref) | copy-start | bytes 221188
  54.5 0.6 copy-start.8
  57.7 38.0 %all-to-all-start = ((f32[256,1,128]{2,1,0:T(1,128)}), f32[256,1,128]{2,1,0:T(1,128)S(1)}, u32[]{:S(2)}, u32[]{:S(2)}) async-start(f32[256,1,128]{2,1,0:T(1,128)} %get-tuple-element.6), calls=%async_computation | async-start | bytes 262144 | tf_op jit(solution)/shard_map/all_to_all | solution.py:390
  95.7 0.7 copy-start.1

commit v2 on v1

v2 whole, which is shorter than its diff:
```python
import functools

import jax
import jax.numpy as jnp
from jax import lax
from jax.experimental import pallas as pl
from jax.experimental.pallas import tpu as pltpu
from jax.sharding import PartitionSpec as P

PATCH = 128
REACH = 32
WIN = 192
NS = 8
P_SIZE = 16
GV = 16
E = 705
E_PAD = 768
LINES = WIN * WIN // 128
PIXELS = float(PATCH * PATCH)
LAMBDA_REG = 0.05
EPSILON = 1e-05
THETA = 8.0
PRECISE = lax.Precision.HIGHEST
F32 = jnp.float32
VMEM = pl.BlockSpec(memory_space=pltpu.VMEM)
SMEM = pl.BlockSpec(memory_space=pltpu.SMEM)


def shifted(x, axis, by):
    length = lax.axis_size(axis)
    pairs = [(i, i + by) for i in range(length) if 0 <= i + by < length]
    return lax.ppermute(x, axis, pairs)


def iota(shape, dim):
    return lax.broadcasted_iota(jnp.int32, shape, dim)


def nt_dot(a, b):
    return lax.dot_general(
        a, b, (((1,), (1,)), ((), ())), precision=PRECISE, preferred_element_type=F32
    )


def pack_kernel(patch_ref, cand_ref, east_ref, south_ref, sems):
    outs = (east_ref, south_ref)
    body_rows = P_SIZE * PATCH
    copies = [
        pltpu.make_async_copy(patch_ref.at[k], outs[k].at[pl.ds(0, body_rows)], sems.at[k])
        for k in range(2)
    ]
    for copy in copies:
        copy.start()
    for k in range(2):
        lists = jnp.concatenate([cand_ref[k].astype(F32), jnp.zeros((14, 128), F32)], axis=0)
        outs[k][body_rows : body_rows + 16, :] = lists.astype(jnp.bfloat16)
    for copy in copies:
        copy.wait()


def frames_kernel(win_ref, out_ref):
    for seam in range(2):

        def one_line(j, carry, seam=seam):
            at = pl.multiple_of(j * 128, 128)
            pixels = win_ref[seam, :, pl.ds(at, 128)].astype(F32)
            base = seam * P_SIZE * LINES + j
            out_ref[pl.ds(base, 8, stride=LINES), :] = pixels[:8]
            out_ref[pl.ds(base + 8 * LINES, 8, stride=LINES), :] = pixels[8:]
            return carry

        lax.fori_loop(0, LINES, one_line, 0, unroll=8)


def springs_kernel(edges_ref, stiff_ref, out_ref, ends_scr, stiff_scr):
    ends_scr[...] = jnp.zeros_like(ends_scr)
    stiff_scr[...] = jnp.zeros_like(stiff_scr)
    ends_scr[0:2, 0:E] = edges_ref[...]
    stiff_scr[0:1, 0:E] = stiff_ref[...]
    first, second = ends_scr[0:1], ends_scr[1:2]
    low, high = jnp.minimum(first, second), jnp.maximum(first, second)
    gap = high - low
    kind = jnp.where(gap == 1, 0, jnp.where(gap == GV, 1, jnp.where(gap == GV + 1, 2, 3)))
    left = jnp.where(iota((GV, E_PAD), 0) == (low >> 4), stiff_scr[0:1], 0.0)
    right = (iota((128, E_PAD), 0) == kind * GV + (low & (GV - 1))).astype(F32)
    out_ref[...] = nt_dot(left, right)


def match_kernel(seam, live_ref, sent_ref, frame_ref, *rest):
    if seam == 0:
        springs_ref, other_ref, out_ref, a_scr, t_scr, s_scr, list_scr, cand_s, sem = rest
    else:
        out_ref, a_scr, t_scr, s_scr, list_scr, cand_s, sem = rest
    lists = sent_ref[P_SIZE * PATCH : P_SIZE * PATCH + 16, :].astype(F32)
    list_scr[...] = lists[0:8].astype(jnp.int32)
    copy = pltpu.make_async_copy(list_scr, cand_s, sem)
    copy.start()
    copy.wait()
    tile_row, tile_col = lax.axis_index("row"), lax.axis_index("col")
    near_row, near_col = (tile_row, tile_col - 1) if seam == 0 else (tile_row - 1, tile_col)
    counts = live_ref[jnp.maximum(near_row, 0), seam : seam + 1, :]
    wanted = (iota((1, 16), 1) == near_col) & (near_row >= 0)
    count = jnp.sum(jnp.where(wanted, counts.astype(F32), 0.0), axis=1, keepdims=True)
    count = count.astype(jnp.int32)
    lane = iota((8, 128), 1)
    row = iota((8, 128), 0)

    def one_patch(p, carry):
        pixels = sent_ref[pl.ds(pl.multiple_of(p * PATCH, PATCH), PATCH), :].astype(F32)
        a_scr[...] = pixels
        a_sum = pixels[0:8]
        a_sq = pixels[0:8] * pixels[0:8]
        for t in range(1, 16):
            part = pixels[8 * t : 8 * t + 8]
            a_sum = a_sum + part
            a_sq = a_sq + part * part
        base = (seam * P_SIZE + p) * LINES
        for s in range(NS):
            move_y = cand_s[0, p * NS + s] + REACH
            move_x = cand_s[1, p * NS + s] + REACH
            odd = move_y & 1
            even_at = base + 3 * ((move_y + odd) >> 1)
            odd_at = base + 3 * ((move_y - odd) >> 1)
            even_late = lane < move_x
            odd_late = lane < move_x + 64
            odd_roll = (move_x + 64) & 127
            cross = jnp.zeros((8, 128), F32)
            total = jnp.zeros((8, 128), F32)
            square = jnp.zeros((8, 128), F32)
            for t in range(8):
                even_b = jnp.where(
                    even_late,
                    frame_ref[pl.ds(even_at + 24 * t + 1, 8, stride=3), :],
                    frame_ref[pl.ds(even_at + 24 * t, 8, stride=3), :],
                )
                odd_b = jnp.where(
                    odd_late,
                    frame_ref[pl.ds(odd_at + 24 * t + 2, 8, stride=3), :],
                    frame_ref[pl.ds(odd_at + 24 * t + 1, 8, stride=3), :],
                )
                even_a = pltpu.roll(a_scr[pl.ds(odd + 16 * t, 8, stride=2), :], move_x, 1)
                odd_a = pltpu.roll(a_scr[pl.ds(1 - odd + 16 * t, 8, stride=2), :], odd_roll, 1)
                cross = cross + even_a * even_b + odd_a * odd_b
                total = total + (even_b + odd_b)
                square = square + even_b * even_b + odd_b * odd_b
            t_scr[8 * s : 8 * s + 8, :] = cross
            t_scr[64 + 8 * s : 72 + 8 * s, :] = total
            t_scr[128 + 8 * s : 136 + 8 * s, :] = square
        spot = pl.multiple_of(p * 8, 8)
        for q in range(3):
            part = t_scr[pl.ds(64 * q, 8, stride=8), :]
            for k in range(1, 8):
                part = part + t_scr[pl.ds(64 * q + k, 8, stride=8), :]
            s_scr[pl.ds(q * 128 + spot, 8), :] = part
        for q, part in ((3, a_sum), (4, a_sq)):
            s_scr[pl.ds(q * 128 + spot, 8), :] = jnp.broadcast_to(
                jnp.sum(part, axis=0, keepdims=True), (8, 128)
            )
        return carry

    lax.fori_loop(0, P_SIZE, one_patch, 0)
    ones = jnp.ones((8, 128), F32)
    cross, total, square, a_sum, a_sq = (
        nt_dot(ones, s_scr[128 * q : 128 * q + 128, :]) / PIXELS for q in range(5)
    )
    cov = cross - a_sum * total
    var_a = a_sq - a_sum * a_sum
    var_b = square - total * total
    ncc = cov / jnp.sqrt((var_a + EPSILON) * (var_b + EPSILON))
    weight = jnp.where((lane >> 3) < count, (1.5 + ncc) * (1.5 + ncc), 0.0)
    parts = jnp.where(
        row == 0,
        weight,
        jnp.where(row == 1, weight * lists[0:1], jnp.where(row == 2, weight * lists[1:2], 0.0)),
    )
    group = ((iota((128, 128), 0) >> 3) == iota((128, 128), 1)).astype(F32)
    sums = jnp.dot(parts, group, precision=PRECISE, preferred_element_type=F32)

    def estimates(w_sum, w_y, w_x, slot):
        alive = slot < count
        conf = jnp.where(alive, w_sum / NS, 0.0)
        along_y = jnp.where(alive, w_y / (REACH * w_sum), 0.0)
        along_x = jnp.where(alive, w_x / (REACH * w_sum), 0.0)
        return conf, along_y, along_x

    conf, along_y, along_x = estimates(sums[0:1], sums[1:2], sums[2:3], lane[0:1])
    if seam == 1:
        lines = (conf, conf * along_y, conf * along_x, along_y, along_x)
        for k, line in enumerate(lines):
            out_ref[k : k + 1, :] = line
        out_ref[5:8, :] = jnp.zeros((3, 128), F32)
    else:
        gather = ((iota((16, 128), 1) >> 3) == iota((16, 128), 0)).astype(F32)
        cols = nt_dot(gather, parts)
        conf_c, y_c, x_c = estimates(cols[:, 0:1], cols[:, 1:2], cols[:, 2:3], iota((16, 1), 0))
        lane16 = iota((16, 128), 1)
        block = springs_ref[...]
        for k, col in enumerate((conf_c, conf_c * y_c, conf_c * x_c)):
            block = jnp.where(lane16 == 64 + k, col, block)
        out_ref[0:16, :] = block
        out_ref[16:24, :] = other_ref[...]
        for k, line in enumerate((along_y, along_x, conf)):
            out_ref[21 + k : 22 + k, :] = line


def krylov_kernel(west_ref, centre_ref, east_ref, u_ref, mom_ref, match_ref):
    lane = iota((48, 128), 1)
    row = iota((48, 128), 0)
    refs = (west_ref, centre_ref, east_ref)
    blocks = [jnp.concatenate([ref[a, 0:16, :] for a in range(3)], axis=0) for ref in refs]

    def both(x):
        return x + pltpu.roll(x, 64, 1)

    def plane(t):
        out = jnp.zeros((48, 128), F32)
        for b in range(3):
            moved = pltpu.roll(blocks[b], (16 * b - 16 * t) % 128, 1)
            out = jnp.where((lane >> 4) == b, moved, out)
        return both(out)

    def west_seam(lane_y, lane_x):
        out = jnp.zeros((48, 128), F32)
        for b in (1, 2):
            out = jnp.where(lane == 16 * b - 1, blocks[b][:, lane_y : lane_y + 1], out)
            out = jnp.where(lane == 16 * b + 63, blocks[b][:, lane_x : lane_x + 1], out)
        return out

    def north_lines(a, r):
        lines = [ref[a, r : r + 1, :] for ref in refs]
        return lines[0] + pltpu.roll(lines[1], 16, 1) + pltpu.roll(lines[2], 32, 1)

    def north_seam(r_y, r_x):
        out = jnp.zeros((48, 128), F32)
        for a in (1, 2):
            line = north_lines(a, r_y) + pltpu.roll(north_lines(a, r_x), 64, 1)
            out = jnp.where(row == 16 * a - 1, line, out)
        return out

    q_h = plane(0) + west_seam(64, 64)
    q_v = plane(1) + north_seam(16, 16)
    q_d = plane(2)
    q_a = plane(3)
    f_h = west_seam(65, 66)
    f_v = north_seam(17, 18)

    def right(x):
        return pltpu.roll(x, 1, 1)

    def left(x):
        return pltpu.roll(x, 127, 1)

    def down(x):
        return pltpu.roll(x, 1, 0)

    def up(x):
        return pltpu.roll(x, 47, 0)

    def operate(v):
        below = up(v)
        h = q_h * (v - left(v))
        s = q_v * (v - below)
        d = q_d * (v - left(below))
        a = q_a * (v - right(below))
        out = (LAMBDA_REG - THETA) * v + (h + s) + (d + a)
        return out - right(h + down(d)) - down(s + left(a))

    u0 = f_h + f_v - right(f_h) - down(f_v)
    u1 = operate(u0)
    u2 = operate(u1)
    u3 = operate(u2)
    own = slice(16, 32)
    lane16 = lane[own]
    inside = ((lane16 >= 16) & (lane16 < 32)) | ((lane16 >= 80) & (lane16 < 96))
    parts = [jnp.where(inside, x[own], 0.0) for x in (u0, u1, u2, u3)]
    lane1 = iota((1, 128), 1)
    moments = jnp.zeros((1, 128), F32)
    for k in range(6):
        product = parts[k // 2] * parts[k // 2 + k % 2]
        value = jnp.sum(jnp.sum(product, axis=0, keepdims=True), axis=1, keepdims=True)
        moments = jnp.where(lane1 == k, value, moments)
    for k in range(3):
        u_ref[k] = parts[k]
    mom_ref[...] = jnp.broadcast_to(moments[None], mom_ref.shape)
    for k, (east_row, south_row) in enumerate(((21, 19), (22, 20), (23, 16))):
        match_ref[k, 0:1, :] = east_ref[1, east_row : east_row + 1, 0:16]
        match_ref[k, 1:2, :] = centre_ref[2, south_row : south_row + 1, 0:16]


def flatten_kernel(u_ref, out_ref):
    vertex = iota((128, 256), 1)
    source = iota((128, 256), 0)
    fields = jnp.concatenate([u_ref[k] for k in range(3)], axis=0)
    keep = iota((16, 256), 0) == (iota((16, 256), 1) >> 4)
    for comp in range(2):
        spread = (source == (vertex & 15) + (16 + 64 * comp)).astype(F32)
        wide = jnp.dot(fields, spread, precision=PRECISE, preferred_element_type=F32)
        for k in range(3):
            line = jnp.where(keep, wide[16 * k : 16 * k + 16], 0.0)
            out_ref[k, comp : comp + 1, :] = jnp.sum(line, axis=0, keepdims=True)


def combine_kernel(mom_ref, u_ref, out_ref):
    total = jnp.sum(mom_ref[...], axis=0, keepdims=True)
    m = [total[:, k : k + 1] for k in range(6)]

    def gram(p, lift):
        out = None
        for i in range(3):
            for j in range(i, 3):
                if p[i] is None or p[j] is None:
                    continue
                term = m[i + j]
                if lift:
                    term = m[i + j + 1] + THETA * term
                term = (term * p[i]) * p[j]
                if j > i:
                    term = term + term
                out = term if out is None else out + term
        return out

    one = jnp.ones((1, 1), F32)
    r = [one, None, None]
    d = r
    rr = m[0]
    x = [None, None, None]

    def plus(a, b):
        return b if a is None else a if b is None else a + b

    def times(s, a):
        return None if a is None else s * a

    for step in range(3):
        alpha = rr / gram(d, True)
        x = [plus(x[i], times(alpha, d[i])) for i in range(3)]
        if step == 2:
            break
        image = [times(THETA, d[0]), plus(d[0], times(THETA, d[1])), plus(d[1], times(THETA, d[2]))]
        r = [plus(r[i], times(-alpha, image[i])) for i in range(3)]
        new = gram(r, False)
        d = [plus(r[i], times(new / rr, d[i])) for i in range(3)]
        rr = new
    out_ref[...] = x[0] * u_ref[0] + x[1] * u_ref[1] + x[2] * u_ref[2]


def limit(mib):
    return pltpu.CompilerParams(vmem_limit_bytes=mib * 1024 * 1024)


def shape(dims, dtype=F32):
    return jax.ShapeDtypeStruct(dims, dtype)


def with_sides(x, axis):
    return shifted(x, axis, 1), shifted(x, axis, -1)


def call_frames(windows):
    return pl.pallas_call(
        frames_kernel,
        out_shape=shape((2 * P_SIZE * LINES, 128)),
        in_specs=[VMEM],
        out_specs=VMEM,
        compiler_params=limit(10),
    )(windows)


def call_match(seam, *operands):
    return pl.pallas_call(
        functools.partial(match_kernel, seam),
        out_shape=shape((24 if seam == 0 else 8, 128)),
        in_specs=[VMEM] * len(operands),
        out_specs=VMEM,
        scratch_shapes=[
            pltpu.VMEM((128, 128), F32),
            pltpu.VMEM((192, 128), F32),
            pltpu.VMEM((640, 128), F32),
            pltpu.VMEM((8, 128), jnp.int32),
            pltpu.SMEM((8, 128), jnp.int32),
            pltpu.SemaphoreType.DMA,
        ],
        compiler_params=limit(10),
    )(*operands)


def body(patches, windows, candidates, live, edges, stiffness):
    to_east, to_south = pl.pallas_call(
        pack_kernel,
        out_shape=(shape((P_SIZE * PATCH + 16, 128), jnp.bfloat16),) * 2,
        in_specs=[pl.BlockSpec(memory_space=pl.ANY), VMEM],
        out_specs=(VMEM, VMEM),
        scratch_shapes=[pltpu.SemaphoreType.DMA((2,))],
        compiler_params=limit(4),
    )(patches.reshape(2, P_SIZE * PATCH, PATCH), candidates[0, 0])
    sent_west = shifted(to_east, "col", 1)
    sent_north = shifted(to_south, "row", 1)
    live = live.transpose(0, 2, 1)

    frames = call_frames(windows[0, 0])
    springs = pl.pallas_call(
        springs_kernel,
        out_shape=shape((GV, 128)),
        in_specs=[VMEM, VMEM],
        out_specs=VMEM,
        scratch_shapes=[pltpu.VMEM((8, E_PAD), jnp.int32), pltpu.VMEM((8, E_PAD), F32)],
        compiler_params=limit(4),
    )(edges[0], stiffness)
    seam_north = call_match(1, live, sent_north, frames)
    own = call_match(0, live, sent_west, frames, springs, seam_north)
    north, south = with_sides(own, "row")
    centre = jnp.stack([north, own, south])
    west, east = with_sides(centre, "col")
    devices = lax.axis_size("row") * lax.axis_size("col")
    basis, moments, matches = pl.pallas_call(
        krylov_kernel,
        out_shape=(shape((3, 16, 128)), shape((devices, 1, 128)), shape((3, 2, P_SIZE))),
        in_specs=[VMEM] * 3,
        out_specs=(VMEM, VMEM, VMEM),
        compiler_params=limit(4),
    )(west, centre, east)
    moments = lax.all_to_all(moments, ("row", "col"), 0, 0).reshape(devices, 128)
    flat = pl.pallas_call(
        flatten_kernel,
        out_shape=shape((3, 2, GV * GV)),
        in_specs=[VMEM],
        out_specs=VMEM,
        compiler_params=limit(4),
    )(basis)
    mesh_shift = pl.pallas_call(
        combine_kernel,
        out_shape=shape((2, GV * GV)),
        in_specs=[VMEM, VMEM],
        out_specs=VMEM,
        compiler_params=limit(4),
    )(moments, flat)
    return matches.transpose(1, 0, 2)[None, None], mesh_shift[None, None]


def solution(mesh):
    return jax.shard_map(
        body,
        mesh=mesh,
        in_specs=(
            P("row", "col", None, None, None, None),
            P("row", "col", None, None, None),
            P("row", "col", None, None, None),
            P(),
            P("row", None, "col"),
            P("row", "col"),
        ),
        out_specs=(P("row", "col", None, None, None), P("row", "col", None, None)),
        check_vma=False,
    )
```

time: 99.9 us -> 79.1 us (0.79)
  starting transfers between devices: 60.4 us -> 40.2 us
  Pallas kernels: 15.2 us -> 19.4 us
  local copies, waits for them, and re-layouts: 7.51 us -> 3.59 us
  between operations: 2.24 us -> 0.8 us
  waiting for transfers between devices: 13.7 us -> 14.7 us
    ppermute x12 -> x6, starting transfers between devices: 35.5 us -> 18.9 us  [shifted(): return lax.ppermute(x, axis, pairs)]
    pallas_call x4 -> x6, Pallas kernels: 9.87 us -> 16.4 us  [the longest x2 11.4 us: call_match(): pl.pallas_call(functools.partial(match_kernel, seam), out_shape=shape((24...]
    all_to_all x1, starting transfers between devices: 24.9 us -> 21.2 us  [body(): lax.all_to_all(moments, ('row', 'col'), 0, 0).reshape(devices, 128)]
    squeeze x2 -> x0, local copies, waits for them, and re-layouts: 2 us -> none  [the longest x1 1.3 us: body(): north_patches = shifted(patches[0, 0, 1], 'row', 1)]
    pallas_call x1, Pallas kernels: 2.86 us -> 1.53 us  [body(): pl.pallas_call(combine_kernel, out_shape=shape((2, GV * GV)), in_specs=[V...]
    dynamic_slice x1 -> x0, local copies, waits for them, and re-layouts: 1.29 us -> none  [body(): live[tile_row, jnp.maximum(tile_col - 1, 0), 0]]
    pallas_call x1 -> x0, local copies, waits for them, and re-layouts: 1.25 us -> none  [body(): pl.pallas_call(krylov_kernel, out_shape=(shape((3, 16, 128)), shape((devi...]
    pallas_call x1, Pallas kernels: 2.5 us -> 1.46 us  [body(): pl.pallas_call(krylov_kernel, out_shape=(shape((3, 16, 128)), shape((devi...]
  transfers between devices with their start and end apart: 13 -> 7, of which waited for: 3 -> 3; matrix products, arithmetic and copies ran while one was open for 3% -> 0% of each run, Pallas kernels for 10% -> 13%
where the time goes in v2:
time: 79.1 us; the launch traced here: 78.7 us
  starting transfers between devices  40.2 us (51%)
  Pallas kernels  19.4 us (25%)
  waiting for transfers between devices  14.7 us (19%)
  local copies, waits for them, and re-layouts  3.59 us (5%)
  between operations  0.8 us (1%)
    all_to_all x1, starting transfers between devices, body(): lax.all_to_all(moments, ('row', 'col'), 0, 0).reshape(devices, 128)  21.2 us
    ppermute x6, starting transfers between devices, shifted(): return lax.ppermute(x, axis, pairs)  18.9 us
    all_to_all x1, waiting for transfers between devices, body(): lax.all_to_all(moments, ('row', 'col'), 0, 0).reshape(devices, 128)  12.8 us
    pallas_call x2, Pallas kernels, call_match(): pl.pallas_call(functools.partial(match_kernel, seam), out_shape=shape((24...  11.4 us
    pallas_call x1, Pallas kernels, call_frames(): pl.pallas_call(frames_kernel, out_shape=shape((2 * P_SIZE * LINES, 128)),...  4.26 us
    unnamed x12, local copies, waits for them, and re-layouts  3.59 us
    ppermute x6, waiting for transfers between devices, shifted(): return lax.ppermute(x, axis, pairs)  1.84 us
  transfers between devices with their start and end apart: 7, of which 3 were waited for; matrix products, arithmetic and copies ran while one was open for 0% of the time, Pallas kernels for 13%

profile of v2, /device:TPU:1, one launch (start us, length us, event | category | flops | bytes accessed | tf_op | source)
XLA Modules:
  0.0 78.7 jit_solution(14073223049005213216)
XLA Ops:
  0.6 0.0 copy-start.4
  0.6 0.0 copy-start.1
  0.7 1.2 %copy-done.1 = bf16[1,1,2,16,128,128]{5,4,3,2,1,0:T(8,128)(2,1)S(1)} copy-done((bf16[1,1,2,16,128,128]{5,4,3,2,1,0:T(8,128)(2,1)S(1)}, bf16[1,1,2,16,128,128]{5,4,3,2,1,0:T(8,128)(2,1)}, u32[]{:S(2)}) %copy-start.1) | copy-done | bytes 1048600
  1.9 0.0 copy-start.5
  1.9 0.7 copy-done.5
  2.6 0.1 shard_map.77
  2.7 4.9 %collective-permute-start.1 = (bf16[2064,128]{1,0:T(8,128)(2,1)S(1)}, bf16[2064,128]{1,0:T(8,128)(2,1)S(1)}, u32[]{:S(2)}, u32[]{:S(2)}) collective-permute-start(bf16[2064,128]{1,0:T(8,128)(2,1)S(1)} %get-tuple-element.8), channel_id=1, source_target_pairs={{0,16},{16,32},{32,48},{48,64},{64,80},{80,96},{96,112},{112,128},... | collective-permute-start | bytes 1585160 | tf_op jit(solution)/shard_map/ppermute | solution.py:32
  7.6 3.1 %collective-permute-start = (bf16[2064,128]{1,0:T(8,128)(2,1)S(1)}, bf16[2064,128]{1,0:T(8,128)(2,1)S(1)}, u32[]{:S(2)}, u32[]{:S(2)}) collective-permute-start(bf16[2064,128]{1,0:T(8,128)(2,1)S(1)} %get-tuple-element.7), channel_id=1, source_target_pairs={{0,1},{1,2},{2,3},{3,4},{4,5},{5,6},{6,7},{7,8},{8,9},{9,10},{10,1... | collective-permute-start | bytes 1585160 | tf_op jit(solution)/shard_map/ppermute | solution.py:32
  10.8 0.0 copy-start
  10.8 1.7 %copy-done = bf16[1,1,2,16,36864]{4,3,2,1,0:T(8,128)(2,1)S(1)} copy-done((bf16[1,1,2,16,36864]{4,3,2,1,0:T(8,128)(2,1)S(1)}, bf16[1,1,2,16,36864]{4,3,2,1,0:T(8,128)(2,1)}, u32[]{:S(2)}) %copy-start) | copy-done | bytes 2359320
  12.4 4.3 %shard_map.78.frame_ref = f32[9216,128]{1,0:T(8,128)S(1)} custom-call(bf16[2,16,36864]{2,1,0:T(8,128)(2,1)S(1)} %bitcast.13), custom_call_target="tpu_custom_call" | custom-call | tf_op jit(solution)/shard_map/pallas_call | solution.py:360
  16.7 0.0 copy-done.4
  16.7 0.0 copy-done.3
  16.7 0.4 shard_map.79.rest_0_
  17.2 0.0 collective-permute-done.1.sent_ref
  17.2 0.0 copy-done.2
  17.2 5.7 %shard_map.80.rest_1_ = f32[8,128]{1,0:T(8,128)S(1)} custom-call(s32[16,2,16]{2,1,0:T(2,128)S(1)} %bitcast.16, bf16[2064,128]{1,0:T(8,128)(2,1)S(1)} %collective-permute-done.1.sent_ref, f32[9216,128]{1,0:T(8,128)S(1)} %shard_map.78.frame_ref), custom_call_target="tpu_custom_call" | custom-call | tf_op jit(solution)/shard_map/pallas_call | solution.py:370
  22.9 0.0 collective-permute-done.sent_ref
  22.9 5.7 %shard_map.81 = f32[24,128]{1,0:T(8,128)S(1)} custom-call(s32[16,2,16]{2,1,0:T(2,128)S(1)} %bitcast.17, bf16[2064,128]{1,0:T(8,128)(2,1)S(1)} %collective-permute-done.sent_ref, f32[9216,128]{1,0:T(8,128)S(1)} %shard_map.78.frame_ref, f32[16,128]{1,0:T(8,128)S(1)} %shard_map.79.rest_0_, f32[8,128]{1,0:T(8,128)S(1)} %shard_map.80.rest_1_), custom_call_target="tpu_custom_call" | custom-call | tf_op jit(solution)/shard_map/pallas_call | solution.py:370
  28.6 1.9 %collective-permute-start.3 = (f32[24,128]{1,0:T(8,128)S(1)}, f32[24,128]{1,0:T(8,128)S(1)}, u32[]{:S(2)}, u32[]{:S(2)}) collective-permute-start(f32[24,128]{1,0:T(8,128)S(1)} %shard_map.81), channel_id=1, source_target_pairs={{16,0},{32,16},{48,32},{64,48},{80,64},{96,80},{112,96},{128,112},... | collective-permute-start | bytes 36872 | tf_op jit(solution)/shard_map/ppermute | solution.py:32
  30.5 3.6 %collective-permute-start.2 = (f32[24,128]{1,0:T(8,128)S(1)}, f32[24,128]{1,0:T(8,128)S(1)}, u32[]{:S(2)}, u32[]{:S(2)}) collective-permute-start(f32[24,128]{1,0:T(8,128)S(1)} %shard_map.81), channel_id=1, source_target_pairs={{0,16},{16,32},{32,48},{48,64},{64,80},{80,96},{96,112},{112,128},... | collective-permute-start | bytes 36872 | tf_op jit(solution)/shard_map/ppermute | solution.py:32
  34.2 0.0 collective-permute-done.3
  34.2 0.8 %collective-permute-done.2 = f32[24,128]{1,0:T(8,128)S(1)} collective-permute-done((f32[24,128]{1,0:T(8,128)S(1)}, f32[24,128]{1,0:T(8,128)S(1)}, u32[]{:S(2)}, u32[]{:S(2)}) %collective-permute-start.2) | collective-permute-done | bytes 12320 | tf_op jit(solution)/shard_map/ppermute | solution.py:32
  35.0 1.3 %collective-permute-start.5 = (f32[3,24,128]{2,1,0:T(8,128)S(1)}, f32[3,24,128]{2,1,0:T(8,128)S(1)}, u32[]{:S(2)}, u32[]{:S(2)}) collective-permute-start(f32[3,24,128]{2,1,0:T(8,128)S(1)} %pad_maximum_fusion.centre_ref), channel_id=1, source_target_pairs={{1,0},{2,1},{3,2},{4,3},{5,4},{6,5},{7,6},{8,7},{9,8},{10,9},{11,1... | collective-permute-start | bytes 110600 | tf_op jit(solution)/shard_map/ppermute | solution.py:32
  36.3 4.0 %collective-permute-start.4 = (f32[3,24,128]{2,1,0:T(8,128)S(1)}, f32[3,24,128]{2,1,0:T(8,128)S(1)}, u32[]{:S(2)}, u32[]{:S(2)}) collective-permute-start(f32[3,24,128]{2,1,0:T(8,128)S(1)} %pad_maximum_fusion.centre_ref), channel_id=1, source_target_pairs={{0,1},{1,2},{2,3},{3,4},{4,5},{5,6},{6,7},{7,8},{8,9},{9,10},{10,1... | collective-permute-start | bytes 110600 | tf_op jit(solution)/shard_map/ppermute | solution.py:32
  40.3 0.0 collective-permute-done.5.east_ref
  40.3 1.0 %collective-permute-done.4.west_ref = f32[3,24,128]{2,1,0:T(8,128)S(1)} collective-permute-done((f32[3,24,128]{2,1,0:T(8,128)S(1)}, f32[3,24,128]{2,1,0:T(8,128)S(1)}, u32[]{:S(2)}, u32[]{:S(2)}) %collective-permute-start.4) | collective-permute-done | bytes 36896 | tf_op jit(solution)/shard_map/ppermute | solution.py:32
  41.3 1.5 %shard_map.82 = (f32[3,16,128]{2,1,0:T(8,128)S(1)}, f32[256,1,128]{2,1,0:T(1,128)}, f32[3,2,16]{2,1,0:T(2,128)}) custom-call(f32[3,24,128]{2,1,0:T(8,128)S(1)} %collective-permute-done.4.west_ref, f32[3,24,128]{2,1,0:T(8,128)S(1)} %pad_maximum_fusion.centre_ref, f32[3,24,128]{2,1,0:T(8,128)S(1)} %collective-permute-done.5.east_ref), custom_call_target="tpu_custom_call" | custom-call | tf_op jit(solution)/shard_map/pallas_call | solution.py:415
  42.8 21.2 %all-to-all-start = ((f32[256,1,128]{2,1,0:T(1,128)}), f32[256,1,128]{2,1,0:T(1,128)S(1)}, u32[]{:S(2)}, u32[]{:S(2)}) async-start(f32[256,1,128]{2,1,0:T(1,128)} %get-tuple-element.10), calls=%async_computation | async-start | bytes 262144 | tf_op jit(solution)/shard_map/all_to_all | solution.py:422
  64.1 0.2 shard_map.83.u_ref
  64.3 12.8 %all-to-all-done = f32[256,1,128]{2,1,0:T(1,128)S(1)} async-done(((f32[256,1,128]{2,1,0:T(1,128)}), f32[256,1,128]{2,1,0:T(1,128)S(1)}, u32[]{:S(2)}, u32[]{:S(2)}) %all-to-all-start) | async-done | bytes 131104 | tf_op jit(solution)/shard_map/all_to_all | solution.py:422
  77.1 1.5 %shard_map.84 = f32[2,256]{1,0:T(2,128)} custom-call(f32[256,128]{1,0:T(8,128)S(1)} %bitcast.15, f32[3,2,256]{2,1,0:T(2,128)S(1)} %shard_map.83.u_ref), custom_call_target="tpu_custom_call" | custom-call | tf_op jit(solution)/shard_map/pallas_call | solution.py:430
  (3 shorter events, 0.0 us)
Async XLA Ops:
  0.6 16.1 %copy-start.4 = (f32[1,705]{1,0:T(1,128)S(1)}, f32[1,705]{1,0:T(1,128)}, u32[]{:S(2)}) copy-start(f32[1,705]{1,0:T(1,128)} %stiff_ref.1) | copy-start | bytes 8464
  0.6 1.2 %copy-start.1 = (bf16[1,1,2,16,128,128]{5,4,3,2,1,0:T(8,128)(2,1)S(1)}, bf16[1,1,2,16,128,128]{5,4,3,2,1,0:T(8,128)(2,1)}, u32[]{:S(2)}) copy-start(bf16[1,1,2,16,128,128]{5,4,3,2,1,0:T(8,128)(2,1)} %param.6) | copy-start | bytes 3145732
  1.9 0.7 copy-start.5
  2.6 14.2 %copy-start.3 = (s32[1,2,705]{2,1,0:T(2,128)S(1)}, s32[1,2,705]{2,1,0:T(2,128)}, u32[]{:S(2)}) copy-start(s32[1,2,705]{2,1,0:T(2,128)} %param.10) | copy-start | bytes 16924
  2.6 14.6 %copy-start.2 = (s32[16,16,2]{1,2,0:T(2,128)S(1)}, s32[16,16,2]{1,2,0:T(2,128)}, u32[]{:S(2)}) copy-start(s32[16,16,2]{1,2,0:T(2,128)} %param.9) | copy-start | bytes 6148
  2.7 14.5 %collective-permute-start.1 = (bf16[2064,128]{1,0:T(8,128)(2,1)S(1)}, bf16[2064,128]{1,0:T(8,128)(2,1)S(1)}, u32[]{:S(2)}, u32[]{:S(2)}) collective-permute-start(bf16[2064,128]{1,0:T(8,128)(2,1)S(1)} %get-tuple-element.8), channel_id=1, source_target_pairs={{0,16},{16,32},{32,48},{48,64},{64,80},{80,96},{96,112},{112,128},... | collective-permute-start | bytes 1585160 | tf_op jit(solution)/shard_map/ppermute | solution.py:32
  7.6 15.3 %collective-permute-start = (bf16[2064,128]{1,0:T(8,128)(2,1)S(1)}, bf16[2064,128]{1,0:T(8,128)(2,1)S(1)}, u32[]{:S(2)}, u32[]{:S(2)}) collective-permute-start(bf16[2064,128]{1,0:T(8,128)(2,1)S(1)} %get-tuple-element.7), channel_id=1, source_target_pairs={{0,1},{1,2},{2,3},{3,4},{4,5},{5,6},{6,7},{7,8},{8,9},{9,10},{10,1... | collective-permute-start | bytes 1585160 | tf_op jit(solution)/shard_map/ppermute | solution.py:32
  10.8 1.7 %copy-start = (bf16[1,1,2,16,36864]{4,3,2,1,0:T(8,128)(2,1)S(1)}, bf16[1,1,2,16,36864]{4,3,2,1,0:T(8,128)(2,1)}, u32[]{:S(2)}) copy-start(bf16[1,1,2,16,36864]{4,3,2,1,0:T(8,128)(2,1)} %param.7) | copy-start | bytes 7077892
  28.6 5.6 %collective-permute-start.3 = (f32[24,128]{1,0:T(8,128)S(1)}, f32[24,128]{1,0:T(8,128)S(1)}, u32[]{:S(2)}, u32[]{:S(2)}) collective-permute-start(f32[24,128]{1,0:T(8,128)S(1)} %shard_map.81), channel_id=1, source_target_pairs={{16,0},{32,16},{48,32},{64,48},{80,64},{96,80},{112,96},{128,112},... | collective-permute-start | bytes 36872 | tf_op jit(solution)/shard_map/ppermute | solution.py:32
  30.5 4.5 %collective-permute-start.2 = (f32[24,128]{1,0:T(8,128)S(1)}, f32[24,128]{1,0:T(8,128)S(1)}, u32[]{:S(2)}, u32[]{:S(2)}) collective-permute-start(f32[24,128]{1,0:T(8,128)S(1)} %shard_map.81), channel_id=1, source_target_pairs={{0,16},{16,32},{32,48},{48,64},{64,80},{80,96},{96,112},{112,128},... | collective-permute-start | bytes 36872 | tf_op jit(solution)/shard_map/ppermute | solution.py:32
  35.0 5.3 %collective-permute-start.5 = (f32[3,24,128]{2,1,0:T(8,128)S(1)}, f32[3,24,128]{2,1,0:T(8,128)S(1)}, u32[]{:S(2)}, u32[]{:S(2)}) collective-permute-start(f32[3,24,128]{2,1,0:T(8,128)S(1)} %pad_maximum_fusion.centre_ref), channel_id=1, source_target_pairs={{1,0},{2,1},{3,2},{4,3},{5,4},{6,5},{7,6},{8,7},{9,8},{10,9},{11,1... | collective-permute-start | bytes 110600 | tf_op jit(solution)/shard_map/ppermute | solution.py:32
  36.3 5.0 %collective-permute-start.4 = (f32[3,24,128]{2,1,0:T(8,128)S(1)}, f32[3,24,128]{2,1,0:T(8,128)S(1)}, u32[]{:S(2)}, u32[]{:S(2)}) collective-permute-start(f32[3,24,128]{2,1,0:T(8,128)S(1)} %pad_maximum_fusion.centre_ref), channel_id=1, source_target_pairs={{0,1},{1,2},{2,3},{3,4},{4,5},{5,6},{6,7},{7,8},{8,9},{9,10},{10,1... | collective-permute-start | bytes 110600 | tf_op jit(solution)/shard_map/ppermute | solution.py:32
  42.8 34.3 %all-to-all-start = ((f32[256,1,128]{2,1,0:T(1,128)}), f32[256,1,128]{2,1,0:T(1,128)S(1)}, u32[]{:S(2)}, u32[]{:S(2)}) async-start(f32[256,1,128]{2,1,0:T(1,128)} %get-tuple-element.10), calls=%async_computation | async-start | bytes 262144 | tf_op jit(solution)/shard_map/all_to_all | solution.py:422

commit v3 on v2

--- a/solution.py
+++ b/solution.py
@@ -12,10 +12,11 @@
 WIN = 192
 NS = 8
 P_SIZE = 16
+P_EARLY = 8
 GV = 16
 E = 705
 E_PAD = 768
-LINES = WIN * WIN // 128
+PITCH = 2 * WIN + 1
 PIXELS = float(PATCH * PATCH)
 LAMBDA_REG = 0.05
 EPSILON = 1e-05
@@ -23,7 +24,7 @@
 PRECISE = lax.Precision.HIGHEST
 F32 = jnp.float32
 VMEM = pl.BlockSpec(memory_space=pltpu.VMEM)
-SMEM = pl.BlockSpec(memory_space=pltpu.SMEM)
+HBM = pl.BlockSpec(memory_space=pltpu.HBM)
 
 
 def shifted(x, axis, by):
@@ -42,34 +43,46 @@
     )
 
 
-def pack_kernel(patch_ref, cand_ref, east_ref, south_ref, sems):
-    outs = (east_ref, south_ref)
-    body_rows = P_SIZE * PATCH
-    copies = [
-        pltpu.make_async_copy(patch_ref.at[k], outs[k].at[pl.ds(0, body_rows)], sems.at[k])
-        for k in range(2)
-    ]
-    for copy in copies:
-        copy.start()
-    for k in range(2):
-        lists = jnp.concatenate([cand_ref[k].astype(F32), jnp.zeros((14, 128), F32)], axis=0)
-        outs[k][body_rows : body_rows + 16, :] = lists.astype(jnp.bfloat16)
+def pack_kernel(patch_ref, cand_ref, first_ref, south_ref, second_ref, sems):
+    moves = ((0, 0, first_ref), (1, 0, south_ref), (0, P_EARLY, second_ref))
+    copies = []
+    for k, (seam, slot, out_ref) in enumerate(moves):
+        rows = out_ref.shape[0] // PATCH * PATCH
+        copies.append(
+            pltpu.make_async_copy(
+                patch_ref.at[seam, pl.ds(slot * PATCH, rows)],
+                out_ref.at[pl.ds(0, rows)],
+                sems.at[k],
+            )
+        )
+        copies[-1].start()
+    for seam, out_ref in ((0, first_ref), (1, south_ref)):
+        rows = out_ref.shape[0] // PATCH * PATCH
+        tile = jnp.concatenate([cand_ref[seam].astype(F32), jnp.zeros((14, 128), F32)], axis=0)
+        out_ref[rows : rows + 16, :] = tile.astype(jnp.bfloat16)
     for copy in copies:
         copy.wait()
 
 
 def frames_kernel(win_ref, out_ref):
+    low = iota((P_SIZE, 128), 1) < 64
     for seam in range(2):
 
-        def one_line(j, carry, seam=seam):
-            at = pl.multiple_of(j * 128, 128)
-            pixels = win_ref[seam, :, pl.ds(at, 128)].astype(F32)
-            base = seam * P_SIZE * LINES + j
-            out_ref[pl.ds(base, 8, stride=LINES), :] = pixels[:8]
-            out_ref[pl.ds(base + 8 * LINES, 8, stride=LINES), :] = pixels[8:]
+        def one_pair(m, carry, seam=seam):
+            line = [
+                win_ref[seam, :, pl.ds(pl.multiple_of(m * 384 + c * 128, 128), 128)].astype(F32)
+                for c in range(3)
+            ]
+            last = pltpu.roll(line[2], 64, 1)
+            middle = jnp.where(low, pltpu.roll(line[1], 64, 1), last)
+            spot = seam * P_SIZE * PITCH + 2 * m
+            for shift, value in ((0, line[0]), (1, middle), (WIN, line[1]), (WIN + 1, last)):
+                for half in range(2):
+                    at = spot + half * 8 * PITCH + shift
+                    out_ref[pl.ds(at, 8, stride=PITCH), :] = value[8 * half : 8 * half + 8]
             return carry
 
-        lax.fori_loop(0, LINES, one_line, 0, unroll=8)
+        lax.fori_loop(0, WIN // 2, one_pair, 0, unroll=32)
 
 
 def springs_kernel(edges_ref, stiff_ref, out_ref, ends_scr, stiff_scr):
@@ -86,16 +99,88 @@
     out_ref[...] = nt_dot(left, right)
 
 
-def match_kernel(seam, live_ref, sent_ref, frame_ref, *rest):
-    if seam == 0:
-        springs_ref, other_ref, out_ref, a_scr, t_scr, s_scr, list_scr, cand_s, sem = rest
-    else:
-        out_ref, a_scr, t_scr, s_scr, list_scr, cand_s, sem = rest
-    lists = sent_ref[P_SIZE * PATCH : P_SIZE * PATCH + 16, :].astype(F32)
+def split3(x):
+    first = x.astype(jnp.bfloat16)
+    rest = x - first.astype(F32)
+    second = rest.astype(jnp.bfloat16)
+    third = (rest - second.astype(F32)).astype(jnp.bfloat16)
+    return first, second, third
+
+
+def fold(x):
+    pieces = [x[8 * t : 8 * t + 8] for t in range(x.shape[0] // 8)]
+    while len(pieces) > 1:
+        pieces = [a + b for a, b in zip(pieces[::2], pieces[1::2])]
+    return pieces[0]
+
+
+def score(seam, first, slots, tail_ref, sent_ref, frame_ref, s_ref, at, scratch):
+    a_scr, t_scr, list_scr, cand_s, sem = scratch
+    rows = s_ref.shape[0] // 5
+    tail = tail_ref.shape[0] // PATCH * PATCH
+    lists = tail_ref[tail : tail + 16, :].astype(F32)
     list_scr[...] = lists[0:8].astype(jnp.int32)
     copy = pltpu.make_async_copy(list_scr, cand_s, sem)
     copy.start()
+    full_lane = iota((PATCH, 128), 1)
+
+    def one_sum(p, carry):
+        pixels = sent_ref[pl.ds(pl.multiple_of(p * PATCH, PATCH), PATCH), :].astype(F32)
+        spot = pl.multiple_of(at + p * 8, 8)
+        for q, part in ((3, fold(pixels)), (4, fold(pixels * pixels))):
+            s_ref[pl.ds(q * rows + spot, 8), :] = jnp.broadcast_to(
+                jnp.sum(part, axis=0, keepdims=True), (8, 128)
+            )
+        return carry
+
+    lax.fori_loop(0, slots, one_sum, 0, unroll=2)
     copy.wait()
+
+    def one_patch(p, carry):
+        pixels = sent_ref[pl.ds(pl.multiple_of(p * PATCH, PATCH), PATCH), :]
+        a_scr[...] = pixels.astype(F32)
+        base = (seam * P_SIZE + first + p) * PITCH
+        for s in range(NS):
+            top = base + (cand_s[0, (first + p) * NS + s] + REACH)
+            move_x = cand_s[1, (first + p) * NS + s] + REACH
+            crop = jnp.where(
+                full_lane < move_x,
+                frame_ref[pl.ds(top + WIN, PATCH), :],
+                frame_ref[pl.ds(top, PATCH), :],
+            )
+            cross = fold(pltpu.roll(a_scr[...], move_x, 1) * crop)
+            total = fold(crop)
+            square = fold(crop * crop)
+            for q, part in enumerate((cross, total, square)):
+                t_scr[72 * q + 9 * s : 72 * q + 9 * s + 8, :] = part
+        spot = pl.multiple_of(at + p * 8, 8)
+        for q in range(3):
+            part = t_scr[pl.ds(72 * q, 8, stride=9), :]
+            for k in range(1, 8):
+                part = part + t_scr[pl.ds(72 * q + k, 8, stride=9), :]
+            s_ref[pl.ds(q * rows + spot, 8), :] = part
+        return carry
+
+    lax.fori_loop(0, slots, one_patch, 0, unroll=2)
+    return lists
+
+
+def early_kernel(tail_ref, frame_ref, s_ref, *scratch):
+    score(0, 0, P_EARLY, tail_ref, tail_ref, frame_ref, s_ref, 0, scratch)
+
+
+def match_kernel(seam, live_ref, tail_ref, frame_ref, *rest):
+    if seam == 0:
+        sent_ref, early_ref, springs_ref, other_ref, out_ref, s_scr = rest[:6]
+        done = P_EARLY * NS
+        for q in range(5):
+            s_scr[128 * q : 128 * q + done, :] = early_ref[done * q : done * q + done, :]
+        lists = score(
+            0, P_EARLY, P_SIZE - P_EARLY, tail_ref, sent_ref, frame_ref, s_scr, done, rest[6:]
+        )
+    else:
+        out_ref, s_scr = rest[:2]
+        lists = score(1, 0, P_SIZE, tail_ref, tail_ref, frame_ref, s_scr, 0, rest[2:])
     tile_row, tile_col = lax.axis_index("row"), lax.axis_index("col")
     near_row, near_col = (tile_row, tile_col - 1) if seam == 0 else (tile_row - 1, tile_col)
     counts = live_ref[jnp.maximum(near_row, 0), seam : seam + 1, :]
@@ -104,77 +189,23 @@
     count = count.astype(jnp.int32)
     lane = iota((8, 128), 1)
     row = iota((8, 128), 0)
-
-    def one_patch(p, carry):
-        pixels = sent_ref[pl.ds(pl.multiple_of(p * PATCH, PATCH), PATCH), :].astype(F32)
-        a_scr[...] = pixels
-        a_sum = pixels[0:8]
-        a_sq = pixels[0:8] * pixels[0:8]
-        for t in range(1, 16):
-            part = pixels[8 * t : 8 * t + 8]
-            a_sum = a_sum + part
-            a_sq = a_sq + part * part
-        base = (seam * P_SIZE + p) * LINES
-        for s in range(NS):
-            move_y = cand_s[0, p * NS + s] + REACH
-            move_x = cand_s[1, p * NS + s] + REACH
-            odd = move_y & 1
-            even_at = base + 3 * ((move_y + odd) >> 1)
-            odd_at = base + 3 * ((move_y - odd) >> 1)
-            even_late = lane < move_x
-            odd_late = lane < move_x + 64
-            odd_roll = (move_x + 64) & 127
-            cross = jnp.zeros((8, 128), F32)
-            total = jnp.zeros((8, 128), F32)
-            square = jnp.zeros((8, 128), F32)
-            for t in range(8):
-                even_b = jnp.where(
-                    even_late,
-                    frame_ref[pl.ds(even_at + 24 * t + 1, 8, stride=3), :],
-                    frame_ref[pl.ds(even_at + 24 * t, 8, stride=3), :],
-                )
-                odd_b = jnp.where(
-                    odd_late,
-                    frame_ref[pl.ds(odd_at + 24 * t + 2, 8, stride=3), :],
-                    frame_ref[pl.ds(odd_at + 24 * t + 1, 8, stride=3), :],
-                )
-                even_a = pltpu.roll(a_scr[pl.ds(odd + 16 * t, 8, stride=2), :], move_x, 1)
-                odd_a = pltpu.roll(a_scr[pl.ds(1 - odd + 16 * t, 8, stride=2), :], odd_roll, 1)
-                cross = cross + even_a * even_b + odd_a * odd_b
-                total = total + (even_b + odd_b)
-                square = square + even_b * even_b + odd_b * odd_b
-            t_scr[8 * s : 8 * s + 8, :] = cross
-            t_scr[64 + 8 * s : 72 + 8 * s, :] = total
-            t_scr[128 + 8 * s : 136 + 8 * s, :] = square
-        spot = pl.multiple_of(p * 8, 8)
-        for q in range(3):
-            part = t_scr[pl.ds(64 * q, 8, stride=8), :]
-            for k in range(1, 8):
-                part = part + t_scr[pl.ds(64 * q + k, 8, stride=8), :]
-            s_scr[pl.ds(q * 128 + spot, 8), :] = part
-        for q, part in ((3, a_sum), (4, a_sq)):
-            s_scr[pl.ds(q * 128 + spot, 8), :] = jnp.broadcast_to(
-                jnp.sum(part, axis=0, keepdims=True), (8, 128)
-            )
-        return carry
-
-    lax.fori_loop(0, P_SIZE, one_patch, 0)
-    ones = jnp.ones((8, 128), F32)
     cross, total, square, a_sum, a_sq = (
-        nt_dot(ones, s_scr[128 * q : 128 * q + 128, :]) / PIXELS for q in range(5)
+        jnp.sum(s_scr[128 * q : 128 * q + 128, :].T, axis=0, keepdims=True) / PIXELS
+        for q in range(5)
     )
     cov = cross - a_sum * total
     var_a = a_sq - a_sum * a_sum
     var_b = square - total * total
     ncc = cov / jnp.sqrt((var_a + EPSILON) * (var_b + EPSILON))
-    weight = jnp.where((lane >> 3) < count, (1.5 + ncc) * (1.5 + ncc), 0.0)
+    weight = jnp.where((lane[0:1] >> 3) < count, (1.5 + ncc) * (1.5 + ncc), 0.0)
     parts = jnp.where(
         row == 0,
         weight,
         jnp.where(row == 1, weight * lists[0:1], jnp.where(row == 2, weight * lists[1:2], 0.0)),
     )
-    group = ((iota((128, 128), 0) >> 3) == iota((128, 128), 1)).astype(F32)
-    sums = jnp.dot(parts, group, precision=PRECISE, preferred_element_type=F32)
+    group = ((iota((128, 128), 0) >> 3) == iota((128, 128), 1)).astype(jnp.bfloat16)
+    sums = [jnp.dot(part, group, preferred_element_type=F32) for part in split3(parts)]
+    sums = sums[0] + sums[1] + sums[2]
 
     def estimates(w_sum, w_y, w_x, slot):
         alive = slot < count
@@ -190,24 +221,26 @@
             out_ref[k : k + 1, :] = line
         out_ref[5:8, :] = jnp.zeros((3, 128), F32)
     else:
-        gather = ((iota((16, 128), 1) >> 3) == iota((16, 128), 0)).astype(F32)
-        cols = nt_dot(gather, parts)
-        conf_c, y_c, x_c = estimates(cols[:, 0:1], cols[:, 1:2], cols[:, 2:3], iota((16, 1), 0))
+        lines = (conf, conf * along_y, conf * along_x)
+        cols = jnp.concatenate(lines + (jnp.zeros((5, 128), F32),), axis=0).T
         lane16 = iota((16, 128), 1)
         block = springs_ref[...]
-        for k, col in enumerate((conf_c, conf_c * y_c, conf_c * x_c)):
-            block = jnp.where(lane16 == 64 + k, col, block)
+        for k in range(3):
+            block = jnp.where(lane16 == 64 + k, cols[0:16, k : k + 1], block)
         out_ref[0:16, :] = block
         out_ref[16:24, :] = other_ref[...]
         for k, line in enumerate((along_y, along_x, conf)):
             out_ref[21 + k : 22 + k, :] = line
 
 
-def krylov_kernel(west_ref, centre_ref, east_ref, u_ref, mom_ref, match_ref):
+def krylov_kernel(inner_ref, centre_ref, outer_ref, u_ref, mom_ref, match_ref):
+    odd = lax.axis_index("col") % 2 == 1
+    west = jnp.where(odd, inner_ref[...], outer_ref[...])
+    east = jnp.where(odd, outer_ref[...], inner_ref[...])
+    tiles = (west, centre_ref[...], east)
     lane = iota((48, 128), 1)
     row = iota((48, 128), 0)
-    refs = (west_ref, centre_ref, east_ref)
-    blocks = [jnp.concatenate([ref[a, 0:16, :] for a in range(3)], axis=0) for ref in refs]
+    blocks = [jnp.concatenate([tile[a, 0:16, :] for a in range(3)], axis=0) for tile in tiles]
 
     def both(x):
         return x + pltpu.roll(x, 64, 1)
@@ -227,7 +260,7 @@
         return out
 
     def north_lines(a, r):
-        lines = [ref[a, r : r + 1, :] for ref in refs]
+        lines = [tile[a, r : r + 1, :] for tile in tiles]
         return lines[0] + pltpu.roll(lines[1], 16, 1) + pltpu.roll(lines[2], 32, 1)
 
     def north_seam(r_y, r_x):
@@ -283,7 +316,7 @@
         u_ref[k] = parts[k]
     mom_ref[...] = jnp.broadcast_to(moments[None], mom_ref.shape)
     for k, (east_row, south_row) in enumerate(((21, 19), (22, 20), (23, 16))):
-        match_ref[k, 0:1, :] = east_ref[1, east_row : east_row + 1, 0:16]
+        match_ref[k, 0:1, :] = east[1, east_row : east_row + 1, 0:16]
         match_ref[k, 1:2, :] = centre_ref[2, south_row : south_row + 1, 0:16]
 
 
@@ -352,18 +385,56 @@
     return jax.ShapeDtypeStruct(dims, dtype)
 
 
-def with_sides(x, axis):
-    return shifted(x, axis, 1), shifted(x, axis, -1)
+def swaps(x, axis):
+    length = lax.axis_size(axis)
+    inner = [(i, i ^ 1) for i in range(length)]
+    outer = [(i, i + 1 if i % 2 else i - 1) for i in range(1, length - 1)]
+    return lax.ppermute(x, axis, inner), lax.ppermute(x, axis, outer)
+
+
+def call_pack(patches, candidates):
+    return pl.pallas_call(
+        pack_kernel,
+        out_shape=tuple(
+            shape((rows, 128), jnp.bfloat16)
+            for rows in (P_EARLY * PATCH + 16, P_SIZE * PATCH + 16, (P_SIZE - P_EARLY) * PATCH)
+        ),
+        in_specs=[HBM, VMEM],
+        out_specs=(VMEM, VMEM, VMEM),
+        scratch_shapes=[pltpu.SemaphoreType.DMA((3,))],
+        compiler_params=limit(4),
+    )(patches, candidates)
 
 
 def call_frames(windows):
     return pl.pallas_call(
         frames_kernel,
-        out_shape=shape((2 * P_SIZE * LINES, 128)),
+        out_shape=shape((2 * P_SIZE * PITCH, 128)),
         in_specs=[VMEM],
         out_specs=VMEM,
-        compiler_params=limit(10),
+        compiler_params=limit(12),
     )(windows)
+
+
+def score_scratch():
+    return [
+        pltpu.VMEM((128, 128), F32),
+        pltpu.VMEM((216, 128), F32),
+        pltpu.VMEM((8, 128), jnp.int32),
+        pltpu.SMEM((8, 128), jnp.int32),
+        pltpu.SemaphoreType.DMA,
+    ]
+
+
+def call_early(*operands):
+    return pl.pallas_call(
+        early_kernel,
+        out_shape=shape((5 * P_EARLY * NS, 128)),
+        in_specs=[VMEM] * len(operands),
+        out_specs=VMEM,
+        scratch_shapes=score_scratch(),
+        compiler_params=limit(12),
+    )(*operands)
 
 
 def call_match(seam, *operands):
@@ -372,29 +443,18 @@
         out_shape=shape((24 if seam == 0 else 8, 128)),
         in_specs=[VMEM] * len(operands),
         out_specs=VMEM,
-        scratch_shapes=[
-            pltpu.VMEM((128, 128), F32),
-            pltpu.VMEM((192, 128), F32),
-            pltpu.VMEM((640, 128), F32),
-            pltpu.VMEM((8, 128), jnp.int32),
-            pltpu.SMEM((8, 128), jnp.int32),
-            pltpu.SemaphoreType.DMA,
-        ],
-        compiler_params=limit(10),
+        scratch_shapes=[pltpu.VMEM((5 * P_SIZE * NS, 128), F32)] + score_scratch(),
+        compiler_params=limit(12),
     )(*operands)
 
 
 def body(patches, windows, candidates, live, edges, stiffness):
-    to_east, to_south = pl.pallas_call(
-        pack_kernel,
-        out_shape=(shape((P_SIZE * PATCH + 16, 128), jnp.bfloat16),) * 2,
-        in_specs=[pl.BlockSpec(memory_space=pl.ANY), VMEM],
-        out_specs=(VMEM, VMEM),
-        scratch_shapes=[pltpu.SemaphoreType.DMA((2,))],
-        compiler_params=limit(4),
-    )(patches.reshape(2, P_SIZE * PATCH, PATCH), candidates[0, 0])
-    sent_west = shifted(to_east, "col", 1)
+    first, to_south, second = call_pack(
+        patches.reshape(2, P_SIZE * PATCH, PATCH), candidates[0, 0]
+    )
+    west_first = shifted(first, "col", 1)
     sent_north = shifted(to_south, "row", 1)
+    west_second = shifted(second, "col", 1)
     live = live.transpose(0, 2, 1)
 
     frames = call_frames(windows[0, 0])
@@ -406,11 +466,13 @@
         scratch_shapes=[pltpu.VMEM((8, E_PAD), jnp.int32), pltpu.VMEM((8, E_PAD), F32)],
         compiler_params=limit(4),
     )(edges[0], stiffness)
+    early = call_early(west_first, frames)
     seam_north = call_match(1, live, sent_north, frames)
-    own = call_match(0, live, sent_west, frames, springs, seam_north)
-    north, south = with_sides(own, "row")
-    centre = jnp.stack([north, own, south])
-    west, east = with_sides(centre, "col")
+    own = call_match(0, live, west_first, frames, west_second, early, springs, seam_north)
+    inner, outer = swaps(own, "row")
+    odd = lax.axis_index("row") % 2 == 1
+    centre = jnp.stack([jnp.where(odd, inner, outer), own, jnp.where(odd, outer, inner)])
+    inner, outer = swaps(centre, "col")
     devices = lax.axis_size("row") * lax.axis_size("col")
     basis, moments, matches = pl.pallas_call(
         krylov_kernel,
@@ -418,7 +480,7 @@
         in_specs=[VMEM] * 3,
         out_specs=(VMEM, VMEM, VMEM),
         compiler_params=limit(4),
-    )(west, centre, east)
+    )(inner, centre, outer)
     moments = lax.all_to_all(moments, ("row", "col"), 0, 0).reshape(devices, 128)
     flat = pl.pallas_call(
         flatten_kernel,

time: 79.1 us -> 70.8 us (0.90)
  Pallas kernels: 19.4 us -> 12.2 us
  starting transfers between devices: 40.2 us -> 37.3 us
  waiting for transfers between devices: 14.7 us -> 16.6 us
    ppermute x0 -> x4, starting transfers between devices: none -> 7.81 us  [swaps(): return (lax.ppermute(x, axis, inner), lax.ppermute(x, axis, outer))]
    ppermute x6 -> x3, starting transfers between devices: 18.9 us -> 11.2 us  [shifted(): return lax.ppermute(x, axis, pairs)]
    pallas_call x2, Pallas kernels: 11.4 us -> 5.51 us  [call_match(): pl.pallas_call(functools.partial(match_kernel, seam), out_shape=shape((24...]
    ppermute x0 -> x4, waiting for transfers between devices: none -> 3.77 us  [swaps(): return (lax.ppermute(x, axis, inner), lax.ppermute(x, axis, outer))]
    all_to_all x1, starting transfers between devices: 21.2 us -> 18.3 us  [body(): lax.all_to_all(moments, ('row', 'col'), 0, 0).reshape(devices, 128)]
    ppermute x6 -> x3, waiting for transfers between devices: 1.84 us -> 0.01 us  [shifted(): return lax.ppermute(x, axis, pairs)]
    pallas_call x2 -> x3, Pallas kernels: 4.35 us -> 3.02 us  [the longest x1 1.78 us: call_early(): pl.pallas_call(early_kernel, out_shape=shape((5 * P_EARLY * NS, 128)), in...]
  transfers between devices with their start and end apart: 7 -> 8, of which waited for: 3 -> 3; matrix products, arithmetic and copies ran while one was open for 0% -> 0% of each run, Pallas kernels for 13% -> 10%
where the time goes in v3:
time: 70.8 us; the launch traced here: 70.4 us
  starting transfers between devices  37.3 us (53%)
  waiting for transfers between devices  16.6 us (23%)
  Pallas kernels  12.2 us (17%)
  local copies, waits for them, and re-layouts  3.58 us (5%)
  between operations  0.82 us (1%)
    all_to_all x1, starting transfers between devices, body(): lax.all_to_all(moments, ('row', 'col'), 0, 0).reshape(devices, 128)  18.3 us
    all_to_all x1, waiting for transfers between devices, body(): lax.all_to_all(moments, ('row', 'col'), 0, 0).reshape(devices, 128)  12.8 us
    ppermute x3, starting transfers between devices, shifted(): return lax.ppermute(x, axis, pairs)  11.2 us
    ppermute x4, starting transfers between devices, swaps(): return (lax.ppermute(x, axis, inner), lax.ppermute(x, axis, outer))  7.81 us
    pallas_call x2, Pallas kernels, call_match(): pl.pallas_call(functools.partial(match_kernel, seam), out_shape=shape((24...  5.51 us
    ppermute x4, waiting for transfers between devices, swaps(): return (lax.ppermute(x, axis, inner), lax.ppermute(x, axis, outer))  3.77 us
    unnamed x12, local copies, waits for them, and re-layouts  3.58 us
    pallas_call x1, Pallas kernels, call_early(): pl.pallas_call(early_kernel, out_shape=shape((5 * P_EARLY * NS, 128)), in...  1.78 us
  transfers between devices with their start and end apart: 8, of which 3 were waited for; matrix products, arithmetic and copies ran while one was open for 0% of the time, Pallas kernels for 10%

profile of v3, /device:TPU:1, one launch (start us, length us, event | category | flops | bytes accessed | tf_op | source)
XLA Modules:
  0.0 70.4 jit_solution(15338692922671497420)
XLA Ops:
  0.6 0.0 copy-start.4
  0.7 1.2 %copy-done.1 = bf16[1,1,2,16,128,128]{5,4,3,2,1,0:T(8,128)(2,1)S(1)} copy-done((bf16[1,1,2,16,128,128]{5,4,3,2,1,0:T(8,128)(2,1)S(1)}, bf16[1,1,2,16,128,128]{5,4,3,2,1,0:T(8,128)(2,1)}, u32[]{:S(2)}) %copy-start.1) | copy-done | bytes 1048600
  1.9 0.7 copy-done.5
  2.6 0.1 shard_map.77
  2.7 4.9 %collective-permute-start.2 = (bf16[2064,128]{1,0:T(8,128)(2,1)S(1)}, bf16[2064,128]{1,0:T(8,128)(2,1)S(1)}, u32[]{:S(2)}, u32[]{:S(2)}) collective-permute-start(bf16[2064,128]{1,0:T(8,128)(2,1)S(1)} %get-tuple-element.10), channel_id=1, source_target_pairs={{0,16},{16,32},{32,48},{48,64},{64,80},{80,96},{96,112},{112,128},... | collective-permute-start | bytes 1585160 | tf_op jit(solution)/shard_map/ppermute | solution.py:33
  7.6 3.1 %collective-permute-start = (bf16[1040,128]{1,0:T(8,128)(2,1)S(1)}, bf16[1040,128]{1,0:T(8,128)(2,1)S(1)}, u32[]{:S(2)}, u32[]{:S(2)}) collective-permute-start(bf16[1040,128]{1,0:T(8,128)(2,1)S(1)} %get-tuple-element.8), channel_id=1, source_target_pairs={{0,1},{1,2},{2,3},{3,4},{4,5},{5,6},{6,7},{7,8},{8,9},{9,10},{10,1... | collective-permute-start | bytes 798728 | tf_op jit(solution)/shard_map/ppermute | solution.py:33
  10.8 3.1 %collective-permute-start.1 = (bf16[1024,128]{1,0:T(8,128)(2,1)S(1)}, bf16[1024,128]{1,0:T(8,128)(2,1)S(1)}, u32[]{:S(2)}, u32[]{:S(2)}) collective-permute-start(bf16[1024,128]{1,0:T(8,128)(2,1)S(1)} %get-tuple-element.9), channel_id=1, source_target_pairs={{0,1},{1,2},{2,3},{3,4},{4,5},{5,6},{6,7},{7,8},{8,9},{9,10},{10,1... | collective-permute-start | bytes 786440 | tf_op jit(solution)/shard_map/ppermute | solution.py:33
  13.9 0.0 copy-start
  13.9 1.7 %copy-done = bf16[1,1,2,16,36864]{4,3,2,1,0:T(8,128)(2,1)S(1)} copy-done((bf16[1,1,2,16,36864]{4,3,2,1,0:T(8,128)(2,1)S(1)}, bf16[1,1,2,16,36864]{4,3,2,1,0:T(8,128)(2,1)}, u32[]{:S(2)}) %copy-start) | copy-done | bytes 2359320
  15.6 1.1 %shard_map.78.frame_ref = f32[12320,128]{1,0:T(8,128)S(1)} custom-call(bf16[2,16,36864]{2,1,0:T(8,128)(2,1)S(1)} %bitcast.15), custom_call_target="tpu_custom_call" | custom-call | tf_op jit(solution)/shard_map/pallas_call | solution.py:410
  16.7 0.0 copy-done.4
  16.7 0.0 copy-done.3
  16.7 0.4 shard_map.80.rest_2_
  17.1 0.0 collective-permute-done.tail_ref
  17.2 1.8 %shard_map.79.rest_1_ = f32[320,128]{1,0:T(8,128)S(1)} custom-call(bf16[1040,128]{1,0:T(8,128)(2,1)S(1)} %collective-permute-done.tail_ref, f32[12320,128]{1,0:T(8,128)S(1)} %shard_map.78.frame_ref), custom_call_target="tpu_custom_call" | custom-call | tf_op jit(solution)/shard_map/pallas_call | solution.py:430
  18.9 0.0 collective-permute-done.2.tail_ref
  19.0 3.3 %shard_map.81.rest_3_ = f32[8,128]{1,0:T(8,128)S(1)} custom-call(s32[16,2,16]{2,1,0:T(2,128)S(1)} %bitcast.18, bf16[2064,128]{1,0:T(8,128)(2,1)S(1)} %collective-permute-done.2.tail_ref, f32[12320,128]{1,0:T(8,128)S(1)} %shard_map.78.frame_ref), custom_call_target="tpu_custom_call" | custom-call | tf_op jit(solution)/shard_map/pallas_call | solution.py:441
  22.2 0.0 collective-permute-done.1.rest_0_
  22.2 2.2 %shard_map.82 = f32[24,128]{1,0:T(8,128)S(1)} custom-call(s32[16,2,16]{2,1,0:T(2,128)S(1)} %bitcast.19, bf16[1040,128]{1,0:T(8,128)(2,1)S(1)} %collective-permute-done.tail_ref, f32[12320,128]{1,0:T(8,128)S(1)} %shard_map.78.frame_ref, bf16[1024,128]{1,0:T(8,128)(2,1)S(1)} %collective-permute-done.1.rest_0_, f32[320,128]{1,0:T(8,128)S(1)} %shard_map.79.rest_1_, ...), custom_call_target="tpu_custom_call" | custom-call | tf_op jit(solution)/shard_map/pallas_call | solution.py:441
  24.5 2.5 %collective-permute-start.4 = (f32[24,128]{1,0:T(8,128)S(1)}, f32[24,128]{1,0:T(8,128)S(1)}, u32[]{:S(2)}, u32[]{:S(2)}) collective-permute-start(f32[24,128]{1,0:T(8,128)S(1)} %shard_map.82), channel_id=1, source_target_pairs={{16,32},{32,16},{48,64},{64,48},{80,96},{96,80},{112,128},{128,112... | collective-permute-start | bytes 36872 | tf_op jit(solution)/shard_map/ppermute | solution.py:392
  27.0 0.1 collective-permute-start.3
  27.1 2.4 %collective-permute-done.4 = f32[24,128]{1,0:T(8,128)S(1)} collective-permute-done((f32[24,128]{1,0:T(8,128)S(1)}, f32[24,128]{1,0:T(8,128)S(1)}, u32[]{:S(2)}, u32[]{:S(2)}) %collective-permute-start.4) | collective-permute-done | bytes 12320 | tf_op jit(solution)/shard_map/ppermute | solution.py:392
  29.5 0.0 collective-permute-done.3
  29.5 0.7 collective-permute-start.6
  30.2 4.6 %collective-permute-start.5 = (f32[3,24,128]{2,1,0:T(8,128)S(1)}, f32[3,24,128]{2,1,0:T(8,128)S(1)}, u32[]{:S(2)}, u32[]{:S(2)}) collective-permute-start(f32[3,24,128]{2,1,0:T(8,128)S(1)} %pad_maximum_fusion.centre_ref), channel_id=1, source_target_pairs={{0,1},{1,0},{2,3},{3,2},{4,5},{5,4},{6,7},{7,6},{8,9},{9,8},{10,11... | collective-permute-start | bytes 110600 | tf_op jit(solution)/shard_map/ppermute | solution.py:392
  34.8 0.0 collective-permute-done.6.outer_ref
  34.8 1.3 %collective-permute-done.5.inner_ref = f32[3,24,128]{2,1,0:T(8,128)S(1)} collective-permute-done((f32[3,24,128]{2,1,0:T(8,128)S(1)}, f32[3,24,128]{2,1,0:T(8,128)S(1)}, u32[]{:S(2)}, u32[]{:S(2)}) %collective-permute-start.5) | collective-permute-done | bytes 36896 | tf_op jit(solution)/shard_map/ppermute | solution.py:392
  36.1 1.4 %shard_map.83 = (f32[3,16,128]{2,1,0:T(8,128)S(1)}, f32[256,1,128]{2,1,0:T(1,128)}, f32[3,2,16]{2,1,0:T(2,128)}) custom-call(f32[3,24,128]{2,1,0:T(8,128)S(1)} %collective-permute-done.5.inner_ref, f32[3,24,128]{2,1,0:T(8,128)S(1)} %pad_maximum_fusion.centre_ref, f32[3,24,128]{2,1,0:T(8,128)S(1)} %collective-permute-done.6.outer_ref), custom_call_target="tpu_custom_call" | custom-call | tf_op jit(solution)/shard_map/pallas_call | solution.py:477
  37.6 18.3 %all-to-all-start = ((f32[256,1,128]{2,1,0:T(1,128)}), f32[256,1,128]{2,1,0:T(1,128)S(1)}, u32[]{:S(2)}, u32[]{:S(2)}) async-start(f32[256,1,128]{2,1,0:T(1,128)} %get-tuple-element.12), calls=%async_computation | async-start | bytes 262144 | tf_op jit(solution)/shard_map/all_to_all | solution.py:484
  55.9 0.2 shard_map.84.u_ref
  56.1 12.8 %all-to-all-done = f32[256,1,128]{2,1,0:T(1,128)S(1)} async-done(((f32[256,1,128]{2,1,0:T(1,128)}), f32[256,1,128]{2,1,0:T(1,128)S(1)}, u32[]{:S(2)}, u32[]{:S(2)}) %all-to-all-start) | async-done | bytes 131104 | tf_op jit(solution)/shard_map/all_to_all | solution.py:484
  68.9 1.5 %shard_map.85 = f32[2,256]{1,0:T(2,128)} custom-call(f32[256,128]{1,0:T(8,128)S(1)} %bitcast.17, f32[3,2,256]{2,1,0:T(2,128)S(1)} %shard_map.84.u_ref), custom_call_target="tpu_custom_call" | custom-call | tf_op jit(solution)/shard_map/pallas_call | solution.py:492
  (7 shorter events, 0.0 us)
Async XLA Ops:
  0.6 16.1 %copy-start.4 = (f32[1,705]{1,0:T(1,128)S(1)}, f32[1,705]{1,0:T(1,128)}, u32[]{:S(2)}) copy-start(f32[1,705]{1,0:T(1,128)} %stiff_ref.1) | copy-start | bytes 8464
  0.6 1.2 %copy-start.1 = (bf16[1,1,2,16,128,128]{5,4,3,2,1,0:T(8,128)(2,1)S(1)}, bf16[1,1,2,16,128,128]{5,4,3,2,1,0:T(8,128)(2,1)}, u32[]{:S(2)}) copy-start(bf16[1,1,2,16,128,128]{5,4,3,2,1,0:T(8,128)(2,1)} %param.6) | copy-start | bytes 3145732
  1.9 0.7 copy-start.5
  2.6 14.1 %copy-start.3 = (s32[1,2,705]{2,1,0:T(2,128)S(1)}, s32[1,2,705]{2,1,0:T(2,128)}, u32[]{:S(2)}) copy-start(s32[1,2,705]{2,1,0:T(2,128)} %param.10) | copy-start | bytes 16924
  2.7 16.3 %collective-permute-start.2 = (bf16[2064,128]{1,0:T(8,128)(2,1)S(1)}, bf16[2064,128]{1,0:T(8,128)(2,1)S(1)}, u32[]{:S(2)}, u32[]{:S(2)}) collective-permute-start(bf16[2064,128]{1,0:T(8,128)(2,1)S(1)} %get-tuple-element.10), channel_id=1, source_target_pairs={{0,16},{16,32},{32,48},{48,64},{64,80},{80,96},{96,112},{112,128},... | collective-permute-start | bytes 1585160 | tf_op jit(solution)/shard_map/ppermute | solution.py:33
  7.6 9.5 %collective-permute-start = (bf16[1040,128]{1,0:T(8,128)(2,1)S(1)}, bf16[1040,128]{1,0:T(8,128)(2,1)S(1)}, u32[]{:S(2)}, u32[]{:S(2)}) collective-permute-start(bf16[1040,128]{1,0:T(8,128)(2,1)S(1)} %get-tuple-element.8), channel_id=1, source_target_pairs={{0,1},{1,2},{2,3},{3,4},{4,5},{5,6},{6,7},{7,8},{8,9},{9,10},{10,1... | collective-permute-start | bytes 798728 | tf_op jit(solution)/shard_map/ppermute | solution.py:33
  10.8 11.5 %collective-permute-start.1 = (bf16[1024,128]{1,0:T(8,128)(2,1)S(1)}, bf16[1024,128]{1,0:T(8,128)(2,1)S(1)}, u32[]{:S(2)}, u32[]{:S(2)}) collective-permute-start(bf16[1024,128]{1,0:T(8,128)(2,1)S(1)} %get-tuple-element.9), channel_id=1, source_target_pairs={{0,1},{1,2},{2,3},{3,4},{4,5},{5,6},{6,7},{7,8},{8,9},{9,10},{10,1... | collective-permute-start | bytes 786440 | tf_op jit(solution)/shard_map/ppermute | solution.py:33
  13.9 1.7 %copy-start = (bf16[1,1,2,16,36864]{4,3,2,1,0:T(8,128)(2,1)S(1)}, bf16[1,1,2,16,36864]{4,3,2,1,0:T(8,128)(2,1)}, u32[]{:S(2)}) copy-start(bf16[1,1,2,16,36864]{4,3,2,1,0:T(8,128)(2,1)} %param.7) | copy-start | bytes 7077892
  15.5 3.4 %copy-start.2 = (s32[16,16,2]{1,2,0:T(2,128)S(1)}, s32[16,16,2]{1,2,0:T(2,128)}, u32[]{:S(2)}) copy-start(s32[16,16,2]{1,2,0:T(2,128)} %param.9) | copy-start | bytes 6148
  24.5 5.0 %collective-permute-start.4 = (f32[24,128]{1,0:T(8,128)S(1)}, f32[24,128]{1,0:T(8,128)S(1)}, u32[]{:S(2)}, u32[]{:S(2)}) collective-permute-start(f32[24,128]{1,0:T(8,128)S(1)} %shard_map.82), channel_id=1, source_target_pairs={{16,32},{32,16},{48,64},{64,48},{80,96},{96,80},{112,128},{128,112... | collective-permute-start | bytes 36872 | tf_op jit(solution)/shard_map/ppermute | solution.py:392
  27.0 2.5 %collective-permute-start.3 = (f32[24,128]{1,0:T(8,128)S(1)}, f32[24,128]{1,0:T(8,128)S(1)}, u32[]{:S(2)}, u32[]{:S(2)}) collective-permute-start(f32[24,128]{1,0:T(8,128)S(1)} %shard_map.82), channel_id=1, source_target_pairs={{0,16},{16,0},{32,48},{48,32},{64,80},{80,64},{96,112},{112,96},{1... | collective-permute-start | bytes 36872 | tf_op jit(solution)/shard_map/ppermute | solution.py:392
  29.5 5.2 %collective-permute-start.6 = (f32[3,24,128]{2,1,0:T(8,128)S(1)}, f32[3,24,128]{2,1,0:T(8,128)S(1)}, u32[]{:S(2)}, u32[]{:S(2)}) collective-permute-start(f32[3,24,128]{2,1,0:T(8,128)S(1)} %pad_maximum_fusion.centre_ref), channel_id=1, source_target_pairs={{1,2},{2,1},{3,4},{4,3},{5,6},{6,5},{7,8},{8,7},{9,10},{10,9},{11,... | collective-permute-start | bytes 110600 | tf_op jit(solution)/shard_map/ppermute | solution.py:392
  30.2 5.9 %collective-permute-start.5 = (f32[3,24,128]{2,1,0:T(8,128)S(1)}, f32[3,24,128]{2,1,0:T(8,128)S(1)}, u32[]{:S(2)}, u32[]{:S(2)}) collective-permute-start(f32[3,24,128]{2,1,0:T(8,128)S(1)} %pad_maximum_fusion.centre_ref), channel_id=1, source_target_pairs={{0,1},{1,0},{2,3},{3,2},{4,5},{5,4},{6,7},{7,6},{8,9},{9,8},{10,11... | collective-permute-start | bytes 110600 | tf_op jit(solution)/shard_map/ppermute | solution.py:392
  37.6 31.3 %all-to-all-start = ((f32[256,1,128]{2,1,0:T(1,128)}), f32[256,1,128]{2,1,0:T(1,128)S(1)}, u32[]{:S(2)}, u32[]{:S(2)}) async-start(f32[256,1,128]{2,1,0:T(1,128)} %get-tuple-element.12), calls=%async_computation | async-start | bytes 262144 | tf_op jit(solution)/shard_map/all_to_all | solution.py:484

commit v4 on v3

--- a/solution.py
+++ b/solution.py
@@ -12,11 +12,12 @@
 WIN = 192
 NS = 8
 P_SIZE = 16
-P_EARLY = 8
 GV = 16
 E = 705
 E_PAD = 768
 PITCH = 2 * WIN + 1
+TOPS = WIN - PATCH + 1
+TAB = 4 * TOPS + 1
 PIXELS = float(PATCH * PATCH)
 LAMBDA_REG = 0.05
 EPSILON = 1e-05
@@ -43,49 +44,82 @@
     )
 
 
-def pack_kernel(patch_ref, cand_ref, first_ref, south_ref, second_ref, sems):
-    moves = ((0, 0, first_ref), (1, 0, south_ref), (0, P_EARLY, second_ref))
-    copies = []
-    for k, (seam, slot, out_ref) in enumerate(moves):
-        rows = out_ref.shape[0] // PATCH * PATCH
-        copies.append(
-            pltpu.make_async_copy(
-                patch_ref.at[seam, pl.ds(slot * PATCH, rows)],
-                out_ref.at[pl.ds(0, rows)],
-                sems.at[k],
-            )
-        )
-        copies[-1].start()
-    for seam, out_ref in ((0, first_ref), (1, south_ref)):
-        rows = out_ref.shape[0] // PATCH * PATCH
-        tile = jnp.concatenate([cand_ref[seam].astype(F32), jnp.zeros((14, 128), F32)], axis=0)
-        out_ref[rows : rows + 16, :] = tile.astype(jnp.bfloat16)
+def pack_kernel(patch_ref, cand_ref, east_ref, south_ref, sems):
+    outs = (east_ref, south_ref)
+    body_rows = P_SIZE * PATCH
+    copies = [
+        pltpu.make_async_copy(patch_ref.at[k], outs[k].at[pl.ds(0, body_rows)], sems.at[k])
+        for k in range(2)
+    ]
+    for copy in copies:
+        copy.start()
+    for k in range(2):
+        tail = outs[k].shape[0] - body_rows
+        tile = jnp.concatenate([cand_ref[k].astype(F32), jnp.zeros((tail - 2, 128), F32)], axis=0)
+        outs[k][body_rows : body_rows + tail, :] = tile.astype(jnp.bfloat16)
     for copy in copies:
         copy.wait()
 
 
-def frames_kernel(win_ref, out_ref):
+def frames_kernel(win_ref, out_ref, tab_ref):
     low = iota((P_SIZE, 128), 1) < 64
+
+    def rows_of(seam, m):
+        line = [
+            win_ref[seam, :, pl.ds(pl.multiple_of(m * 384 + c * 128, 128), 128)].astype(F32)
+            for c in range(3)
+        ]
+        last = pltpu.roll(line[2], 64, 1)
+        middle = jnp.where(low, pltpu.roll(line[1], 64, 1), last)
+        spot = seam * P_SIZE * PITCH + 2 * m
+        for shift, value in ((0, line[0]), (1, middle), (WIN, line[1]), (WIN + 1, last)):
+            for half in range(2):
+                at = spot + half * 8 * PITCH + shift
+                out_ref[pl.ds(at, 8, stride=PITCH), :] = value[8 * half : 8 * half + 8]
+        return (line[0], line[1]), (middle, last)
+
+    def grown(sums, row):
+        left, right = row
+        return (sums[0] + left, sums[1] + right, sums[2] + left * left, sums[3] + right * right)
+
+    def put(seam, top, sums, add):
+        for k in range(4):
+            for half in range(2):
+                at = (seam * P_SIZE + 8 * half) * TAB + k * TOPS + top
+                spot = pl.ds(at, 8, stride=TAB)
+                value = sums[k][8 * half : 8 * half + 8]
+                tab_ref[spot, :] = tab_ref[spot, :] + value if add else value
+
     for seam in range(2):
 
-        def one_pair(m, carry, seam=seam):
-            line = [
-                win_ref[seam, :, pl.ds(pl.multiple_of(m * 384 + c * 128, 128), 128)].astype(F32)
-                for c in range(3)
-            ]
-            last = pltpu.roll(line[2], 64, 1)
-            middle = jnp.where(low, pltpu.roll(line[1], 64, 1), last)
-            spot = seam * P_SIZE * PITCH + 2 * m
-            for shift, value in ((0, line[0]), (1, middle), (WIN, line[1]), (WIN + 1, last)):
-                for half in range(2):
-                    at = spot + half * 8 * PITCH + shift
-                    out_ref[pl.ds(at, 8, stride=PITCH), :] = value[8 * half : 8 * half + 8]
-            return carry
-
-        lax.fori_loop(0, WIN // 2, one_pair, 0, unroll=32)
-
-
-def springs_kernel(edges_ref, stiff_ref, out_ref, ends_scr, stiff_scr):
+        def always(i, sums, seam=seam):
+            even, odd = rows_of(seam, 32 + i)
+            return grown(grown(sums, even), odd)
+
+        def above(i, sums, seam=seam):
+            even, odd = rows_of(seam, 31 - i)
+            sums = grown(sums, odd)
+            put(seam, 63 - 2 * i, sums, False)
+            sums = grown(sums, even)
+            put(seam, 62 - 2 * i, sums, False)
+            return sums
+
+        def below(i, sums, seam=seam):
+            even, odd = rows_of(seam, 64 + i)
+            sums = grown(sums, even)
+            put(seam, 2 * i + 1, sums, True)
+            sums = grown(sums, odd)
+            put(seam, 2 * i + 2, sums, True)
+            return sums
+
+        none = (jnp.zeros((P_SIZE, 128), F32),) * 4
+        sums = lax.fori_loop(0, 32, always, none, unroll=16)
+        put(seam, 64, sums, False)
+        lax.fori_loop(0, 32, above, sums, unroll=16)
+        lax.fori_loop(0, 32, below, none, unroll=16)
+
+
+def springs_kernel(edges_ref, stiff_ref, live_ref, out_ref, ends_scr, stiff_scr):
     ends_scr[...] = jnp.zeros_like(ends_scr)
     stiff_scr[...] = jnp.zeros_like(stiff_scr)
     ends_scr[0:2, 0:E] = edges_ref[...]
@@ -96,7 +130,14 @@
     kind = jnp.where(gap == 1, 0, jnp.where(gap == GV, 1, jnp.where(gap == GV + 1, 2, 3)))
     left = jnp.where(iota((GV, E_PAD), 0) == (low >> 4), stiff_scr[0:1], 0.0)
     right = (iota((128, E_PAD), 0) == kind * GV + (low & (GV - 1))).astype(F32)
-    out_ref[...] = nt_dot(left, right)
+    out_ref[0:GV, :] = nt_dot(left, right)
+    tile_row, tile_col = lax.axis_index("row"), lax.axis_index("col")
+    for seam, (near_row, near_col) in enumerate(((tile_row, tile_col - 1), (tile_row - 1, tile_col))):
+        counts = live_ref[jnp.maximum(near_row, 0), seam : seam + 1, :]
+        wanted = (iota(counts.shape, 1) == near_col) & (near_row >= 0)
+        count = jnp.sum(jnp.where(wanted, counts.astype(F32), 0.0), axis=1, keepdims=True)
+        out_ref[GV + seam : GV + seam + 1, :] = jnp.broadcast_to(count, (1, 128))
+    out_ref[GV + 2 : GV + 8, :] = jnp.zeros((6, 128), F32)
 
 
 def split3(x):
@@ -114,81 +155,62 @@
     return pieces[0]
 
 
-def score(seam, first, slots, tail_ref, sent_ref, frame_ref, s_ref, at, scratch):
-    a_scr, t_scr, list_scr, cand_s, sem = scratch
-    rows = s_ref.shape[0] // 5
-    tail = tail_ref.shape[0] // PATCH * PATCH
-    lists = tail_ref[tail : tail + 16, :].astype(F32)
+def match_kernel(seam, springs_ref, sent_ref, frame_ref, tab_ref, *rest):
+    if seam == 0:
+        other_ref, out_ref, a_scr, t_scr, s_scr, list_scr, cand_s, sem = rest
+    else:
+        out_ref, a_scr, t_scr, s_scr, list_scr, cand_s, sem = rest
+    lists = sent_ref[P_SIZE * PATCH : P_SIZE * PATCH + 16, :].astype(F32)
     list_scr[...] = lists[0:8].astype(jnp.int32)
     copy = pltpu.make_async_copy(list_scr, cand_s, sem)
     copy.start()
-    full_lane = iota((PATCH, 128), 1)
 
     def one_sum(p, carry):
         pixels = sent_ref[pl.ds(pl.multiple_of(p * PATCH, PATCH), PATCH), :].astype(F32)
-        spot = pl.multiple_of(at + p * 8, 8)
+        spot = pl.multiple_of(p * 8, 8)
         for q, part in ((3, fold(pixels)), (4, fold(pixels * pixels))):
-            s_ref[pl.ds(q * rows + spot, 8), :] = jnp.broadcast_to(
+            s_scr[pl.ds(q * 128 + spot, 8), :] = jnp.broadcast_to(
                 jnp.sum(part, axis=0, keepdims=True), (8, 128)
             )
         return carry
 
-    lax.fori_loop(0, slots, one_sum, 0, unroll=2)
+    lax.fori_loop(0, P_SIZE, one_sum, 0, unroll=2)
     copy.wait()
+    count = springs_ref[GV + seam : GV + seam + 1, 0:1].astype(jnp.int32)
+    lane = iota((8, 128), 1)
+    full_lane = iota((PATCH, 128), 1)
+    row = iota((8, 128), 0)
 
     def one_patch(p, carry):
         pixels = sent_ref[pl.ds(pl.multiple_of(p * PATCH, PATCH), PATCH), :]
         a_scr[...] = pixels.astype(F32)
-        base = (seam * P_SIZE + first + p) * PITCH
+        base = (seam * P_SIZE + p) * PITCH
         for s in range(NS):
-            top = base + (cand_s[0, (first + p) * NS + s] + REACH)
-            move_x = cand_s[1, (first + p) * NS + s] + REACH
+            move_y = cand_s[0, p * NS + s] + REACH
+            top = base + move_y
+            move_x = cand_s[1, p * NS + s] + REACH
             crop = jnp.where(
                 full_lane < move_x,
                 frame_ref[pl.ds(top + WIN, PATCH), :],
                 frame_ref[pl.ds(top, PATCH), :],
             )
             cross = fold(pltpu.roll(a_scr[...], move_x, 1) * crop)
-            total = fold(crop)
-            square = fold(crop * crop)
-            for q, part in enumerate((cross, total, square)):
-                t_scr[72 * q + 9 * s : 72 * q + 9 * s + 8, :] = part
-        spot = pl.multiple_of(at + p * 8, 8)
-        for q in range(3):
-            part = t_scr[pl.ds(72 * q, 8, stride=9), :]
-            for k in range(1, 8):
-                part = part + t_scr[pl.ds(72 * q + k, 8, stride=9), :]
-            s_ref[pl.ds(q * rows + spot, 8), :] = part
+            t_scr[9 * s : 9 * s + 8, :] = cross
+            at = (seam * P_SIZE + p) * TAB + move_y
+            for q in range(2):
+                line = jnp.where(
+                    full_lane[0:1] < move_x,
+                    tab_ref[pl.ds(at + (2 * q + 1) * TOPS, 1), :],
+                    tab_ref[pl.ds(at + 2 * q * TOPS, 1), :],
+                )
+                s_scr[pl.ds((q + 1) * 128 + p * 8 + s, 1), :] = line
+        part = t_scr[pl.ds(0, 8, stride=9), :]
+        for k in range(1, 8):
+            part = part + t_scr[pl.ds(k, 8, stride=9), :]
+        s_scr[pl.ds(pl.multiple_of(p * 8, 8), 8), :] = part
         return carry
 
-    lax.fori_loop(0, slots, one_patch, 0, unroll=2)
-    return lists
-
-
-def early_kernel(tail_ref, frame_ref, s_ref, *scratch):
-    score(0, 0, P_EARLY, tail_ref, tail_ref, frame_ref, s_ref, 0, scratch)
-
-
-def match_kernel(seam, live_ref, tail_ref, frame_ref, *rest):
-    if seam == 0:
-        sent_ref, early_ref, springs_ref, other_ref, out_ref, s_scr = rest[:6]
-        done = P_EARLY * NS
-        for q in range(5):
-            s_scr[128 * q : 128 * q + done, :] = early_ref[done * q : done * q + done, :]
-        lists = score(
-            0, P_EARLY, P_SIZE - P_EARLY, tail_ref, sent_ref, frame_ref, s_scr, done, rest[6:]
-        )
-    else:
-        out_ref, s_scr = rest[:2]
-        lists = score(1, 0, P_SIZE, tail_ref, tail_ref, frame_ref, s_scr, 0, rest[2:])
-    tile_row, tile_col = lax.axis_index("row"), lax.axis_index("col")
-    near_row, near_col = (tile_row, tile_col - 1) if seam == 0 else (tile_row - 1, tile_col)
-    counts = live_ref[jnp.maximum(near_row, 0), seam : seam + 1, :]
-    wanted = (iota((1, 16), 1) == near_col) & (near_row >= 0)
-    count = jnp.sum(jnp.where(wanted, counts.astype(F32), 0.0), axis=1, keepdims=True)
-    count = count.astype(jnp.int32)
-    lane = iota((8, 128), 1)
-    row = iota((8, 128), 0)
+    lax.fori_loop(0, P_SIZE, one_patch, 0, unroll=4)
     cross, total, square, a_sum, a_sq = (
         jnp.sum(s_scr[128 * q : 128 * q + 128, :].T, axis=0, keepdims=True) / PIXELS
         for q in range(5)
@@ -224,7 +246,7 @@
         lines = (conf, conf * along_y, conf * along_x)
         cols = jnp.concatenate(lines + (jnp.zeros((5, 128), F32),), axis=0).T
         lane16 = iota((16, 128), 1)
-        block = springs_ref[...]
+        block = springs_ref[0:GV, :]
         for k in range(3):
             block = jnp.where(lane16 == 64 + k, cols[0:16, k : k + 1], block)
         out_ref[0:16, :] = block
@@ -335,7 +357,13 @@
 
 def combine_kernel(mom_ref, u_ref, out_ref):
     total = jnp.sum(mom_ref[...], axis=0, keepdims=True)
-    m = [total[:, k : k + 1] for k in range(6)]
+    lane = iota((1, 128), 1)
+    m = [
+        jnp.broadcast_to(
+            jnp.sum(jnp.where(lane == k, total, 0.0), axis=1, keepdims=True), (1, 128)
+        )
+        for k in range(6)
+    ]
 
     def gram(p, lift):
         out = None
@@ -352,7 +380,7 @@
                 out = term if out is None else out + term
         return out
 
-    one = jnp.ones((1, 1), F32)
+    one = jnp.ones((1, 128), F32)
     r = [one, None, None]
     d = r
     rr = m[0]
@@ -374,7 +402,8 @@
         new = gram(r, False)
         d = [plus(r[i], times(new / rr, d[i])) for i in range(3)]
         rr = new
-    out_ref[...] = x[0] * u_ref[0] + x[1] * u_ref[1] + x[2] * u_ref[2]
+    wide = [jnp.concatenate([c, c], axis=1) for c in x]
+    out_ref[...] = wide[0] * u_ref[0] + wide[1] * u_ref[1] + wide[2] * u_ref[2]
 
 
 def limit(mib):
@@ -396,12 +425,11 @@
     return pl.pallas_call(
         pack_kernel,
         out_shape=tuple(
-            shape((rows, 128), jnp.bfloat16)
-            for rows in (P_EARLY * PATCH + 16, P_SIZE * PATCH + 16, (P_SIZE - P_EARLY) * PATCH)
+            shape((P_SIZE * PATCH + tail, 128), jnp.bfloat16) for tail in (32, 16)
         ),
         in_specs=[HBM, VMEM],
-        out_specs=(VMEM, VMEM, VMEM),
-        scratch_shapes=[pltpu.SemaphoreType.DMA((3,))],
+        out_specs=(VMEM, VMEM),
+        scratch_shapes=[pltpu.SemaphoreType.DMA((2,))],
         compiler_params=limit(4),
     )(patches, candidates)
 
@@ -409,32 +437,11 @@
 def call_frames(windows):
     return pl.pallas_call(
         frames_kernel,
-        out_shape=shape((2 * P_SIZE * PITCH, 128)),
+        out_shape=(shape((2 * P_SIZE * PITCH, 128)), shape((2 * P_SIZE * TAB, 128))),
         in_specs=[VMEM],
-        out_specs=VMEM,
-        compiler_params=limit(12),
+        out_specs=(VMEM, VMEM),
+        compiler_params=limit(16),
     )(windows)
-
-
-def score_scratch():
-    return [
-        pltpu.VMEM((128, 128), F32),
-        pltpu.VMEM((216, 128), F32),
-        pltpu.VMEM((8, 128), jnp.int32),
-        pltpu.SMEM((8, 128), jnp.int32),
-        pltpu.SemaphoreType.DMA,
-    ]
-
-
-def call_early(*operands):
-    return pl.pallas_call(
-        early_kernel,
-        out_shape=shape((5 * P_EARLY * NS, 128)),
-        in_specs=[VMEM] * len(operands),
-        out_specs=VMEM,
-        scratch_shapes=score_scratch(),
-        compiler_params=limit(12),
-    )(*operands)
 
 
 def call_match(seam, *operands):
@@ -443,32 +450,34 @@
         out_shape=shape((24 if seam == 0 else 8, 128)),
         in_specs=[VMEM] * len(operands),
         out_specs=VMEM,
-        scratch_shapes=[pltpu.VMEM((5 * P_SIZE * NS, 128), F32)] + score_scratch(),
-        compiler_params=limit(12),
+        scratch_shapes=[
+            pltpu.VMEM((128, 128), F32),
+            pltpu.VMEM((72, 128), F32),
+            pltpu.VMEM((640, 128), F32),
+            pltpu.VMEM((8, 128), jnp.int32),
+            pltpu.SMEM((8, 128), jnp.int32),
+            pltpu.SemaphoreType.DMA,
+        ],
+        compiler_params=limit(14),
     )(*operands)
 
 
 def body(patches, windows, candidates, live, edges, stiffness):
-    first, to_south, second = call_pack(
-        patches.reshape(2, P_SIZE * PATCH, PATCH), candidates[0, 0]
-    )
-    west_first = shifted(first, "col", 1)
+    to_east, to_south = call_pack(patches.reshape(2, P_SIZE * PATCH, PATCH), candidates[0, 0])
+    sent_west = shifted(to_east, "col", 1)
     sent_north = shifted(to_south, "row", 1)
-    west_second = shifted(second, "col", 1)
-    live = live.transpose(0, 2, 1)
-
-    frames = call_frames(windows[0, 0])
+
+    frames, table = call_frames(windows[0, 0])
     springs = pl.pallas_call(
         springs_kernel,
-        out_shape=shape((GV, 128)),
-        in_specs=[VMEM, VMEM],
+        out_shape=shape((GV + 8, 128)),
+        in_specs=[VMEM, VMEM, VMEM],
         out_specs=VMEM,
         scratch_shapes=[pltpu.VMEM((8, E_PAD), jnp.int32), pltpu.VMEM((8, E_PAD), F32)],
         compiler_params=limit(4),
-    )(edges[0], stiffness)
-    early = call_early(west_first, frames)
-    seam_north = call_match(1, live, sent_north, frames)
-    own = call_match(0, live, west_first, frames, west_second, early, springs, seam_north)
+    )(edges[0], stiffness, live.transpose(0, 2, 1))
+    seam_north = call_match(1, springs, sent_north, frames, table)
+    own = call_match(0, springs, sent_west, frames, table, seam_north)
     inner, outer = swaps(own, "row")
     odd = lax.axis_index("row") % 2 == 1
     centre = jnp.stack([jnp.where(odd, inner, outer), own, jnp.where(odd, outer, inner)])

time: 70.8 us -> 68.8 us (0.972)
  starting transfers between devices: 37.3 us -> 35.2 us
  local copies, waits for them, and re-layouts: 3.58 us -> 5.65 us
  waiting for transfers between devices: 16.6 us -> 15.4 us
  Pallas kernels: 12.2 us -> 11.3 us
    ppermute x3 -> x2, starting transfers between devices: 11.2 us -> 8.36 us  [shifted(): return lax.ppermute(x, axis, pairs)]
    unnamed x12, local copies, waits for them, and re-layouts: 3.58 us -> 5.65 us
    ppermute x4, waiting for transfers between devices: 3.77 us -> 2.6 us  [swaps(): return (lax.ppermute(x, axis, inner), lax.ppermute(x, axis, outer))]
    pallas_call x1, Pallas kernels: 1.53 us -> 0.76 us  [body(): pl.pallas_call(combine_kernel, out_shape=shape((2, GV * GV)), in_specs=[V...]
    pallas_call x4 -> x3, Pallas kernels: 3.46 us -> 3.06 us  [the longest x1 2.52 us: call_frames(): pl.pallas_call(frames_kernel, out_shape=(shape((2 * P_SIZE * PITCH, 128))...]
  transfers between devices with their start and end apart: 8 -> 7, of which waited for: 3 -> 3; matrix products, arithmetic and copies ran while one was open for 0% -> 0% of each run, Pallas kernels for 10% -> 9%
where the time goes in v4:
time: 68.8 us; the launch traced here: 68.4 us
  starting transfers between devices  35.2 us (51%)
  waiting for transfers between devices  15.4 us (22%)
  Pallas kernels  11.3 us (16%)
  local copies, waits for them, and re-layouts  5.65 us (8%)
  between operations  0.78 us (1%)
    all_to_all x1, starting transfers between devices, body(): lax.all_to_all(moments, ('row', 'col'), 0, 0).reshape(devices, 128)  18.7 us
    all_to_all x1, waiting for transfers between devices, body(): lax.all_to_all(moments, ('row', 'col'), 0, 0).reshape(devices, 128)  12.8 us
    ppermute x2, starting transfers between devices, shifted(): return lax.ppermute(x, axis, pairs)  8.36 us
    ppermute x4, starting transfers between devices, swaps(): return (lax.ppermute(x, axis, inner), lax.ppermute(x, axis, outer))  8.09 us
    pallas_call x2, Pallas kernels, call_match(): pl.pallas_call(functools.partial(match_kernel, seam), out_shape=shape((24...  5.82 us
    unnamed x12, local copies, waits for them, and re-layouts  5.65 us
    ppermute x4, waiting for transfers between devices, swaps(): return (lax.ppermute(x, axis, inner), lax.ppermute(x, axis, outer))  2.6 us
    pallas_call x1, Pallas kernels, call_frames(): pl.pallas_call(frames_kernel, out_shape=(shape((2 * P_SIZE * PITCH, 128))...  2.52 us
  transfers between devices with their start and end apart: 7, of which 3 were waited for; matrix products, arithmetic and copies ran while one was open for 0% of the time, Pallas kernels for 9%

profile of v4, /device:TPU:1, one launch (start us, length us, event | category | flops | bytes accessed | tf_op | source)
XLA Modules:
  0.0 68.4 jit_solution(15416058423115957543)
XLA Ops:
  0.6 0.0 copy-start.1
  0.6 1.2 %copy-done.1 = bf16[1,1,2,16,128,128]{5,4,3,2,1,0:T(8,128)(2,1)S(1)} copy-done((bf16[1,1,2,16,128,128]{5,4,3,2,1,0:T(8,128)(2,1)S(1)}, bf16[1,1,2,16,128,128]{5,4,3,2,1,0:T(8,128)(2,1)}, u32[]{:S(2)}) %copy-start.1) | copy-done | bytes 1048600
  1.9 0.0 copy-start.5
  1.9 0.7 copy-done.5
  2.5 0.1 shard_map.78
  2.6 4.0 %collective-permute-start = (bf16[2080,128]{1,0:T(8,128)(2,1)S(1)}, bf16[2080,128]{1,0:T(8,128)(2,1)S(1)}, u32[]{:S(2)}, u32[]{:S(2)}) collective-permute-start(bf16[2080,128]{1,0:T(8,128)(2,1)S(1)} %get-tuple-element.9), channel_id=1, source_target_pairs={{0,1},{1,2},{2,3},{3,4},{4,5},{5,6},{6,7},{7,8},{8,9},{9,10},{10,1... | collective-permute-start | bytes 1597448 | tf_op jit(solution)/shard_map/ppermute | solution.py:34
  6.6 4.4 %collective-permute-start.1 = (bf16[2064,128]{1,0:T(8,128)(2,1)S(1)}, bf16[2064,128]{1,0:T(8,128)(2,1)S(1)}, u32[]{:S(2)}, u32[]{:S(2)}) collective-permute-start(bf16[2064,128]{1,0:T(8,128)(2,1)S(1)} %get-tuple-element.12), channel_id=1, source_target_pairs={{0,16},{16,32},{32,48},{48,64},{64,80},{80,96},{96,112},{112,128},... | collective-permute-start | bytes 1585160 | tf_op jit(solution)/shard_map/ppermute | solution.py:34
  11.0 0.0 copy-start
  11.0 1.7 %copy-done = bf16[1,1,2,16,36864]{4,3,2,1,0:T(8,128)(2,1)S(1)} copy-done((bf16[1,1,2,16,36864]{4,3,2,1,0:T(8,128)(2,1)S(1)}, bf16[1,1,2,16,36864]{4,3,2,1,0:T(8,128)(2,1)}, u32[]{:S(2)}) %copy-start) | copy-done | bytes 2359320
  12.7 2.5 %shard_map.79 = (f32[12320,128]{1,0:T(8,128)S(1)}, f32[8352,128]{1,0:T(8,128)S(1)}) custom-call(bf16[2,16,36864]{2,1,0:T(8,128)(2,1)S(1)} %bitcast.15), custom_call_target="tpu_custom_call" | custom-call | tf_op jit(solution)/shard_map/pallas_call | solution.py:438
  15.2 0.0 copy-start.2
  15.2 0.7 %copy-done.2 = s32[16,16,2]{1,2,0:T(2,128)S(1)} copy-done((s32[16,16,2]{1,2,0:T(2,128)S(1)}, s32[16,16,2]{1,2,0:T(2,128)}, u32[]{:S(2)}) %copy-start.2) | copy-done | bytes 2072
  15.9 0.7 %copy-done.3 = s32[1,2,705]{2,1,0:T(2,128)S(1)} copy-done((s32[1,2,705]{2,1,0:T(2,128)S(1)}, s32[1,2,705]{2,1,0:T(2,128)}, u32[]{:S(2)}) %copy-start.3) | copy-done | bytes 5664
  16.6 0.7 copy-done.4
  17.3 0.4 shard_map.77.springs_ref
  17.8 0.0 collective-permute-done.1.sent_ref
  17.8 2.9 %shard_map.80.rest_0_ = f32[8,128]{1,0:T(8,128)S(1)} custom-call(f32[24,128]{1,0:T(8,128)S(1)} %shard_map.77.springs_ref, bf16[2064,128]{1,0:T(8,128)(2,1)S(1)} %collective-permute-done.1.sent_ref, f32[12320,128]{1,0:T(8,128)S(1)} %get-tuple-element.10.frame_ref, f32[8352,128]{1,0:T(8,128)S(1)} %get-tuple-element.11.tab_ref), custom_call_target="tpu_custom_call" | custom-call | tf_op jit(solution)/shard_map/pallas_call | solution.py:448
  20.6 0.0 collective-permute-done.sent_ref
  20.7 2.9 %shard_map.81 = f32[24,128]{1,0:T(8,128)S(1)} custom-call(f32[24,128]{1,0:T(8,128)S(1)} %shard_map.77.springs_ref, bf16[2080,128]{1,0:T(8,128)(2,1)S(1)} %collective-permute-done.sent_ref, f32[12320,128]{1,0:T(8,128)S(1)} %get-tuple-element.10.frame_ref, f32[8352,128]{1,0:T(8,128)S(1)} %get-tuple-element.11.tab_ref, f32[8,128]{1,0:T(8,128)S(1)} %shard_map.80.rest_0_), custom_call_target="tpu_custom_call" | custom-call | tf_op jit(solution)/shard_map/pallas_call | solution.py:448
  23.6 3.8 %collective-permute-start.3 = (f32[24,128]{1,0:T(8,128)S(1)}, f32[24,128]{1,0:T(8,128)S(1)}, u32[]{:S(2)}, u32[]{:S(2)}) collective-permute-start(f32[24,128]{1,0:T(8,128)S(1)} %shard_map.81), channel_id=1, source_target_pairs={{16,32},{32,16},{48,64},{64,48},{80,96},{96,80},{112,128},{128,112... | collective-permute-start | bytes 36872 | tf_op jit(solution)/shard_map/ppermute | solution.py:421
  27.4 0.1 collective-permute-start.2
  27.5 1.3 %collective-permute-done.3 = f32[24,128]{1,0:T(8,128)S(1)} collective-permute-done((f32[24,128]{1,0:T(8,128)S(1)}, f32[24,128]{1,0:T(8,128)S(1)}, u32[]{:S(2)}, u32[]{:S(2)}) %collective-permute-start.3) | collective-permute-done | bytes 12320 | tf_op jit(solution)/shard_map/ppermute | solution.py:421
  28.8 0.0 collective-permute-done.2
  28.8 0.7 collective-permute-start.5
  29.5 3.5 %collective-permute-start.4 = (f32[3,24,128]{2,1,0:T(8,128)S(1)}, f32[3,24,128]{2,1,0:T(8,128)S(1)}, u32[]{:S(2)}, u32[]{:S(2)}) collective-permute-start(f32[3,24,128]{2,1,0:T(8,128)S(1)} %pad_maximum_fusion.centre_ref), channel_id=1, source_target_pairs={{0,1},{1,0},{2,3},{3,2},{4,5},{5,4},{6,7},{7,6},{8,9},{9,8},{10,11... | collective-permute-start | bytes 110600 | tf_op jit(solution)/shard_map/ppermute | solution.py:421
  33.0 0.0 collective-permute-done.5.outer_ref
  33.0 1.3 %collective-permute-done.4.inner_ref = f32[3,24,128]{2,1,0:T(8,128)S(1)} collective-permute-done((f32[3,24,128]{2,1,0:T(8,128)S(1)}, f32[3,24,128]{2,1,0:T(8,128)S(1)}, u32[]{:S(2)}, u32[]{:S(2)}) %collective-permute-start.4) | collective-permute-done | bytes 36896 | tf_op jit(solution)/shard_map/ppermute | solution.py:421
  34.4 1.4 %shard_map.82 = (f32[3,16,128]{2,1,0:T(8,128)S(1)}, f32[256,1,128]{2,1,0:T(1,128)}, f32[3,2,16]{2,1,0:T(2,128)}) custom-call(f32[3,24,128]{2,1,0:T(8,128)S(1)} %collective-permute-done.4.inner_ref, f32[3,24,128]{2,1,0:T(8,128)S(1)} %pad_maximum_fusion.centre_ref, f32[3,24,128]{2,1,0:T(8,128)S(1)} %collective-permute-done.5.outer_ref), custom_call_target="tpu_custom_call" | custom-call | tf_op jit(solution)/shard_map/pallas_call | solution.py:486
  35.8 18.7 %all-to-all-start = ((f32[256,1,128]{2,1,0:T(1,128)}), f32[256,1,128]{2,1,0:T(1,128)S(1)}, u32[]{:S(2)}, u32[]{:S(2)}) async-start(f32[256,1,128]{2,1,0:T(1,128)} %get-tuple-element.14), calls=%async_computation | async-start | bytes 262144 | tf_op jit(solution)/shard_map/all_to_all | solution.py:493
  54.5 0.2 shard_map.83.u_ref
  54.8 12.8 %all-to-all-done = f32[256,1,128]{2,1,0:T(1,128)S(1)} async-done(((f32[256,1,128]{2,1,0:T(1,128)}), f32[256,1,128]{2,1,0:T(1,128)S(1)}, u32[]{:S(2)}, u32[]{:S(2)}) %all-to-all-start) | async-done | bytes 131104 | tf_op jit(solution)/shard_map/all_to_all | solution.py:493
  67.6 0.8 %shard_map.84 = f32[2,256]{1,0:T(2,128)} custom-call(f32[256,128]{1,0:T(8,128)S(1)} %bitcast.17, f32[3,2,256]{2,1,0:T(2,128)S(1)} %shard_map.83.u_ref), custom_call_target="tpu_custom_call" | custom-call | tf_op jit(solution)/shard_map/pallas_call | solution.py:501
  (4 shorter events, 0.0 us)
Async XLA Ops:
  0.6 1.2 %copy-start.1 = (bf16[1,1,2,16,128,128]{5,4,3,2,1,0:T(8,128)(2,1)S(1)}, bf16[1,1,2,16,128,128]{5,4,3,2,1,0:T(8,128)(2,1)}, u32[]{:S(2)}) copy-start(bf16[1,1,2,16,128,128]{5,4,3,2,1,0:T(8,128)(2,1)} %param.6) | copy-start | bytes 3145732
  1.9 0.7 copy-start.5
  2.6 18.0 %collective-permute-start = (bf16[2080,128]{1,0:T(8,128)(2,1)S(1)}, bf16[2080,128]{1,0:T(8,128)(2,1)S(1)}, u32[]{:S(2)}, u32[]{:S(2)}) collective-permute-start(bf16[2080,128]{1,0:T(8,128)(2,1)S(1)} %get-tuple-element.9), channel_id=1, source_target_pairs={{0,1},{1,2},{2,3},{3,4},{4,5},{5,6},{6,7},{7,8},{8,9},{9,10},{10,1... | collective-permute-start | bytes 1597448 | tf_op jit(solution)/shard_map/ppermute | solution.py:34
  6.6 11.1 %collective-permute-start.1 = (bf16[2064,128]{1,0:T(8,128)(2,1)S(1)}, bf16[2064,128]{1,0:T(8,128)(2,1)S(1)}, u32[]{:S(2)}, u32[]{:S(2)}) collective-permute-start(bf16[2064,128]{1,0:T(8,128)(2,1)S(1)} %get-tuple-element.12), channel_id=1, source_target_pairs={{0,16},{16,32},{32,48},{48,64},{64,80},{80,96},{96,112},{112,128},... | collective-permute-start | bytes 1585160 | tf_op jit(solution)/shard_map/ppermute | solution.py:34
  11.0 1.7 %copy-start = (bf16[1,1,2,16,36864]{4,3,2,1,0:T(8,128)(2,1)S(1)}, bf16[1,1,2,16,36864]{4,3,2,1,0:T(8,128)(2,1)}, u32[]{:S(2)}) copy-start(bf16[1,1,2,16,36864]{4,3,2,1,0:T(8,128)(2,1)} %param.7) | copy-start | bytes 7077892
  15.2 0.7 %copy-start.2 = (s32[16,16,2]{1,2,0:T(2,128)S(1)}, s32[16,16,2]{1,2,0:T(2,128)}, u32[]{:S(2)}) copy-start(s32[16,16,2]{1,2,0:T(2,128)} %param.9) | copy-start | bytes 6148
  15.9 0.7 %copy-start.3 = (s32[1,2,705]{2,1,0:T(2,128)S(1)}, s32[1,2,705]{2,1,0:T(2,128)}, u32[]{:S(2)}) copy-start(s32[1,2,705]{2,1,0:T(2,128)} %param.10) | copy-start | bytes 16924
  16.6 0.7 %copy-start.4 = (f32[1,705]{1,0:T(1,128)S(1)}, f32[1,705]{1,0:T(1,128)}, u32[]{:S(2)}) copy-start(f32[1,705]{1,0:T(1,128)} %stiff_ref.1) | copy-start | bytes 8464
  23.6 5.2 %collective-permute-start.3 = (f32[24,128]{1,0:T(8,128)S(1)}, f32[24,128]{1,0:T(8,128)S(1)}, u32[]{:S(2)}, u32[]{:S(2)}) collective-permute-start(f32[24,128]{1,0:T(8,128)S(1)} %shard_map.81), channel_id=1, source_target_pairs={{16,32},{32,16},{48,64},{64,48},{80,96},{96,80},{112,128},{128,112... | collective-permute-start | bytes 36872 | tf_op jit(solution)/shard_map/ppermute | solution.py:421
  27.4 1.4 %collective-permute-start.2 = (f32[24,128]{1,0:T(8,128)S(1)}, f32[24,128]{1,0:T(8,128)S(1)}, u32[]{:S(2)}, u32[]{:S(2)}) collective-permute-start(f32[24,128]{1,0:T(8,128)S(1)} %shard_map.81), channel_id=1, source_target_pairs={{0,16},{16,0},{32,48},{48,32},{64,80},{80,64},{96,112},{112,96},{1... | collective-permute-start | bytes 36872 | tf_op jit(solution)/shard_map/ppermute | solution.py:421
  28.8 4.2 %collective-permute-start.5 = (f32[3,24,128]{2,1,0:T(8,128)S(1)}, f32[3,24,128]{2,1,0:T(8,128)S(1)}, u32[]{:S(2)}, u32[]{:S(2)}) collective-permute-start(f32[3,24,128]{2,1,0:T(8,128)S(1)} %pad_maximum_fusion.centre_ref), channel_id=1, source_target_pairs={{1,2},{2,1},{3,4},{4,3},{5,6},{6,5},{7,8},{8,7},{9,10},{10,9},{11,... | collective-permute-start | bytes 110600 | tf_op jit(solution)/shard_map/ppermute | solution.py:421
  29.5 4.9 %collective-permute-start.4 = (f32[3,24,128]{2,1,0:T(8,128)S(1)}, f32[3,24,128]{2,1,0:T(8,128)S(1)}, u32[]{:S(2)}, u32[]{:S(2)}) collective-permute-start(f32[3,24,128]{2,1,0:T(8,128)S(1)} %pad_maximum_fusion.centre_ref), channel_id=1, source_target_pairs={{0,1},{1,0},{2,3},{3,2},{4,5},{5,4},{6,7},{7,6},{8,9},{9,8},{10,11... | collective-permute-start | bytes 110600 | tf_op jit(solution)/shard_map/ppermute | solution.py:421
  35.8 31.8 %all-to-all-start = ((f32[256,1,128]{2,1,0:T(1,128)}), f32[256,1,128]{2,1,0:T(1,128)S(1)}, u32[]{:S(2)}, u32[]{:S(2)}) async-start(f32[256,1,128]{2,1,0:T(1,128)} %get-tuple-element.14), calls=%async_computation | async-start | bytes 262144 | tf_op jit(solution)/shard_map/all_to_all | solution.py:493

commit v5 on v4

--- a/solution.py
+++ b/solution.py
@@ -210,7 +210,7 @@
         s_scr[pl.ds(pl.multiple_of(p * 8, 8), 8), :] = part
         return carry
 
-    lax.fori_loop(0, P_SIZE, one_patch, 0, unroll=4)
+    lax.fori_loop(0, P_SIZE, one_patch, 0, unroll=8)
     cross, total, square, a_sum, a_sq = (
         jnp.sum(s_scr[128 * q : 128 * q + 128, :].T, axis=0, keepdims=True) / PIXELS
         for q in range(5)
@@ -260,22 +260,25 @@
     west = jnp.where(odd, inner_ref[...], outer_ref[...])
     east = jnp.where(odd, outer_ref[...], inner_ref[...])
     tiles = (west, centre_ref[...], east)
-    lane = iota((48, 128), 1)
-    row = iota((48, 128), 0)
-    blocks = [jnp.concatenate([tile[a, 0:16, :] for a in range(3)], axis=0) for tile in tiles]
+    lane = iota((32, 128), 1)
+    row = iota((32, 128), 0)
+    spans = (slice(8, 16), slice(0, 16), slice(0, 8))
+    blocks = [
+        jnp.concatenate([tile[a, spans[a], :] for a in range(3)], axis=0) for tile in tiles
+    ]
 
     def both(x):
         return x + pltpu.roll(x, 64, 1)
 
     def plane(t):
-        out = jnp.zeros((48, 128), F32)
+        out = jnp.zeros((32, 128), F32)
         for b in range(3):
             moved = pltpu.roll(blocks[b], (16 * b - 16 * t) % 128, 1)
             out = jnp.where((lane >> 4) == b, moved, out)
         return both(out)
 
     def west_seam(lane_y, lane_x):
-        out = jnp.zeros((48, 128), F32)
+        out = jnp.zeros((32, 128), F32)
         for b in (1, 2):
             out = jnp.where(lane == 16 * b - 1, blocks[b][:, lane_y : lane_y + 1], out)
             out = jnp.where(lane == 16 * b + 63, blocks[b][:, lane_x : lane_x + 1], out)
@@ -286,10 +289,10 @@
         return lines[0] + pltpu.roll(lines[1], 16, 1) + pltpu.roll(lines[2], 32, 1)
 
     def north_seam(r_y, r_x):
-        out = jnp.zeros((48, 128), F32)
+        out = jnp.zeros((32, 128), F32)
         for a in (1, 2):
             line = north_lines(a, r_y) + pltpu.roll(north_lines(a, r_x), 64, 1)
-            out = jnp.where(row == 16 * a - 1, line, out)
+            out = jnp.where(row == 16 * a - 9, line, out)
         return out
 
     q_h = plane(0) + west_seam(64, 64)
@@ -309,7 +312,7 @@
         return pltpu.roll(x, 1, 0)
 
     def up(x):
-        return pltpu.roll(x, 47, 0)
+        return pltpu.roll(x, 31, 0)
 
     def operate(v):
         below = up(v)
@@ -324,7 +327,7 @@
     u1 = operate(u0)
     u2 = operate(u1)
     u3 = operate(u2)
-    own = slice(16, 32)
+    own = slice(8, 24)
     lane16 = lane[own]
     inside = ((lane16 >= 16) & (lane16 < 32)) | ((lane16 >= 80) & (lane16 < 96))
     parts = [jnp.where(inside, x[own], 0.0) for x in (u0, u1, u2, u3)]

time: 68.8 us -> 68.1 us (0.990)
  no operation moved by 1% of the time
where the time goes in v5:
time: 68.1 us; the launch traced here: 67.7 us
  starting transfers between devices  35.1 us (52%)
  waiting for transfers between devices  15.4 us (23%)
  Pallas kernels  10.7 us (16%)
  local copies, waits for them, and re-layouts  5.65 us (8%)
  between operations  0.78 us (1%)
    all_to_all x1, starting transfers between devices, body(): lax.all_to_all(moments, ('row', 'col'), 0, 0).reshape(devices, 128)  18.7 us
    all_to_all x1, waiting for transfers between devices, body(): lax.all_to_all(moments, ('row', 'col'), 0, 0).reshape(devices, 128)  12.8 us
    ppermute x2, starting transfers between devices, shifted(): return lax.ppermute(x, axis, pairs)  8.36 us
    ppermute x4, starting transfers between devices, swaps(): return (lax.ppermute(x, axis, inner), lax.ppermute(x, axis, outer))  8.06 us
    unnamed x12, local copies, waits for them, and re-layouts  5.65 us
    pallas_call x2, Pallas kernels, call_match(): pl.pallas_call(functools.partial(match_kernel, seam), out_shape=shape((24...  5.22 us
    ppermute x4, waiting for transfers between devices, swaps(): return (lax.ppermute(x, axis, inner), lax.ppermute(x, axis, outer))  2.6 us
    pallas_call x1, Pallas kernels, call_frames(): pl.pallas_call(frames_kernel, out_shape=(shape((2 * P_SIZE * PITCH, 128))...  2.52 us
  transfers between devices with their start and end apart: 7, of which 3 were waited for; matrix products, arithmetic and copies ran while one was open for 0% of the time, Pallas kernels for 9%

profile of v5, /device:TPU:1, one launch (start us, length us, event | category | flops | bytes accessed | tf_op | source)
XLA Modules:
  0.0 67.7 jit_solution(13776670506096283995)
XLA Ops:
  0.6 0.0 copy-start.1
  0.6 1.2 %copy-done.1 = bf16[1,1,2,16,128,128]{5,4,3,2,1,0:T(8,128)(2,1)S(1)} copy-done((bf16[1,1,2,16,128,128]{5,4,3,2,1,0:T(8,128)(2,1)S(1)}, bf16[1,1,2,16,128,128]{5,4,3,2,1,0:T(8,128)(2,1)}, u32[]{:S(2)}) %copy-start.1) | copy-done | bytes 1048600
  1.9 0.0 copy-start.5
  1.9 0.7 %copy-done.5 = s32[1,1,2,2,128]{4,3,2,1,0:T(2,128)S(1)} copy-done((s32[1,1,2,2,128]{4,3,2,1,0:T(2,128)S(1)}, s32[1,1,2,2,128]{4,3,2,1,0:T(2,128)}, u32[]{:S(2)}) %copy-start.5) | copy-done | bytes 2072
  2.5 0.1 shard_map.78
  2.6 4.0 %collective-permute-start = (bf16[2080,128]{1,0:T(8,128)(2,1)S(1)}, bf16[2080,128]{1,0:T(8,128)(2,1)S(1)}, u32[]{:S(2)}, u32[]{:S(2)}) collective-permute-start(bf16[2080,128]{1,0:T(8,128)(2,1)S(1)} %get-tuple-element.9), channel_id=1, source_target_pairs={{0,1},{1,2},{2,3},{3,4},{4,5},{5,6},{6,7},{7,8},{8,9},{9,10},{10,1... | collective-permute-start | bytes 1597448 | tf_op jit(solution)/shard_map/ppermute | solution.py:34
  6.6 4.4 %collective-permute-start.1 = (bf16[2064,128]{1,0:T(8,128)(2,1)S(1)}, bf16[2064,128]{1,0:T(8,128)(2,1)S(1)}, u32[]{:S(2)}, u32[]{:S(2)}) collective-permute-start(bf16[2064,128]{1,0:T(8,128)(2,1)S(1)} %get-tuple-element.12), channel_id=1, source_target_pairs={{0,16},{16,32},{32,48},{48,64},{64,80},{80,96},{96,112},{112,128},... | collective-permute-start | bytes 1585160 | tf_op jit(solution)/shard_map/ppermute | solution.py:34
  11.0 0.0 copy-start
  11.0 1.7 %copy-done = bf16[1,1,2,16,36864]{4,3,2,1,0:T(8,128)(2,1)S(1)} copy-done((bf16[1,1,2,16,36864]{4,3,2,1,0:T(8,128)(2,1)S(1)}, bf16[1,1,2,16,36864]{4,3,2,1,0:T(8,128)(2,1)}, u32[]{:S(2)}) %copy-start) | copy-done | bytes 2359320
  12.7 2.5 %shard_map.79 = (f32[12320,128]{1,0:T(8,128)S(1)}, f32[8352,128]{1,0:T(8,128)S(1)}) custom-call(bf16[2,16,36864]{2,1,0:T(8,128)(2,1)S(1)} %bitcast.15), custom_call_target="tpu_custom_call" | custom-call | tf_op jit(solution)/shard_map/pallas_call | solution.py:441
  15.2 0.0 copy-start.2
  15.2 0.7 %copy-done.2 = s32[16,16,2]{1,2,0:T(2,128)S(1)} copy-done((s32[16,16,2]{1,2,0:T(2,128)S(1)}, s32[16,16,2]{1,2,0:T(2,128)}, u32[]{:S(2)}) %copy-start.2) | copy-done | bytes 2072
  15.9 0.7 %copy-done.3 = s32[1,2,705]{2,1,0:T(2,128)S(1)} copy-done((s32[1,2,705]{2,1,0:T(2,128)S(1)}, s32[1,2,705]{2,1,0:T(2,128)}, u32[]{:S(2)}) %copy-start.3) | copy-done | bytes 5664
  16.6 0.7 %copy-done.4 = f32[1,705]{1,0:T(1,128)S(1)} copy-done((f32[1,705]{1,0:T(1,128)S(1)}, f32[1,705]{1,0:T(1,128)}, u32[]{:S(2)}) %copy-start.4) | copy-done | bytes 2844
  17.3 0.4 shard_map.77.springs_ref
  17.8 0.0 collective-permute-done.1.sent_ref
  17.8 2.6 %shard_map.80.rest_0_ = f32[8,128]{1,0:T(8,128)S(1)} custom-call(f32[24,128]{1,0:T(8,128)S(1)} %shard_map.77.springs_ref, bf16[2064,128]{1,0:T(8,128)(2,1)S(1)} %collective-permute-done.1.sent_ref, f32[12320,128]{1,0:T(8,128)S(1)} %get-tuple-element.10.frame_ref, f32[8352,128]{1,0:T(8,128)S(1)} %get-tuple-element.11.tab_ref), custom_call_target="tpu_custom_call" | custom-call | tf_op jit(solution)/shard_map/pallas_call | solution.py:451
  20.4 0.0 collective-permute-done.sent_ref
  20.4 2.6 %shard_map.81 = f32[24,128]{1,0:T(8,128)S(1)} custom-call(f32[24,128]{1,0:T(8,128)S(1)} %shard_map.77.springs_ref, bf16[2080,128]{1,0:T(8,128)(2,1)S(1)} %collective-permute-done.sent_ref, f32[12320,128]{1,0:T(8,128)S(1)} %get-tuple-element.10.frame_ref, f32[8352,128]{1,0:T(8,128)S(1)} %get-tuple-element.11.tab_ref, f32[8,128]{1,0:T(8,128)S(1)} %shard_map.80.rest_0_), custom_call_target="tpu_custom_call" | custom-call | tf_op jit(solution)/shard_map/pallas_call | solution.py:451
  23.0 3.8 %collective-permute-start.3 = (f32[24,128]{1,0:T(8,128)S(1)}, f32[24,128]{1,0:T(8,128)S(1)}, u32[]{:S(2)}, u32[]{:S(2)}) collective-permute-start(f32[24,128]{1,0:T(8,128)S(1)} %shard_map.81), channel_id=1, source_target_pairs={{16,32},{32,16},{48,64},{64,48},{80,96},{96,80},{112,128},{128,112... | collective-permute-start | bytes 36872 | tf_op jit(solution)/shard_map/ppermute | solution.py:424
  26.8 0.1 collective-permute-start.2
  26.9 1.3 %collective-permute-done.3 = f32[24,128]{1,0:T(8,128)S(1)} collective-permute-done((f32[24,128]{1,0:T(8,128)S(1)}, f32[24,128]{1,0:T(8,128)S(1)}, u32[]{:S(2)}, u32[]{:S(2)}) %collective-permute-start.3) | collective-permute-done | bytes 12320 | tf_op jit(solution)/shard_map/ppermute | solution.py:424
  28.2 0.0 collective-permute-done.2
  28.2 0.7 collective-permute-start.5
  28.9 3.5 %collective-permute-start.4 = (f32[3,24,128]{2,1,0:T(8,128)S(1)}, f32[3,24,128]{2,1,0:T(8,128)S(1)}, u32[]{:S(2)}, u32[]{:S(2)}) collective-permute-start(f32[3,24,128]{2,1,0:T(8,128)S(1)} %pad_maximum_fusion.centre_ref), channel_id=1, source_target_pairs={{0,1},{1,0},{2,3},{3,2},{4,5},{5,4},{6,7},{7,6},{8,9},{9,8},{10,11... | collective-permute-start | bytes 110600 | tf_op jit(solution)/shard_map/ppermute | solution.py:424
  32.4 0.0 collective-permute-done.5.outer_ref
  32.4 1.3 %collective-permute-done.4.inner_ref = f32[3,24,128]{2,1,0:T(8,128)S(1)} collective-permute-done((f32[3,24,128]{2,1,0:T(8,128)S(1)}, f32[3,24,128]{2,1,0:T(8,128)S(1)}, u32[]{:S(2)}, u32[]{:S(2)}) %collective-permute-start.4) | collective-permute-done | bytes 36896 | tf_op jit(solution)/shard_map/ppermute | solution.py:424
  33.7 1.4 %shard_map.82 = (f32[3,16,128]{2,1,0:T(8,128)S(1)}, f32[256,1,128]{2,1,0:T(1,128)}, f32[3,2,16]{2,1,0:T(2,128)}) custom-call(f32[3,24,128]{2,1,0:T(8,128)S(1)} %collective-permute-done.4.inner_ref, f32[3,24,128]{2,1,0:T(8,128)S(1)} %pad_maximum_fusion.centre_ref, f32[3,24,128]{2,1,0:T(8,128)S(1)} %collective-permute-done.5.outer_ref), custom_call_target="tpu_custom_call" | custom-call | tf_op jit(solution)/shard_map/pallas_call | solution.py:489
  35.2 18.7 %all-to-all-start = ((f32[256,1,128]{2,1,0:T(1,128)}), f32[256,1,128]{2,1,0:T(1,128)S(1)}, u32[]{:S(2)}, u32[]{:S(2)}) async-start(f32[256,1,128]{2,1,0:T(1,128)} %get-tuple-element.14), calls=%async_computation | async-start | bytes 262144 | tf_op jit(solution)/shard_map/all_to_all | solution.py:496
  53.9 0.2 shard_map.83.u_ref
  54.1 12.8 %all-to-all-done = f32[256,1,128]{2,1,0:T(1,128)S(1)} async-done(((f32[256,1,128]{2,1,0:T(1,128)}), f32[256,1,128]{2,1,0:T(1,128)S(1)}, u32[]{:S(2)}, u32[]{:S(2)}) %all-to-all-start) | async-done | bytes 131104 | tf_op jit(solution)/shard_map/all_to_all | solution.py:496
  66.9 0.8 %shard_map.84 = f32[2,256]{1,0:T(2,128)} custom-call(f32[256,128]{1,0:T(8,128)S(1)} %bitcast.17, f32[3,2,256]{2,1,0:T(2,128)S(1)} %shard_map.83.u_ref), custom_call_target="tpu_custom_call" | custom-call | tf_op jit(solution)/shard_map/pallas_call | solution.py:504
  (4 shorter events, 0.0 us)
Async XLA Ops:
  0.6 1.2 %copy-start.1 = (bf16[1,1,2,16,128,128]{5,4,3,2,1,0:T(8,128)(2,1)S(1)}, bf16[1,1,2,16,128,128]{5,4,3,2,1,0:T(8,128)(2,1)}, u32[]{:S(2)}) copy-start(bf16[1,1,2,16,128,128]{5,4,3,2,1,0:T(8,128)(2,1)} %param.6) | copy-start | bytes 3145732
  1.9 0.7 %copy-start.5 = (s32[1,1,2,2,128]{4,3,2,1,0:T(2,128)S(1)}, s32[1,1,2,2,128]{4,3,2,1,0:T(2,128)}, u32[]{:S(2)}) copy-start(s32[1,1,2,2,128]{4,3,2,1,0:T(2,128)} %param.8) | copy-start | bytes 6148
  2.6 17.7 %collective-permute-start = (bf16[2080,128]{1,0:T(8,128)(2,1)S(1)}, bf16[2080,128]{1,0:T(8,128)(2,1)S(1)}, u32[]{:S(2)}, u32[]{:S(2)}) collective-permute-start(bf16[2080,128]{1,0:T(8,128)(2,1)S(1)} %get-tuple-element.9), channel_id=1, source_target_pairs={{0,1},{1,2},{2,3},{3,4},{4,5},{5,6},{6,7},{7,8},{8,9},{9,10},{10,1... | collective-permute-start | bytes 1597448 | tf_op jit(solution)/shard_map/ppermute | solution.py:34
  6.6 11.1 %collective-permute-start.1 = (bf16[2064,128]{1,0:T(8,128)(2,1)S(1)}, bf16[2064,128]{1,0:T(8,128)(2,1)S(1)}, u32[]{:S(2)}, u32[]{:S(2)}) collective-permute-start(bf16[2064,128]{1,0:T(8,128)(2,1)S(1)} %get-tuple-element.12), channel_id=1, source_target_pairs={{0,16},{16,32},{32,48},{48,64},{64,80},{80,96},{96,112},{112,128},... | collective-permute-start | bytes 1585160 | tf_op jit(solution)/shard_map/ppermute | solution.py:34
  11.0 1.7 %copy-start = (bf16[1,1,2,16,36864]{4,3,2,1,0:T(8,128)(2,1)S(1)}, bf16[1,1,2,16,36864]{4,3,2,1,0:T(8,128)(2,1)}, u32[]{:S(2)}) copy-start(bf16[1,1,2,16,36864]{4,3,2,1,0:T(8,128)(2,1)} %param.7) | copy-start | bytes 7077892
  15.2 0.7 %copy-start.2 = (s32[16,16,2]{1,2,0:T(2,128)S(1)}, s32[16,16,2]{1,2,0:T(2,128)}, u32[]{:S(2)}) copy-start(s32[16,16,2]{1,2,0:T(2,128)} %param.9) | copy-start | bytes 6148
  15.9 0.7 %copy-start.3 = (s32[1,2,705]{2,1,0:T(2,128)S(1)}, s32[1,2,705]{2,1,0:T(2,128)}, u32[]{:S(2)}) copy-start(s32[1,2,705]{2,1,0:T(2,128)} %param.10) | copy-start | bytes 16924
  16.6 0.7 %copy-start.4 = (f32[1,705]{1,0:T(1,128)S(1)}, f32[1,705]{1,0:T(1,128)}, u32[]{:S(2)}) copy-start(f32[1,705]{1,0:T(1,128)} %stiff_ref.1) | copy-start | bytes 8464
  23.0 5.2 %collective-permute-start.3 = (f32[24,128]{1,0:T(8,128)S(1)}, f32[24,128]{1,0:T(8,128)S(1)}, u32[]{:S(2)}, u32[]{:S(2)}) collective-permute-start(f32[24,128]{1,0:T(8,128)S(1)} %shard_map.81), channel_id=1, source_target_pairs={{16,32},{32,16},{48,64},{64,48},{80,96},{96,80},{112,128},{128,112... | collective-permute-start | bytes 36872 | tf_op jit(solution)/shard_map/ppermute | solution.py:424
  26.8 1.4 %collective-permute-start.2 = (f32[24,128]{1,0:T(8,128)S(1)}, f32[24,128]{1,0:T(8,128)S(1)}, u32[]{:S(2)}, u32[]{:S(2)}) collective-permute-start(f32[24,128]{1,0:T(8,128)S(1)} %shard_map.81), channel_id=1, source_target_pairs={{0,16},{16,0},{32,48},{48,32},{64,80},{80,64},{96,112},{112,96},{1... | collective-permute-start | bytes 36872 | tf_op jit(solution)/shard_map/ppermute | solution.py:424
  28.2 4.2 %collective-permute-start.5 = (f32[3,24,128]{2,1,0:T(8,128)S(1)}, f32[3,24,128]{2,1,0:T(8,128)S(1)}, u32[]{:S(2)}, u32[]{:S(2)}) collective-permute-start(f32[3,24,128]{2,1,0:T(8,128)S(1)} %pad_maximum_fusion.centre_ref), channel_id=1, source_target_pairs={{1,2},{2,1},{3,4},{4,3},{5,6},{6,5},{7,8},{8,7},{9,10},{10,9},{11,... | collective-permute-start | bytes 110600 | tf_op jit(solution)/shard_map/ppermute | solution.py:424
  28.9 4.9 %collective-permute-start.4 = (f32[3,24,128]{2,1,0:T(8,128)S(1)}, f32[3,24,128]{2,1,0:T(8,128)S(1)}, u32[]{:S(2)}, u32[]{:S(2)}) collective-permute-start(f32[3,24,128]{2,1,0:T(8,128)S(1)} %pad_maximum_fusion.centre_ref), channel_id=1, source_target_pairs={{0,1},{1,0},{2,3},{3,2},{4,5},{5,4},{6,7},{7,6},{8,9},{9,8},{10,11... | collective-permute-start | bytes 110600 | tf_op jit(solution)/shard_map/ppermute | solution.py:424
  35.2 31.8 %all-to-all-start = ((f32[256,1,128]{2,1,0:T(1,128)}), f32[256,1,128]{2,1,0:T(1,128)S(1)}, u32[]{:S(2)}, u32[]{:S(2)}) async-start(f32[256,1,128]{2,1,0:T(1,128)} %get-tuple-element.14), calls=%async_computation | async-start | bytes 262144 | tf_op jit(solution)/shard_map/all_to_all | solution.py:496

commit v6 on v5

--- a/solution.py
+++ b/solution.py
@@ -314,14 +314,17 @@
     def up(x):
         return pltpu.roll(x, 31, 0)
 
+    from_west, from_above = right(q_h), down(q_v)
+    from_corner, from_other = down(right(q_d)), down(left(q_a))
+    own_q = (LAMBDA_REG - THETA) + (q_h + from_west) + (q_v + from_above)
+    own_q = own_q + (q_d + from_corner) + (q_a + from_other)
+
     def operate(v):
-        below = up(v)
-        h = q_h * (v - left(v))
-        s = q_v * (v - below)
-        d = q_d * (v - left(below))
-        a = q_a * (v - right(below))
-        out = (LAMBDA_REG - THETA) * v + (h + s) + (d + a)
-        return out - right(h + down(d)) - down(s + left(a))
+        above, below = down(v), up(v)
+        out = own_q * v - q_v * below - from_above * above
+        out = out - (q_h * left(v) + from_west * right(v))
+        out = out - (q_d * left(below) + from_corner * right(above))
+        return out - (q_a * right(below) + from_other * left(above))
 
     u0 = f_h + f_v - right(f_h) - down(f_v)
     u1 = operate(u0)

time: 68.1 us -> 68 us (level)
  no operation moved by 1% of the time
where the time goes in v6:
time: 68 us; the launch traced here: 67.5 us
  starting transfers between devices  35.1 us (52%)
  waiting for transfers between devices  15.4 us (23%)
  Pallas kernels  10.5 us (15%)
  local copies, waits for them, and re-layouts  5.65 us (8%)
  between operations  0.78 us (1%)
    all_to_all x1, starting transfers between devices, body(): lax.all_to_all(moments, ('row', 'col'), 0, 0).reshape(devices, 128)  18.7 us
    all_to_all x1, waiting for transfers between devices, body(): lax.all_to_all(moments, ('row', 'col'), 0, 0).reshape(devices, 128)  12.8 us
    ppermute x2, starting transfers between devices, shifted(): return lax.ppermute(x, axis, pairs)  8.36 us
    ppermute x4, starting transfers between devices, swaps(): return (lax.ppermute(x, axis, inner), lax.ppermute(x, axis, outer))  8.09 us
    unnamed x12, local copies, waits for them, and re-layouts  5.65 us
    pallas_call x2, Pallas kernels, call_match(): pl.pallas_call(functools.partial(match_kernel, seam), out_shape=shape((24...  5.19 us
    ppermute x4, waiting for transfers between devices, swaps(): return (lax.ppermute(x, axis, inner), lax.ppermute(x, axis, outer))  2.6 us
    pallas_call x1, Pallas kernels, call_frames(): pl.pallas_call(frames_kernel, out_shape=(shape((2 * P_SIZE * PITCH, 128))...  2.52 us
  transfers between devices with their start and end apart: 7, of which 3 were waited for; matrix products, arithmetic and copies ran while one was open for 0% of the time, Pallas kernels for 9%

profile of v6, /device:TPU:1, one launch (start us, length us, event | category | flops | bytes accessed | tf_op | source)
XLA Modules:
  0.0 67.5 jit_solution(5830730180976171052)
XLA Ops:
  0.6 0.0 copy-start.1
  0.6 1.2 %copy-done.1 = bf16[1,1,2,16,128,128]{5,4,3,2,1,0:T(8,128)(2,1)S(1)} copy-done((bf16[1,1,2,16,128,128]{5,4,3,2,1,0:T(8,128)(2,1)S(1)}, bf16[1,1,2,16,128,128]{5,4,3,2,1,0:T(8,128)(2,1)}, u32[]{:S(2)}) %copy-start.1) | copy-done | bytes 1048600
  1.9 0.0 copy-start.5
  1.9 0.7 %copy-done.5 = s32[1,1,2,2,128]{4,3,2,1,0:T(2,128)S(1)} copy-done((s32[1,1,2,2,128]{4,3,2,1,0:T(2,128)S(1)}, s32[1,1,2,2,128]{4,3,2,1,0:T(2,128)}, u32[]{:S(2)}) %copy-start.5) | copy-done | bytes 2072
  2.5 0.1 shard_map.78
  2.6 4.0 %collective-permute-start = (bf16[2080,128]{1,0:T(8,128)(2,1)S(1)}, bf16[2080,128]{1,0:T(8,128)(2,1)S(1)}, u32[]{:S(2)}, u32[]{:S(2)}) collective-permute-start(bf16[2080,128]{1,0:T(8,128)(2,1)S(1)} %get-tuple-element.9), channel_id=1, source_target_pairs={{0,1},{1,2},{2,3},{3,4},{4,5},{5,6},{6,7},{7,8},{8,9},{9,10},{10,1... | collective-permute-start | bytes 1597448 | tf_op jit(solution)/shard_map/ppermute | solution.py:34
  6.6 4.4 %collective-permute-start.1 = (bf16[2064,128]{1,0:T(8,128)(2,1)S(1)}, bf16[2064,128]{1,0:T(8,128)(2,1)S(1)}, u32[]{:S(2)}, u32[]{:S(2)}) collective-permute-start(bf16[2064,128]{1,0:T(8,128)(2,1)S(1)} %get-tuple-element.12), channel_id=1, source_target_pairs={{0,16},{16,32},{32,48},{48,64},{64,80},{80,96},{96,112},{112,128},... | collective-permute-start | bytes 1585160 | tf_op jit(solution)/shard_map/ppermute | solution.py:34
  11.0 0.0 copy-start
  11.0 1.7 %copy-done = bf16[1,1,2,16,36864]{4,3,2,1,0:T(8,128)(2,1)S(1)} copy-done((bf16[1,1,2,16,36864]{4,3,2,1,0:T(8,128)(2,1)S(1)}, bf16[1,1,2,16,36864]{4,3,2,1,0:T(8,128)(2,1)}, u32[]{:S(2)}) %copy-start) | copy-done | bytes 2359320
  12.7 2.5 %shard_map.79 = (f32[12320,128]{1,0:T(8,128)S(1)}, f32[8352,128]{1,0:T(8,128)S(1)}) custom-call(bf16[2,16,36864]{2,1,0:T(8,128)(2,1)S(1)} %bitcast.15), custom_call_target="tpu_custom_call" | custom-call | tf_op jit(solution)/shard_map/pallas_call | solution.py:444
  15.2 0.0 copy-start.2
  15.2 0.7 %copy-done.2 = s32[16,16,2]{1,2,0:T(2,128)S(1)} copy-done((s32[16,16,2]{1,2,0:T(2,128)S(1)}, s32[16,16,2]{1,2,0:T(2,128)}, u32[]{:S(2)}) %copy-start.2) | copy-done | bytes 2072
  15.9 0.7 %copy-done.3 = s32[1,2,705]{2,1,0:T(2,128)S(1)} copy-done((s32[1,2,705]{2,1,0:T(2,128)S(1)}, s32[1,2,705]{2,1,0:T(2,128)}, u32[]{:S(2)}) %copy-start.3) | copy-done | bytes 5664
  16.6 0.7 %copy-done.4 = f32[1,705]{1,0:T(1,128)S(1)} copy-done((f32[1,705]{1,0:T(1,128)S(1)}, f32[1,705]{1,0:T(1,128)}, u32[]{:S(2)}) %copy-start.4) | copy-done | bytes 2844
  17.3 0.4 shard_map.77.springs_ref
  17.8 0.0 collective-permute-done.1.sent_ref
  17.8 2.6 %shard_map.80.rest_0_ = f32[8,128]{1,0:T(8,128)S(1)} custom-call(f32[24,128]{1,0:T(8,128)S(1)} %shard_map.77.springs_ref, bf16[2064,128]{1,0:T(8,128)(2,1)S(1)} %collective-permute-done.1.sent_ref, f32[12320,128]{1,0:T(8,128)S(1)} %get-tuple-element.10.frame_ref, f32[8352,128]{1,0:T(8,128)S(1)} %get-tuple-element.11.tab_ref), custom_call_target="tpu_custom_call" | custom-call | tf_op jit(solution)/shard_map/pallas_call | solution.py:454
  20.3 0.0 collective-permute-done.sent_ref
  20.3 2.6 %shard_map.81 = f32[24,128]{1,0:T(8,128)S(1)} custom-call(f32[24,128]{1,0:T(8,128)S(1)} %shard_map.77.springs_ref, bf16[2080,128]{1,0:T(8,128)(2,1)S(1)} %collective-permute-done.sent_ref, f32[12320,128]{1,0:T(8,128)S(1)} %get-tuple-element.10.frame_ref, f32[8352,128]{1,0:T(8,128)S(1)} %get-tuple-element.11.tab_ref, f32[8,128]{1,0:T(8,128)S(1)} %shard_map.80.rest_0_), custom_call_target="tpu_custom_call" | custom-call | tf_op jit(solution)/shard_map/pallas_call | solution.py:454
  23.0 3.8 %collective-permute-start.3 = (f32[24,128]{1,0:T(8,128)S(1)}, f32[24,128]{1,0:T(8,128)S(1)}, u32[]{:S(2)}, u32[]{:S(2)}) collective-permute-start(f32[24,128]{1,0:T(8,128)S(1)} %shard_map.81), channel_id=1, source_target_pairs={{16,32},{32,16},{48,64},{64,48},{80,96},{96,80},{112,128},{128,112... | collective-permute-start | bytes 36872 | tf_op jit(solution)/shard_map/ppermute | solution.py:427
  26.8 0.1 collective-permute-start.2
  26.9 1.3 %collective-permute-done.3 = f32[24,128]{1,0:T(8,128)S(1)} collective-permute-done((f32[24,128]{1,0:T(8,128)S(1)}, f32[24,128]{1,0:T(8,128)S(1)}, u32[]{:S(2)}, u32[]{:S(2)}) %collective-permute-start.3) | collective-permute-done | bytes 12320 | tf_op jit(solution)/shard_map/ppermute | solution.py:427
  28.1 0.0 collective-permute-done.2
  28.2 0.7 collective-permute-start.5
  28.8 3.6 %collective-permute-start.4 = (f32[3,24,128]{2,1,0:T(8,128)S(1)}, f32[3,24,128]{2,1,0:T(8,128)S(1)}, u32[]{:S(2)}, u32[]{:S(2)}) collective-permute-start(f32[3,24,128]{2,1,0:T(8,128)S(1)} %pad_maximum_fusion.centre_ref), channel_id=1, source_target_pairs={{0,1},{1,0},{2,3},{3,2},{4,5},{5,4},{6,7},{7,6},{8,9},{9,8},{10,11... | collective-permute-start | bytes 110600 | tf_op jit(solution)/shard_map/ppermute | solution.py:427
  32.4 0.0 collective-permute-done.5.outer_ref
  32.4 1.3 %collective-permute-done.4.inner_ref = f32[3,24,128]{2,1,0:T(8,128)S(1)} collective-permute-done((f32[3,24,128]{2,1,0:T(8,128)S(1)}, f32[3,24,128]{2,1,0:T(8,128)S(1)}, u32[]{:S(2)}, u32[]{:S(2)}) %collective-permute-start.4) | collective-permute-done | bytes 36896 | tf_op jit(solution)/shard_map/ppermute | solution.py:427
  33.7 1.3 %shard_map.82 = (f32[3,16,128]{2,1,0:T(8,128)S(1)}, f32[256,1,128]{2,1,0:T(1,128)}, f32[3,2,16]{2,1,0:T(2,128)}) custom-call(f32[3,24,128]{2,1,0:T(8,128)S(1)} %collective-permute-done.4.inner_ref, f32[3,24,128]{2,1,0:T(8,128)S(1)} %pad_maximum_fusion.centre_ref, f32[3,24,128]{2,1,0:T(8,128)S(1)} %collective-permute-done.5.outer_ref), custom_call_target="tpu_custom_call" | custom-call | tf_op jit(solution)/shard_map/pallas_call | solution.py:492
  35.0 18.7 %all-to-all-start = ((f32[256,1,128]{2,1,0:T(1,128)}), f32[256,1,128]{2,1,0:T(1,128)S(1)}, u32[]{:S(2)}, u32[]{:S(2)}) async-start(f32[256,1,128]{2,1,0:T(1,128)} %get-tuple-element.14), calls=%async_computation | async-start | bytes 262144 | tf_op jit(solution)/shard_map/all_to_all | solution.py:499
  53.7 0.2 shard_map.83.u_ref
  53.9 12.8 %all-to-all-done = f32[256,1,128]{2,1,0:T(1,128)S(1)} async-done(((f32[256,1,128]{2,1,0:T(1,128)}), f32[256,1,128]{2,1,0:T(1,128)S(1)}, u32[]{:S(2)}, u32[]{:S(2)}) %all-to-all-start) | async-done | bytes 131104 | tf_op jit(solution)/shard_map/all_to_all | solution.py:499
  66.8 0.8 %shard_map.84 = f32[2,256]{1,0:T(2,128)} custom-call(f32[256,128]{1,0:T(8,128)S(1)} %bitcast.17, f32[3,2,256]{2,1,0:T(2,128)S(1)} %shard_map.83.u_ref), custom_call_target="tpu_custom_call" | custom-call | tf_op jit(solution)/shard_map/pallas_call | solution.py:507
  (4 shorter events, 0.0 us)
Async XLA Ops:
  0.6 1.2 %copy-start.1 = (bf16[1,1,2,16,128,128]{5,4,3,2,1,0:T(8,128)(2,1)S(1)}, bf16[1,1,2,16,128,128]{5,4,3,2,1,0:T(8,128)(2,1)}, u32[]{:S(2)}) copy-start(bf16[1,1,2,16,128,128]{5,4,3,2,1,0:T(8,128)(2,1)} %param.6) | copy-start | bytes 3145732
  1.9 0.7 %copy-start.5 = (s32[1,1,2,2,128]{4,3,2,1,0:T(2,128)S(1)}, s32[1,1,2,2,128]{4,3,2,1,0:T(2,128)}, u32[]{:S(2)}) copy-start(s32[1,1,2,2,128]{4,3,2,1,0:T(2,128)} %param.8) | copy-start | bytes 6148
  2.6 17.7 %collective-permute-start = (bf16[2080,128]{1,0:T(8,128)(2,1)S(1)}, bf16[2080,128]{1,0:T(8,128)(2,1)S(1)}, u32[]{:S(2)}, u32[]{:S(2)}) collective-permute-start(bf16[2080,128]{1,0:T(8,128)(2,1)S(1)} %get-tuple-element.9), channel_id=1, source_target_pairs={{0,1},{1,2},{2,3},{3,4},{4,5},{5,6},{6,7},{7,8},{8,9},{9,10},{10,1... | collective-permute-start | bytes 1597448 | tf_op jit(solution)/shard_map/ppermute | solution.py:34
  6.6 11.1 %collective-permute-start.1 = (bf16[2064,128]{1,0:T(8,128)(2,1)S(1)}, bf16[2064,128]{1,0:T(8,128)(2,1)S(1)}, u32[]{:S(2)}, u32[]{:S(2)}) collective-permute-start(bf16[2064,128]{1,0:T(8,128)(2,1)S(1)} %get-tuple-element.12), channel_id=1, source_target_pairs={{0,16},{16,32},{32,48},{48,64},{64,80},{80,96},{96,112},{112,128},... | collective-permute-start | bytes 1585160 | tf_op jit(solution)/shard_map/ppermute | solution.py:34
  11.0 1.7 %copy-start = (bf16[1,1,2,16,36864]{4,3,2,1,0:T(8,128)(2,1)S(1)}, bf16[1,1,2,16,36864]{4,3,2,1,0:T(8,128)(2,1)}, u32[]{:S(2)}) copy-start(bf16[1,1,2,16,36864]{4,3,2,1,0:T(8,128)(2,1)} %param.7) | copy-start | bytes 7077892
  15.2 0.7 %copy-start.2 = (s32[16,16,2]{1,2,0:T(2,128)S(1)}, s32[16,16,2]{1,2,0:T(2,128)}, u32[]{:S(2)}) copy-start(s32[16,16,2]{1,2,0:T(2,128)} %param.9) | copy-start | bytes 6148
  15.9 0.7 %copy-start.3 = (s32[1,2,705]{2,1,0:T(2,128)S(1)}, s32[1,2,705]{2,1,0:T(2,128)}, u32[]{:S(2)}) copy-start(s32[1,2,705]{2,1,0:T(2,128)} %param.10) | copy-start | bytes 16924
  16.6 0.7 %copy-start.4 = (f32[1,705]{1,0:T(1,128)S(1)}, f32[1,705]{1,0:T(1,128)}, u32[]{:S(2)}) copy-start(f32[1,705]{1,0:T(1,128)} %stiff_ref.1) | copy-start | bytes 8464
  23.0 5.2 %collective-permute-start.3 = (f32[24,128]{1,0:T(8,128)S(1)}, f32[24,128]{1,0:T(8,128)S(1)}, u32[]{:S(2)}, u32[]{:S(2)}) collective-permute-start(f32[24,128]{1,0:T(8,128)S(1)} %shard_map.81), channel_id=1, source_target_pairs={{16,32},{32,16},{48,64},{64,48},{80,96},{96,80},{112,128},{128,112... | collective-permute-start | bytes 36872 | tf_op jit(solution)/shard_map/ppermute | solution.py:427
  26.8 1.4 %collective-permute-start.2 = (f32[24,128]{1,0:T(8,128)S(1)}, f32[24,128]{1,0:T(8,128)S(1)}, u32[]{:S(2)}, u32[]{:S(2)}) collective-permute-start(f32[24,128]{1,0:T(8,128)S(1)} %shard_map.81), channel_id=1, source_target_pairs={{0,16},{16,0},{32,48},{48,32},{64,80},{80,64},{96,112},{112,96},{1... | collective-permute-start | bytes 36872 | tf_op jit(solution)/shard_map/ppermute | solution.py:427
  28.2 4.2 %collective-permute-start.5 = (f32[3,24,128]{2,1,0:T(8,128)S(1)}, f32[3,24,128]{2,1,0:T(8,128)S(1)}, u32[]{:S(2)}, u32[]{:S(2)}) collective-permute-start(f32[3,24,128]{2,1,0:T(8,128)S(1)} %pad_maximum_fusion.centre_ref), channel_id=1, source_target_pairs={{1,2},{2,1},{3,4},{4,3},{5,6},{6,5},{7,8},{8,7},{9,10},{10,9},{11,... | collective-permute-start | bytes 110600 | tf_op jit(solution)/shard_map/ppermute | solution.py:427
  28.8 4.9 %collective-permute-start.4 = (f32[3,24,128]{2,1,0:T(8,128)S(1)}, f32[3,24,128]{2,1,0:T(8,128)S(1)}, u32[]{:S(2)}, u32[]{:S(2)}) collective-permute-start(f32[3,24,128]{2,1,0:T(8,128)S(1)} %pad_maximum_fusion.centre_ref), channel_id=1, source_target_pairs={{0,1},{1,0},{2,3},{3,2},{4,5},{5,4},{6,7},{7,6},{8,9},{9,8},{10,11... | collective-permute-start | bytes 110600 | tf_op jit(solution)/shard_map/ppermute | solution.py:427
  35.0 31.7 %all-to-all-start = ((f32[256,1,128]{2,1,0:T(1,128)}), f32[256,1,128]{2,1,0:T(1,128)S(1)}, u32[]{:S(2)}, u32[]{:S(2)}) async-start(f32[256,1,128]{2,1,0:T(1,128)} %get-tuple-element.14), calls=%async_computation | async-start | bytes 262144 | tf_op jit(solution)/shard_map/all_to_all | solution.py:499
